TPU v7x, 32 devices: a whole 2x2x4 slice. The times are simulated.
32 devices in a mesh: groups: 2 (over x), inline: 16 (over z, y, core).
Axes of the slice: x: 2, y: 2, z: 4, core: 2. Of those that a mesh axis runs over, the one named last changes fastest.
Arguments:
- data: float32 [256, 8, 4096], P(('groups', 'inline')), parts along dimension 0, may hold values from -6 to 6
- trace_mask: int32 [256, 4096], P(('groups', 'inline')), parts along dimension 0, may hold values 0 or 1
- slope_inline: float32 [256, 8, 4096], P(('groups', 'inline')), parts along dimension 0, may hold values from -1 to 1
- slope_cross: float32 [256, 8, 4096], P(('groups', 'inline')), parts along dimension 0, may hold values from -1 to 1
- model: float32 [256, 8, 4096], P(('groups', 'inline')), parts along dimension 0, may hold values from -6 to 6
- direction: float32 [256, 8, 4096], P(('groups', 'inline')), parts along dimension 0, may hold values from -6 to 6
Outputs:
- model_out: float32 [256, 8, 4096], P(('groups', 'inline')), parts along dimension 0
- direction_out: float32 [256, 8, 4096], P(('groups', 'inline')), parts along dimension 0
There are 2 independent parts, one for each index of `groups`. A program takes and returns all parts, laid end to end along the dimension named above; each array names one. Nothing has to cross between parts.
Inputs may be any that keep to these rules, and one draw needn't show every extreme that they name: `trace_mask`: 1 marks a recorded trace, 0 a missing one.
All inputs are finite; a program needn't handle non-finite values. No bound on the sum of `trace_mask` on one device may be relied on, other than what follows from the above.
Results may differ from a plain program's by a relative error of at most 0.0001.
Values sent between devices are 32-bit elements; how exact they have to be, the bound alone decides.
No kernel may reach another device: no remote copies, remote signals or barrier semaphores. Data moves between devices by JAX's collectives and lax.ppermute only.
A program may use at most 64 MiB of HBM per device.

v0:
```python
import jax
import jax.numpy as jnp
from jax import lax
from jax.sharding import PartitionSpec as P

ITERS = 3


reg_weight = 1.0


def from_behind(x, axis, by):
    peers = lax.axis_size(axis)
    pairs = [(i, i + by) for i in range(peers) if 0 <= i + by < peers]
    return lax.ppermute(x, axis, pairs)


def shift_ahead(values, along):
    length_along = values.shape[along]
    remaining = lax.slice_in_dim(values, 1, length_along, axis=along)
    return jnp.concatenate(
        [remaining, jnp.zeros_like(lax.slice_in_dim(values, 0, 1, axis=along))], along
    )


def shift_behind(values, along):
    length_along = values.shape[along]
    remaining = lax.slice_in_dim(values, 0, length_along - 1, axis=along)
    return jnp.concatenate(
        [jnp.zeros_like(lax.slice_in_dim(values, 0, 1, axis=along)), remaining], along
    )


def apply_form(values, ahead_cells, lower_coef, upper_coef):
    return lower_coef * (ahead_cells - shift_ahead(values, 1)) + upper_coef * (
        shift_ahead(ahead_cells, 1) - values
    )


def inline_form(values, edge_row, coefficients):
    ahead_cells = jnp.concatenate([values[1:], edge_row], 0)
    return apply_form(values, ahead_cells, coefficients[0], coefficients[1])


def cross_form(values, coefficients):
    return apply_form(values, shift_ahead(values, 2), coefficients[2], coefficients[3])


def cross_adjoint_of(cross_res, lower_coef, upper_coef):
    lower_cross = lower_coef * cross_res
    upper_cross = upper_coef * cross_res
    return (
        shift_behind(lower_cross, 2)
        - shift_behind(lower_cross, 1)
        + shift_behind(shift_behind(upper_cross, 2), 1)
        - upper_cross
    )


def inner_sum(left_terms, right_terms):
    total = jnp.sum(left_terms[0] * right_terms[0])
    total = total + jnp.sum(left_terms[1] * right_terms[1])
    return total + jnp.sum(left_terms[2] * right_terms[2])


def make_image(values, edge_row, known_traces, coefficients):
    return (
        known_traces * values,
        reg_weight * inline_form(values, edge_row, coefficients),
        reg_weight * cross_form(values, coefficients),
    )


def state_images(model, direction, data, known_traces, coefficients):
    model_row, direction_row = from_behind((model[:1], direction[:1]), "inline", -1)
    residual = (
        known_traces * (data - model),
        -reg_weight * inline_form(model, model_row, coefficients),
        -reg_weight * cross_form(model, coefficients),
    )
    return (residual, make_image(direction, direction_row, known_traces, coefficients))


def on_device(data, trace_mask, slope_inline, slope_cross, model, direction):
    known_traces = trace_mask.astype(jnp.float32)[:, None, :]
    coefficients = (
        (1.0 - slope_inline) * 0.5,
        (1.0 + slope_inline) * 0.5,
        (1.0 - slope_cross) * 0.5,
        (1.0 + slope_cross) * 0.5,
    )
    residual = None
    dir_image = None
    for iteration in range(ITERS):
        residual, dir_image = state_images(model, direction, data, known_traces, coefficients)
        lower_inline = coefficients[0] * residual[1]
        upper_inline = coefficients[1] * residual[1]
        lower_edge, upper_edge = from_behind((lower_inline[-1:], upper_inline[-1:]), "inline", 1)
        lower_behind = jnp.concatenate([lower_edge, lower_inline[:-1]], 0)
        upper_behind = jnp.concatenate([upper_edge, upper_inline[:-1]], 0)
        inline_adjoint = (
            lower_behind
            - shift_behind(lower_inline, 1)
            + shift_behind(upper_behind, 1)
            - upper_inline
        )
        cross_adjoint = cross_adjoint_of(residual[2], coefficients[2], coefficients[3])
        gradient = known_traces * residual[0] + reg_weight * (inline_adjoint + cross_adjoint)
        gradient_row = from_behind(gradient[:1], "inline", -1)
        grad_image = make_image(gradient, gradient_row, known_traces, coefficients)
        cross_term, dir_norm = lax.psum(
            (inner_sum(grad_image, dir_image), inner_sum(dir_image, dir_image)), "inline"
        )
        mixing = -cross_term / dir_norm
        conjugate = tuple(
            (grad_term + mixing * dir_term for grad_term, dir_term in zip(grad_image, dir_image))
        )
        fit_term, conj_norm = lax.psum(
            (inner_sum(residual, conjugate), inner_sum(conjugate, conjugate)), "inline"
        )
        step_size = fit_term / conj_norm
        direction = gradient + mixing * direction
        model = model + step_size * direction
    return (model, direction)


def solution(mesh):
    placed = (
        P(("groups", "inline"), None, None),
        P(("groups", "inline"), None),
        P(("groups", "inline"), None, None),
        P(("groups", "inline"), None, None),
        P(("groups", "inline"), None, None),
        P(("groups", "inline"), None, None),
    )
    return jax.shard_map(
        on_device,
        mesh=mesh,
        in_specs=placed,
        out_specs=(P(("groups", "inline"), None, None), P(("groups", "inline"), None, None)),
        check_vma=False,
    )
```

profile of v0, /device:TPU:0, one launch (start us, length us, event | category | flops | bytes accessed | tf_op | source)
XLA Modules:
  0.0 332.0 jit_solution(15053970562731234975)
XLA Ops:
  0.6 0.9 slice.282
  1.5 1.3 collective-permute-start.4
  2.8 0.9 slice.262
  3.8 1.4 collective-permute-start
  5.2 1.6 slice.271
  6.8 0.3 slice.287
  7.3 1.1 copy-done.6
  8.8 0.8 copy-done.37
  9.7 1.1 copy-done
  11.2 0.9 fusion.53
  12.0 3.7 %collective-permute-start.1 = (f32[1,8,4096]{2,1,0:T(8,128)S(1)}, f32[1,8,4096]{2,1,0:T(8,128)S(1)}, u32[]{:S(2)}, u32[]{:S(2)}) collective-permute-start(f32[1,8,4096]{2,1,0:T(8,128)S(1)} %slice.347), channel_id=1, source_target_pairs={{0,1},{1,2},{2,3},{3,4},{4,5},{5,6},{6,7},{7,8},{8,9},{9,10},{10,1... | collective-permute-start | bytes 393224 | tf_op jit(solution)/shard_map/ppermute | solution.py:15
  15.9 4.5 %collective-permute-start.2 = (f32[1,8,4096]{2,1,0:T(8,128)S(1)}, f32[1,8,4096]{2,1,0:T(8,128)S(1)}, u32[]{:S(2)}, u32[]{:S(2)}) collective-permute-start(f32[1,8,4096]{2,1,0:T(8,128)S(1)} %slice.350), channel_id=1, source_target_pairs={{0,1},{1,2},{2,3},{3,4},{4,5},{5,6},{6,7},{7,8},{8,9},{9,10},{10,1... | collective-permute-start | bytes 393224 | tf_op jit(solution)/shard_map/ppermute | solution.py:15
  20.6 0.3 pad_slice_fusion.20
  21.4 1.0 copy-done.12
  22.4 2.1 multiply_reduce_fusion.32
  24.5 0.3 slice.362
  24.8 1.3 collective-permute-start.3
  26.4 1.7 collective-permute-done.3
  28.2 3.9 %multiply_reduce_fusion.30 = (f32[]{:T(128)}, f32[]{:T(128)}, f32[8,8,4096]{2,1,0:T(8,128)}, f32[8,8,4096]{2,1,0:T(8,128)}, f32[]{:T(128)}, /*index=5*/f32[8,8,4096]{2,1,0:T(8,128)}, f32[]{:T(128)}, f32[8,8,4096]{2,1,0:T(8,128)}) fusion(f32[8,8,4096]{2,1,0:T(8,128)S(1)} %get-tuple-element.78, f32[8,7,4096]{2,1,0:T(8,128)S(1)} %pad_slice_fusion.28, ...), kind=kLoop, calls=%fused_computation.140 | loop fusion | flops 9961468 | bytes 18087440 | tf_op jit(solution)/shard_map/reduce_sum | solution.py:63
  35.8 35.8 %all-reduce.59 = (f32[]{:T(128)}, f32[]{:T(128)}) all-reduce(f32[]{:T(128)S(6)} %add.358, f32[]{:T(128)S(6)} %add.360), channel_id=1, replica_groups=mesh['groups'=2,'inline'=16] {'inline'}, use_global_device_ids=true, to_apply=%region_3.0 | all-reduce | flops 2 | bytes 16 | tf_op jit(solution)/shard_map/psum | solution.py:111
  73.0 3.0 multiply_reduce_fusion.26
  76.0 2.8 multiply_reduce_fusion.24
  82.6 30.0 %all-reduce.58 = (f32[]{:T(128)}, f32[]{:T(128)}) all-reduce(f32[]{:T(128)S(6)} %add.365, f32[]{:T(128)S(6)} %add.367), channel_id=1, replica_groups=mesh['groups'=2,'inline'=16] {'inline'}, use_global_device_ids=true, to_apply=%region_11.0 | all-reduce | flops 2 | bytes 16 | tf_op jit(solution)/shard_map/psum | solution.py:118
  114.0 2.0 multiply_add_fusion.14
  116.1 0.3 slice.373
  116.4 0.3 slice.388
  116.8 1.3 collective-permute-start.9
  118.1 1.3 collective-permute-start.5
  119.9 2.0 collective-permute-done.5
  122.0 0.9 fusion.52
  122.9 5.5 %collective-permute-start.6 = (f32[1,8,4096]{2,1,0:T(8,128)S(1)}, f32[1,8,4096]{2,1,0:T(8,128)S(1)}, u32[]{:S(2)}, u32[]{:S(2)}) collective-permute-start(f32[1,8,4096]{2,1,0:T(8,128)S(1)} %slice.368), channel_id=1, source_target_pairs={{0,1},{1,2},{2,3},{3,4},{4,5},{5,6},{6,7},{7,8},{8,9},{9,10},{10,1... | collective-permute-start | bytes 393224 | tf_op jit(solution)/shard_map/ppermute | solution.py:15
  128.6 2.1 collective-permute-start.7
  130.9 0.3 pad_slice_fusion.19
  131.5 1.1 copy-done.13
  132.6 2.1 multiply_reduce_fusion.20
  134.8 0.3 slice.387
  135.1 1.3 collective-permute-start.8
  136.7 1.7 collective-permute-done.8
  138.5 4.0 %multiply_reduce_fusion.18 = (f32[]{:T(128)}, f32[]{:T(128)}, f32[8,8,4096]{2,1,0:T(8,128)}, f32[8,8,4096]{2,1,0:T(8,128)}, f32[]{:T(128)}, /*index=5*/f32[8,8,4096]{2,1,0:T(8,128)}, f32[]{:T(128)}, f32[8,8,4096]{2,1,0:T(8,128)}) fusion(f32[8,8,4096]{2,1,0:T(8,128)S(1)} %get-tuple-element.67, f32[8,7,4096]{2,1,0:T(8,128)S(1)} %pad_slice_fusion.25, ...), kind=kLoop, calls=%fused_computation.118 | loop fusion | flops 9961468 | bytes 18087440 | tf_op jit(solution)/shard_map/reduce_sum | solution.py:63
  146.3 33.6 %all-reduce.57 = (f32[]{:T(128)}, f32[]{:T(128)}) all-reduce(f32[]{:T(128)S(6)} %add.381, f32[]{:T(128)S(6)} %add.383), channel_id=1, replica_groups=mesh['groups'=2,'inline'=16] {'inline'}, use_global_device_ids=true, to_apply=%region_19.0 | all-reduce | flops 2 | bytes 16 | tf_op jit(solution)/shard_map/psum | solution.py:111
  181.3 3.0 multiply_reduce_fusion.14
  184.3 1.0 multiply_reduce_fusion.13
  186.2 1.0 multiply_reduce_fusion.12
  190.9 30.1 %all-reduce.56 = (f32[]{:T(128)}, f32[]{:T(128)}) all-reduce(f32[]{:T(128)S(6)} %add.388, f32[]{:T(128)S(6)} %add.390), channel_id=1, replica_groups=mesh['groups'=2,'inline'=16] {'inline'}, use_global_device_ids=true, to_apply=%region_27.0 | all-reduce | flops 2 | bytes 16 | tf_op jit(solution)/shard_map/psum | solution.py:118
  222.3 2.0 multiply_add_fusion.7
  224.4 0.3 slice.399
  224.7 0.3 slice.414
  225.0 1.3 collective-permute-start.14
  226.3 1.3 collective-permute-start.10
  228.2 2.0 collective-permute-done.10
  230.3 0.9 fusion.51
  231.2 5.5 %collective-permute-start.11 = (f32[1,8,4096]{2,1,0:T(8,128)S(1)}, f32[1,8,4096]{2,1,0:T(8,128)S(1)}, u32[]{:S(2)}, u32[]{:S(2)}) collective-permute-start(f32[1,8,4096]{2,1,0:T(8,128)S(1)} %slice.394), channel_id=1, source_target_pairs={{0,1},{1,2},{2,3},{3,4},{4,5},{5,6},{6,7},{7,8},{8,9},{9,10},{10,1... | collective-permute-start | bytes 393224 | tf_op jit(solution)/shard_map/ppermute | solution.py:15
  236.9 1.9 collective-permute-start.12
  239.8 1.0 copy-done.14
  240.8 2.1 multiply_reduce_fusion.8
  243.2 1.5 collective-permute-start.13
  245.0 1.4 collective-permute-done.13
  246.6 3.9 %multiply_reduce_fusion.6 = (f32[]{:T(128)}, f32[]{:T(128)}, f32[8,8,4096]{2,1,0:T(8,128)}, f32[8,8,4096]{2,1,0:T(8,128)}, f32[]{:T(128)}, /*index=5*/f32[8,8,4096]{2,1,0:T(8,128)}, f32[]{:T(128)}, f32[8,8,4096]{2,1,0:T(8,128)}) fusion(f32[8,8,4096]{2,1,0:T(8,128)S(1)} %get-tuple-element.56, f32[8,7,4096]{2,1,0:T(8,128)S(1)} %pad_slice_fusion.22, ...), kind=kLoop, calls=%fused_computation.96 | loop fusion | flops 9961468 | bytes 18087440 | tf_op jit(solution)/shard_map/reduce_sum | solution.py:63
  254.2 33.8 %all-reduce.55 = (f32[]{:T(128)}, f32[]{:T(128)}) all-reduce(f32[]{:T(128)S(6)} %add.404, f32[]{:T(128)S(6)} %add.406), channel_id=1, replica_groups=mesh['groups'=2,'inline'=16] {'inline'}, use_global_device_ids=true, to_apply=%region_35.0 | all-reduce | flops 2 | bytes 16 | tf_op jit(solution)/shard_map/psum | solution.py:111
  289.3 3.0 multiply_reduce_fusion.2
  292.3 1.0 multiply_reduce_fusion.1
  294.1 1.1 multiply_reduce_fusion
  299.0 30.1 %all-reduce.54 = (f32[]{:T(128)}, f32[]{:T(128)}) all-reduce(f32[]{:T(128)S(6)} %add.411, f32[]{:T(128)S(6)} %add.413), channel_id=1, replica_groups=mesh['groups'=2,'inline'=16] {'inline'}, use_global_device_ids=true, to_apply=%region_43.0 | all-reduce | flops 2 | bytes 16 | tf_op jit(solution)/shard_map/psum | solution.py:118
  330.4 1.5 multiply_add_fusion
  (144 shorter events, 7.9 us)
Async XLA Ops:
  1.5 19.4 %collective-permute-start.4 = (f32[1,8,4096]{2,1,0:T(8,128)S(1)}, f32[1,8,4096]{2,1,0:T(8,128)S(1)}, u32[]{:S(2)}, u32[]{:S(2)}) collective-permute-start(f32[1,8,4096]{2,1,0:T(8,128)S(1)} %slice.282), channel_id=1, source_target_pairs={{1,0},{2,1},{3,2},{4,3},{5,4},{6,5},{7,6},{8,7},{9,8},{10,9},{11,1... | collective-permute-start | bytes 393224 | tf_op jit(solution)/shard_map/ppermute | solution.py:15
  3.8 3.0 copy-start.7
  3.8 5.9 %collective-permute-start = (f32[1,8,4096]{2,1,0:T(8,128)S(1)}, f32[1,8,4096]{2,1,0:T(8,128)S(1)}, u32[]{:S(2)}, u32[]{:S(2)}) collective-permute-start(f32[1,8,4096]{2,1,0:T(8,128)S(1)} %slice.262), channel_id=1, source_target_pairs={{1,0},{2,1},{3,2},{4,3},{5,4},{6,5},{7,6},{8,7},{9,8},{10,9},{11,1... | collective-permute-start | bytes 393224 | tf_op jit(solution)/shard_map/ppermute | solution.py:15
  7.2 1.2 copy-start.6
  8.7 0.9 copy-start.37
  9.6 1.2 copy-start
  9.6 1.5 copy-start.1
  12.0 3.9 %copy-start.23 = (f32[8,8,4096]{2,1,0:T(8,128)}, f32[8,8,4096]{2,1,0:T(8,128)S(1)}, u32[]{:S(2)}) copy-start(f32[8,8,4096]{2,1,0:T(8,128)S(1)} %get-tuple-element.82) | copy-start | bytes 3145732
  12.0 8.4 %copy-start.25 = (f32[8,8,4096]{2,1,0:T(8,128)}, f32[8,8,4096]{2,1,0:T(8,128)S(1)}, u32[]{:S(2)}) copy-start(f32[8,8,4096]{2,1,0:T(8,128)S(1)} %get-tuple-element.100) | copy-start | bytes 3145732
  12.0 9.2 %collective-permute-start.1 = (f32[1,8,4096]{2,1,0:T(8,128)S(1)}, f32[1,8,4096]{2,1,0:T(8,128)S(1)}, u32[]{:S(2)}, u32[]{:S(2)}) collective-permute-start(f32[1,8,4096]{2,1,0:T(8,128)S(1)} %slice.347), channel_id=1, source_target_pairs={{0,1},{1,2},{2,3},{3,4},{4,5},{5,6},{6,7},{7,8},{8,9},{9,10},{10,1... | collective-permute-start | bytes 393224 | tf_op jit(solution)/shard_map/ppermute | solution.py:15
  15.9 5.5 %collective-permute-start.2 = (f32[1,8,4096]{2,1,0:T(8,128)S(1)}, f32[1,8,4096]{2,1,0:T(8,128)S(1)}, u32[]{:S(2)}, u32[]{:S(2)}) collective-permute-start(f32[1,8,4096]{2,1,0:T(8,128)S(1)} %slice.350), channel_id=1, source_target_pairs={{0,1},{1,2},{2,3},{3,4},{4,5},{5,6},{6,7},{7,8},{8,9},{9,10},{10,1... | collective-permute-start | bytes 393224 | tf_op jit(solution)/shard_map/ppermute | solution.py:15
  21.1 1.2 copy-start.12
  24.5 3.7 %copy-start.11 = (f32[8,8,4096]{2,1,0:T(8,128)}, f32[8,8,4096]{2,1,0:T(8,128)S(1)}, u32[]{:S(2)}) copy-start(f32[8,8,4096]{2,1,0:T(8,128)S(1)} %get-tuple-element.78) | copy-start | bytes 3145732
  24.8 3.2 collective-permute-start.3
  72.9 3.1 copy-start.24
  72.9 3.1 copy-start.26
  72.9 3.1 copy-start.35
  73.0 3.1 copy-start.36
  116.0 22.5 %copy-start.5 = (f32[8,8,4096]{2,1,0:T(8,128)}, f32[8,8,4096]{2,1,0:T(8,128)S(1)}, u32[]{:S(2)}) copy-start(f32[8,8,4096]{2,1,0:T(8,128)S(1)} %get-tuple-element.73) | copy-start | bytes 3145732
  116.0 65.2 %copy-start.2 = (f32[8,8,4096]{2,1,0:T(8,128)}, f32[8,8,4096]{2,1,0:T(8,128)S(1)}, u32[]{:S(2)}) copy-start(f32[8,8,4096]{2,1,0:T(8,128)S(1)} %get-tuple-element.72) | copy-start | bytes 3145732
  116.8 14.5 %collective-permute-start.9 = (f32[1,8,4096]{2,1,0:T(8,128)S(1)}, f32[1,8,4096]{2,1,0:T(8,128)S(1)}, u32[]{:S(2)}, u32[]{:S(2)}) collective-permute-start(f32[1,8,4096]{2,1,0:T(8,128)S(1)} %slice.383), channel_id=1, source_target_pairs={{1,0},{2,1},{3,2},{4,3},{5,4},{6,5},{7,6},{8,7},{9,8},{10,9},{11,1... | collective-permute-start | bytes 393224 | tf_op jit(solution)/shard_map/ppermute | solution.py:15
  118.1 3.9 %collective-permute-start.5 = (f32[1,8,4096]{2,1,0:T(8,128)S(1)}, f32[1,8,4096]{2,1,0:T(8,128)S(1)}, u32[]{:S(2)}, u32[]{:S(2)}) collective-permute-start(f32[1,8,4096]{2,1,0:T(8,128)S(1)} %slice.364), channel_id=1, source_target_pairs={{1,0},{2,1},{3,2},{4,3},{5,4},{6,5},{7,6},{8,7},{9,8},{10,9},{11,1... | collective-permute-start | bytes 393224 | tf_op jit(solution)/shard_map/ppermute | solution.py:15
  122.9 5.7 %copy-start.21 = (f32[8,8,4096]{2,1,0:T(8,128)}, f32[8,8,4096]{2,1,0:T(8,128)S(1)}, u32[]{:S(2)}) copy-start(f32[8,8,4096]{2,1,0:T(8,128)S(1)} %get-tuple-element.71) | copy-start | bytes 3145732
  122.9 7.8 %copy-start.17 = (f32[8,8,4096]{2,1,0:T(8,128)}, f32[8,8,4096]{2,1,0:T(8,128)S(1)}, u32[]{:S(2)}) copy-start(f32[8,8,4096]{2,1,0:T(8,128)S(1)} %get-tuple-element.98) | copy-start | bytes 3145732
  122.9 8.6 %collective-permute-start.6 = (f32[1,8,4096]{2,1,0:T(8,128)S(1)}, f32[1,8,4096]{2,1,0:T(8,128)S(1)}, u32[]{:S(2)}, u32[]{:S(2)}) collective-permute-start(f32[1,8,4096]{2,1,0:T(8,128)S(1)} %slice.368), channel_id=1, source_target_pairs={{0,1},{1,2},{2,3},{3,4},{4,5},{5,6},{6,7},{7,8},{8,9},{9,10},{10,1... | collective-permute-start | bytes 393224 | tf_op jit(solution)/shard_map/ppermute | solution.py:15
  128.6 2.9 collective-permute-start.7
  131.4 1.2 copy-start.13
  134.8 3.7 %copy-start.10 = (f32[8,8,4096]{2,1,0:T(8,128)}, f32[8,8,4096]{2,1,0:T(8,128)S(1)}, u32[]{:S(2)}) copy-start(f32[8,8,4096]{2,1,0:T(8,128)S(1)} %get-tuple-element.67) | copy-start | bytes 3145732
  135.1 3.2 collective-permute-start.8
  181.2 3.1 copy-start.22
  181.2 3.1 copy-start.33
  181.3 3.1 copy-start.34
  184.3 1.2 copy-start.18
  184.3 1.5 copy-start.29
  184.3 1.8 copy-start.30
  224.3 22.2 %copy-start.3 = (f32[8,8,4096]{2,1,0:T(8,128)}, f32[8,8,4096]{2,1,0:T(8,128)S(1)}, u32[]{:S(2)}) copy-start(f32[8,8,4096]{2,1,0:T(8,128)S(1)} %get-tuple-element.62) | copy-start | bytes 3145732
  225.0 14.3 %collective-permute-start.14 = (f32[1,8,4096]{2,1,0:T(8,128)S(1)}, f32[1,8,4096]{2,1,0:T(8,128)S(1)}, u32[]{:S(2)}, u32[]{:S(2)}) collective-permute-start(f32[1,8,4096]{2,1,0:T(8,128)S(1)} %slice.409), channel_id=1, source_target_pairs={{1,0},{2,1},{3,2},{4,3},{5,4},{6,5},{7,6},{8,7},{9,8},{10,9},{11,1... | collective-permute-start | bytes 393224 | tf_op jit(solution)/shard_map/ppermute | solution.py:15
  226.3 3.9 %collective-permute-start.10 = (f32[1,8,4096]{2,1,0:T(8,128)S(1)}, f32[1,8,4096]{2,1,0:T(8,128)S(1)}, u32[]{:S(2)}, u32[]{:S(2)}) collective-permute-start(f32[1,8,4096]{2,1,0:T(8,128)S(1)} %slice.390), channel_id=1, source_target_pairs={{1,0},{2,1},{3,2},{4,3},{5,4},{6,5},{7,6},{8,7},{9,8},{10,9},{11,1... | collective-permute-start | bytes 393224 | tf_op jit(solution)/shard_map/ppermute | solution.py:15
  231.2 5.7 %copy-start.19 = (f32[8,8,4096]{2,1,0:T(8,128)}, f32[8,8,4096]{2,1,0:T(8,128)S(1)}, u32[]{:S(2)}) copy-start(f32[8,8,4096]{2,1,0:T(8,128)S(1)} %get-tuple-element.60) | copy-start | bytes 3145732
  231.2 7.6 %copy-start.15 = (f32[8,8,4096]{2,1,0:T(8,128)}, f32[8,8,4096]{2,1,0:T(8,128)S(1)}, u32[]{:S(2)}) copy-start(f32[8,8,4096]{2,1,0:T(8,128)S(1)} %get-tuple-element.96) | copy-start | bytes 3145732
  231.2 8.4 %collective-permute-start.11 = (f32[1,8,4096]{2,1,0:T(8,128)S(1)}, f32[1,8,4096]{2,1,0:T(8,128)S(1)}, u32[]{:S(2)}, u32[]{:S(2)}) collective-permute-start(f32[1,8,4096]{2,1,0:T(8,128)S(1)} %slice.394), channel_id=1, source_target_pairs={{0,1},{1,2},{2,3},{3,4},{4,5},{5,6},{6,7},{7,8},{8,9},{9,10},{10,1... | collective-permute-start | bytes 393224 | tf_op jit(solution)/shard_map/ppermute | solution.py:15
  236.9 2.9 collective-permute-start.12
  239.5 1.2 copy-start.14
  242.8 3.7 %copy-start.8 = (f32[8,8,4096]{2,1,0:T(8,128)}, f32[8,8,4096]{2,1,0:T(8,128)S(1)}, u32[]{:S(2)}) copy-start(f32[8,8,4096]{2,1,0:T(8,128)S(1)} %get-tuple-element.56) | copy-start | bytes 3145732
  243.2 3.2 collective-permute-start.13
  289.2 3.0 copy-start.20
  289.2 3.0 copy-start.31
  289.3 3.0 copy-start.32
  292.3 1.2 copy-start.16
  292.3 1.5 copy-start.27
  292.3 1.8 copy-start.28
  294.1 36.3 %copy-start.4 = (f32[8,8,4096]{2,1,0:T(8,128)S(1)}, f32[8,8,4096]{2,1,0:T(8,128)}, u32[]{:S(2)}) copy-start(f32[8,8,4096]{2,1,0:T(8,128)} %copy-done.3) | copy-start | bytes 3145732
  294.1 36.3 %copy-start.9 = (f32[8,8,4096]{2,1,0:T(8,128)S(1)}, f32[8,8,4096]{2,1,0:T(8,128)}, u32[]{:S(2)}) copy-start(f32[8,8,4096]{2,1,0:T(8,128)} %copy-done.8) | copy-start | bytes 3145732
where the time goes:
time: 333 us; the launch traced here: 332 us
  blocking collectives  193 us (58%)
  other arithmetic  44.1 us (13%)
  starting transfers between devices  35.1 us (11%)
  between operations  32.2 us (10%)
  local copies, waits for them, and re-layouts  18 us (5%)
  waiting for transfers between devices  9.18 us (3%)
    psum x3, blocking collectives, on_device(): lax.psum((inner_sum(grad_image, dir_image), inner_sum(dir_image, dir_imag...  103 us
    psum x3, blocking collectives, on_device(): lax.psum((inner_sum(residual, conjugate), inner_sum(conjugate, conjugate)...  90.1 us
    ppermute x15, starting transfers between devices, from_behind(): return lax.ppermute(x, axis, pairs)  35.1 us
    reduce_sum x6, other arithmetic, inner_sum(): return total + jnp.sum(left_terms[2] * right_terms[2])  16.6 us
    reduce_sum x6, other arithmetic, inner_sum(): total = jnp.sum(left_terms[0] * right_terms[0])  15.4 us
    ppermute x15, waiting for transfers between devices, from_behind(): return lax.ppermute(x, axis, pairs)  9.18 us
    unnamed x76, local copies, waits for them, and re-layouts  8.23 us
  transfers between devices with their start and end apart: 15, of which 7 were waited for; matrix products, arithmetic and copies ran while one was open for 3% of the time, Pallas kernels for 0%

commit v1 on v0

v1 whole, which is shorter than its diff:
```python
import functools

import jax
import jax.numpy as jnp
from jax import lax
from jax.experimental import pallas as pl
from jax.experimental.pallas import tpu as pltpu
from jax.sharding import PartitionSpec as P

ITERS = 3
NT = 8
LANES = 128
CHUNK = 512
SHIFT = 18.0
M0, D0, SI0, SC0, G0, BG0, B2G0, BD0, B2D0 = range(9)
M1, D1, SI1, SC1, G1, BG1, BD1, SJ1 = range(8)
N_MOMENTS = 18
VMEM_LIMIT = 16 * 1024 * 1024

f32 = jnp.float32


def time_ahead(v):
    rolled = pltpu.roll(v, NT - 1, 0)
    return jnp.where(lax.broadcasted_iota(jnp.int32, v.shape, 0) == NT - 1, 0.0, rolled)


def time_behind(v):
    rolled = pltpu.roll(v, 1, 0)
    return jnp.where(lax.broadcasted_iota(jnp.int32, v.shape, 0) == 0, 0.0, rolled)


def sum_diff(v):
    ahead = time_ahead(v)
    return ahead + v, ahead - v


def head(pair, width):
    return pair[0][:, :width], pair[1][:, :width]


def inline_res(here, after, slope):
    return (after[0] - here[0]) + slope * (after[1] + here[1])


def parts(res, slope):
    scaled = slope * res
    return res - scaled, res + scaled


def to_next(ef):
    return ef[0] + time_behind(ef[1])


def to_self(ef):
    return -(ef[1] + time_behind(ef[0]))


def lane_ahead(v):
    width = v.shape[1]
    return pltpu.roll(v, width - 1, 1)[:, : width - LANES]


def lane_behind(before, v):
    joined = jnp.concatenate([before, v], axis=1)
    return pltpu.roll(joined, 1, 1)[:, LANES:]


def cross_res(sd, slope):
    width = sd[0].shape[1] - LANES
    here = head(sd, width)
    return (lane_ahead(sd[0]) - here[0]) + slope * (lane_ahead(sd[1]) + here[1])


def cross_terms(sd, slope, carry, slot):
    e, f = parts(cross_res(sd, slope), slope)
    e_behind = lane_behind(carry[slot, 0], e)
    f_behind = lane_behind(carry[slot, 1], f)
    carry[slot, 0] = e[:, -LANES:]
    carry[slot, 1] = f[:, -LANES:]
    return e_behind - f, f_behind - e


def stencil(load, slope_in, slope_cr, lo, hi, res_lo, res_hi, carry, slot, scale_lo=None):
    out = {}
    sd = {}

    def pair(i):
        if i not in sd:
            sd[i] = sum_diff(load(i))
        return sd[i]

    before = None
    for i in range(lo - 1, hi + 1):
        here = None
        if res_lo <= i <= res_hi:
            first = pair(i)
            second = pair(i + 1)
            width = first[0].shape[1] - LANES
            slope = slope_in(i)
            res = inline_res(head(first, width), head(second, width), slope)
            if i == -1 and scale_lo is not None:
                res = res * scale_lo
            here = parts(res, slope)
        if i >= lo:
            same, later = cross_terms(pair(i), slope_cr(i), carry, slot + i - lo)
            if before is not None:
                same = same + before[0]
                later = later + before[1]
            if here is not None:
                same = same - here[1]
                later = later - here[0]
            out[i] = same + time_behind(later)
        before = here
    return out


class Mended:
    def __init__(self, n, depth, whole, ends):
        self.n, self.depth, self.whole, self.ends = n, depth, whole, ends

    def at(self, i):
        if i < self.depth:
            return self.ends, i + 1
        if i >= self.n - self.depth:
            return self.ends, i - self.n + 2 * self.depth + 1
        return self.whole, i + 1

    def load(self, i, lanes):
        ref, row = self.at(i)
        return ref[row, :, lanes]

    def store(self, i, lanes, value):
        ref, row = self.at(i)
        ref[row, :, lanes] = value


def mended(n, whole, ends):
    return [Mended(n, depth, w, e) for depth, w, e in zip((1, 2, 3, 1, 2), whole, ends)]


def chunks(x):
    return x // CHUNK


def at_chunk(c):
    return pl.multiple_of(c * CHUNK, CHUNK)


def edge_kernel(
    n, x,
    data_hbm, mask_hbm, si_hbm, sc_hbm, model_hbm, dir_hbm, up_ref, down_ref,
    data_ref, mask_ref, si_ref, sc_ref, m_ref, d_ref, g_ref, bg_ref, bd_ref, carry, sems,
):
    lanes = pl.ds(0, x)
    copies = [pltpu.make_async_copy(mask_hbm, mask_ref, sems.at[0])]
    for ref, dst in ((model_hbm, m_ref), (si_hbm, si_ref), (sc_hbm, sc_ref), (data_hbm, data_ref), (dir_hbm, d_ref)):
        for rows in (pl.ds(0, 4), pl.ds(n - 3, 3)):
            to = dst.at[rows] if dst.shape[2] == x else dst.at[rows, :, lanes]
            copies.append(pltpu.make_async_copy(ref.at[rows], to, sems.at[len(copies)]))
    for copy in copies:
        copy.start()
    for ref in (m_ref, d_ref, g_ref, bg_ref, bd_ref):
        ref[:, :, pl.ds(x, LANES)] = jnp.zeros((n, NT, LANES), f32)
    carry[...] = jnp.zeros(carry.shape, f32)
    share = x // NT
    for copy in copies:
        copy.wait()
    for s in range(NT):
        up_ref[pl.ds(s, 1), pl.ds(9 * x, share)] = mask_ref[pl.ds(0, 1), pl.ds(s * share, share)].astype(f32)
        down_ref[pl.ds(s, 1), pl.ds(8 * x, share)] = mask_ref[pl.ds(n - 1, 1), pl.ds(s * share, share)].astype(f32)

    def known4(i, x0):
        return mask_ref[pl.ds(i, 1), pl.ds(x0, CHUNK)].astype(f32) * 4.0

    def level(x0, src, lo, hi, slot):
        return stencil(
            lambda i: src[i, :, pl.ds(x0, CHUNK + LANES)],
            lambda i: si_ref[i, :, pl.ds(x0, CHUNK)],
            lambda i: sc_ref[i, :, pl.ds(x0, CHUNK)],
            lo, hi, 0, n - 2, carry, slot,
        )

    def applied(x0, src, lo, hi, slot):
        out = level(x0, src, lo, hi, slot)
        return {i: (known4(i, x0) - SHIFT) * src[i, :, pl.ds(x0, CHUNK)] + out[i] for i in out}

    def send_up(slot, x0, value):
        up_ref[:, pl.ds(pl.multiple_of(x0 + slot * x, CHUNK), CHUNK)] = value

    def send_down(slot, x0, value):
        down_ref[:, pl.ds(pl.multiple_of(x0 + slot * x, CHUNK), CHUNK)] = value

    def first(c, _):
        x0 = at_chunk(c)
        here = pl.ds(x0, CHUNK)
        out = level(x0, m_ref, 0, 2, 0)
        out.update(level(x0, m_ref, n - 2, n - 1, 3))
        for i, value in out.items():
            out[i] = known4(i, x0) * (data_ref[i, :, here] - m_ref[i, :, here]) - value
            g_ref[i, :, here] = out[i]
        send_up(G0, x0, out[0])
        send_down(G1, x0, out[n - 1])
        out = applied(x0, d_ref, 0, 1, 5)
        for i in (0, 1):
            bd_ref[i, :, here] = out[i]
        send_up(BD0, x0, out[0])
        out = applied(x0, d_ref, n - 1, n - 1, 7)
        send_down(BD1, x0, out[n - 1])
        for slot, row in ((M0, m_ref), (D0, d_ref), (SI0, si_ref), (SC0, sc_ref)):
            send_up(slot, x0, row[0, :, here])
        for slot, row in ((M1, m_ref), (D1, d_ref), (SI1, si_ref), (SC1, sc_ref)):
            send_down(slot, x0, row[n - 1, :, here])
        send_down(SJ1, x0, si_ref[n - 2, :, here])
        return 0

    lax.fori_loop(0, chunks(x), first, 0)
    carry[...] = jnp.zeros(carry.shape, f32)

    def second(c, _):
        x0 = at_chunk(c)
        here = pl.ds(x0, CHUNK)
        out = applied(x0, g_ref, 0, 1, 0)
        for i in (0, 1):
            bg_ref[i, :, here] = out[i]
        send_up(BG0, x0, out[0])
        send_down(BG1, x0, applied(x0, g_ref, n - 1, n - 1, 2)[n - 1])
        send_up(B2D0, x0, applied(x0, bd_ref, 0, 0, 3)[0])
        return 0

    lax.fori_loop(0, chunks(x), second, 0)
    carry[...] = jnp.zeros(carry.shape, f32)

    def third(c, _):
        x0 = at_chunk(c)
        send_up(B2G0, x0, applied(x0, bg_ref, 0, 0, 0)[0])
        return 0

    lax.fori_loop(0, chunks(x), third, 0)


def local_kernel(
    n, x,
    data_hbm, mask_hbm, si_hbm, sc_hbm, model_hbm, dir_hbm,
    m_ref, d_ref, si_ref, sc_ref, mask_ref, g_ref, bg_ref, b2g_ref, bd_ref, b2d_ref, sums_ref,
    data_ref, carry, sems,
):
    body = (pl.ds(1, n), slice(None), pl.ds(0, x))
    copies = [
        pltpu.make_async_copy(model_hbm, m_ref.at[body], sems.at[0]),
        pltpu.make_async_copy(si_hbm, si_ref.at[pl.ds(1, n)], sems.at[1]),
        pltpu.make_async_copy(sc_hbm, sc_ref, sems.at[2]),
        pltpu.make_async_copy(data_hbm, data_ref, sems.at[3]),
        pltpu.make_async_copy(mask_hbm, mask_ref, sems.at[4]),
        pltpu.make_async_copy(dir_hbm, d_ref.at[body], sems.at[5]),
    ]
    for copy in copies:
        copy.start()
    pad = jnp.zeros((n + 2, NT, LANES), f32)
    for ref in (m_ref, d_ref, g_ref, bg_ref, b2g_ref, bd_ref, b2d_ref):
        ref[:, :, pl.ds(x, LANES)] = pad
    carry[...] = jnp.zeros(carry.shape, f32)
    sums_ref[...] = jnp.zeros(sums_ref.shape, f32)
    for copy in copies:
        copy.wait()

    def known4(i, x0):
        return mask_ref[pl.ds(i, 1), pl.ds(x0, CHUNK)].astype(f32) * 4.0

    def level(x0, src, lo, hi, slot):
        return stencil(
            lambda i: src[i + 1, :, pl.ds(x0, CHUNK + LANES)],
            lambda i: si_ref[i + 1, :, pl.ds(x0, CHUNK)],
            lambda i: sc_ref[i, :, pl.ds(x0, CHUNK)],
            lo, hi, 0, n - 2, carry, slot,
        )

    def apply(x0, src, dst, lo, hi, slot):
        here = pl.ds(x0, CHUNK)
        out = level(x0, src, lo, hi, slot)
        for i in range(lo, hi + 1):
            dst[i + 1, :, here] = (known4(i, x0) - SHIFT) * src[i + 1, :, here] + out[i]

    def first(c, _):
        x0 = at_chunk(c)
        here = pl.ds(x0, CHUNK)
        out = level(x0, m_ref, 0, n - 1, 0)
        for i in range(n):
            g_ref[i + 1, :, here] = known4(i, x0) * (data_ref[i, :, here] - m_ref[i + 1, :, here]) - out[i]
        apply(x0, d_ref, bd_ref, 0, n - 1, n)
        return 0

    lax.fori_loop(0, chunks(x), first, 0)
    carry[...] = jnp.zeros(carry.shape, f32)

    def second(c, _):
        x0 = at_chunk(c)
        apply(x0, g_ref, bg_ref, 2, n - 3, 0)
        apply(x0, bd_ref, b2d_ref, 2, n - 3, n)
        return 0

    lax.fori_loop(0, chunks(x), second, 0)
    carry[...] = jnp.zeros(carry.shape, f32)

    def third(c, _):
        apply(at_chunk(c), bg_ref, b2g_ref, 3, n - 4, 0)
        return 0

    lax.fori_loop(0, chunks(x), third, 0)

    def fourth(c, _):
        x0 = at_chunk(c)
        products(
            x0, range(3, n - 3), range(3, n - 4),
            [lambda i, lanes, ref=ref: ref[i + 1, :, lanes] for ref in (g_ref, bg_ref, b2g_ref, d_ref, bd_ref, b2d_ref)],
            known4, si_ref, sc_ref, sums_ref,
        )
        return 0

    lax.fori_loop(0, chunks(x), fourth, 0)


PAIRS = ((0, 0), (0, 1), (1, 1), (1, 2), (2, 2), None, (0, 3), (0, 4), (1, 4), (1, 5), (2, 5), None,
         (3, 3), (3, 4), (4, 4), (4, 5), (5, 5), None)


def products(x0, rows, inline_rows, loads, known4, si_ref, sc_ref, sums):
    here = pl.ds(x0, CHUNK)
    wide = pl.ds(x0, CHUNK + LANES)
    totals = [None] * N_MOMENTS

    def add(k, product):
        acc = product[:, :LANES]
        for j in range(1, CHUNK // LANES):
            acc = acc + product[:, j * LANES:(j + 1) * LANES]
        totals[k] = acc if totals[k] is None else totals[k] + acc

    def add_pairs(u, v):
        add(5, u * u)
        add(11, u * v)
        add(17, v * v)

    sums_of = {}

    def pair(which, i):
        if (which, i) not in sums_of:
            sums_of[which, i] = sum_diff(loads[which](i, wide))
        return sums_of[which, i]

    for i in sorted(set(rows) | set(inline_rows)):
        if i in inline_rows:
            slope = si_ref[i + 1, :, here]
            add_pairs(*(inline_res(head(pair(k, i), CHUNK), head(pair(k, i + 1), CHUNK), slope) for k in (2, 5)))
        if i in rows:
            cross = sc_ref[i, :, here]
            add_pairs(*(cross_res(pair(k, i), cross) for k in (2, 5)))
            values = [load(i, here) for load in loads]
            for k, which in enumerate(PAIRS):
                if which is not None:
                    add(k, values[which[0]] * values[which[1]])
            known = known4(i, x0)
            kept_g = known * values[2]
            add(5, kept_g * values[2])
            add(11, kept_g * values[5])
            add(17, known * values[5] * values[5])
    for k in range(N_MOMENTS):
        sums[k] = sums[k] + totals[k]


def join_kernel(
    n, x,
    m_ref, d_ref, si_ref, sc_ref, mask_ref, g_in, bg_in, b2g_in, bd_in, b2d_in, sums_in, up_ref, down_ref,
    g_out, bg_out, b2g_out, bd_out, b2d_out, moments_ref,
    eps_ref, eta_ref, epsb_ref, mask_up, mask_down, carry, sums,
):
    place = lax.axis_index("inline")
    not_first = (place > 0).astype(f32)
    not_last = (place < lax.axis_size("inline") - 1).astype(f32)
    share = x // NT
    pad = jnp.zeros((NT, LANES), f32)
    for i in range(3):
        eps_ref[i, :, pl.ds(x, LANES)] = pad
    eta_ref[:, pl.ds(x, LANES)] = pad
    for ref in (g_out, bg_out, b2g_out, bd_out, b2d_out):
        for i in range(ref.shape[0]):
            ref[i, :, pl.ds(x, LANES)] = pad
    g_rows, bg_rows, b2g_rows, bd_rows, b2d_rows = mended(
        n, (g_in, bg_in, b2g_in, bd_in, b2d_in), (g_out, bg_out, b2g_out, bd_out, b2d_out))
    epsb_ref[:, pl.ds(x, LANES)] = pad
    carry[...] = jnp.zeros(carry.shape, f32)
    sums[...] = sums_in[...]
    for s in range(NT):
        mask_up[:, pl.ds(s * share, share)] = up_ref[pl.ds(s, 1), pl.ds(9 * x, share)] * 4.0 - SHIFT
        mask_down[:, pl.ds(s * share, share)] = down_ref[pl.ds(s, 1), pl.ds(8 * x, share)] * 4.0 - SHIFT

    def from_up(slot, x0):
        return up_ref[:, pl.ds(pl.multiple_of(x0 + slot * x, CHUNK), CHUNK)]

    def from_down(slot, x0):
        return down_ref[:, pl.ds(pl.multiple_of(x0 + slot * x, CHUNK), CHUNK)]

    def known4(i, x0):
        return mask_ref[pl.ds(i, 1), pl.ds(x0, CHUNK)].astype(f32) * 4.0

    def zeroth(c, _):
        x0 = at_chunk(c)
        here = pl.ds(x0, CHUNK)
        slope = si_ref[n, :, here]

        ef = parts(inline_res(sum_diff(m_ref[n, :, here]), sum_diff(from_up(M0, x0)), slope), slope)
        eps = -to_next(ef)
        eps_ref[0, :, here] = eps
        g_rows.store(n, here, (from_up(G0, x0) + eps) * not_last)
        g_rows.store(n - 1, here, g_in[n, :, here] - to_self(ef))
        ef = parts(inline_res(sum_diff(d_ref[n, :, here]), sum_diff(from_up(D0, x0)), slope), slope)
        eta = to_next(ef)
        eta_ref[:, here] = eta
        bd_rows.store(n, here, (from_up(BD0, x0) + eta) * not_last)
        bd_rows.store(n - 1, here, bd_in[n, :, here] + to_self(ef))

        slope = from_down(SI1, x0)
        res = inline_res(sum_diff(from_down(M1, x0)), sum_diff(m_ref[1, :, here]), slope) * not_first
        ef = parts(res, slope)
        eps = -to_self(ef)
        epsb_ref[:, here] = eps
        g_rows.store(-1, here, from_down(G1, x0) + eps)
        g_rows.store(0, here, g_in[1, :, here] - to_next(ef))
        res = inline_res(sum_diff(from_down(D1, x0)), sum_diff(d_ref[1, :, here]), slope) * not_first
        ef = parts(res, slope)
        bd_rows.store(-1, here, from_down(BD1, x0) + to_self(ef))
        bd_rows.store(0, here, bd_in[1, :, here] + to_next(ef))
        return 0

    lax.fori_loop(0, chunks(x), zeroth, 0)

    def slope_in(x0):
        def get(i):
            if i == -1:
                return from_down(SI1, x0)
            return si_ref[i + 1, :, pl.ds(x0, CHUNK)]
        return get

    def edges(x0, src, dst, depth, slot):
        here = pl.ds(x0, CHUNK)
        for lo, hi in ((0, depth), (n - 1 - depth, n - 1)):
            out = stencil(
                lambda i: src.load(i, pl.ds(x0, CHUNK + LANES)),
                slope_in(x0),
                lambda i: sc_ref[i, :, here],
                lo, hi, -1, n - 1, carry, slot, not_first,
            )
            for i in range(lo, hi + 1):
                dst.store(i, here, (known4(i, x0) - SHIFT) * src.load(i, here) + out[i])
            slot += hi - lo + 1
        return slot

    def boundary(src, row, slope, here, scale=None):
        res = inline_res(sum_diff(src.load(row, here)), sum_diff(src.load(row + 1, here)), slope)
        if scale is not None:
            res = res * scale
        return parts(res, slope)

    def first(c, _):
        x0 = at_chunk(c)
        here = pl.ds(x0, CHUNK)
        wide = pl.ds(x0, CHUNK + LANES)
        slot = edges(x0, g_rows, bg_rows, 1, 0)
        slot = edges(x0, bd_rows, b2d_rows, 1, slot)
        slope = si_ref[n, :, here]
        slope_up = from_up(SI0, x0)
        cross_up = from_up(SC0, x0)
        sd = sum_diff(eps_ref[0, :, wide])
        near = head(sd, CHUNK)
        ef8 = parts(slope_up * near[1] - near[0], slope_up)
        same, later = cross_terms(sd, cross_up, carry, slot)
        own = mask_up[:, here] * eps_ref[0, :, here] + (same - ef8[1]) + time_behind(later - ef8[0])
        eps = own + to_next(boundary(g_rows, n - 1, slope, here))
        eps_ref[1, :, here] = eps
        eps_ref[2, :, here] = to_next(ef8)
        bg_rows.store(n, here, (from_up(BG0, x0) + eps) * not_last)
        sd = sum_diff(eta_ref[:, wide])
        near = head(sd, CHUNK)
        ef8 = parts(slope_up * near[1] - near[0], slope_up)
        same, later = cross_terms(sd, cross_up, carry, slot + 1)
        own = mask_up[:, here] * eta_ref[:, here] + (same - ef8[1]) + time_behind(later - ef8[0])
        b2d_rows.store(n, here, (from_up(B2D0, x0) + own + to_next(boundary(bd_rows, n - 1, slope, here))) * not_last)
        slope_low = from_down(SJ1, x0)
        sd = sum_diff(epsb_ref[:, wide])
        near = head(sd, CHUNK)
        ef2 = parts(near[0] + slope_low * near[1], slope_low)
        same, later = cross_terms(sd, from_down(SC1, x0), carry, slot + 2)
        own = mask_down[:, here] * epsb_ref[:, here] + (same + ef2[0]) + time_behind(later + ef2[1])
        bg_rows.store(-1, here, (
            from_down(BG1, x0) + own + to_self(boundary(g_rows, -1, from_down(SI1, x0), here, not_first))
        ))
        return 0

    lax.fori_loop(0, chunks(x), first, 0)
    carry[...] = jnp.zeros(carry.shape, f32)

    def second(c, _):
        x0 = at_chunk(c)
        here = pl.ds(x0, CHUNK)
        wide = pl.ds(x0, CHUNK + LANES)
        slot = edges(x0, bg_rows, b2g_rows, 2, 0)
        slope_up = from_up(SI0, x0)
        sd = sum_diff(eps_ref[1, :, wide])
        near = head(sd, CHUNK)
        ef8 = parts(inline_res(near, sum_diff(eps_ref[2, :, here]), slope_up), slope_up)
        same, later = cross_terms(sd, from_up(SC0, x0), carry, slot)
        own = mask_up[:, here] * eps_ref[1, :, here] + (same - ef8[1]) + time_behind(later - ef8[0])
        b2g_rows.store(n, here, (
            from_up(B2G0, x0) + own + to_next(boundary(bg_rows, n - 1, si_ref[n, :, here], here))
        ) * not_last)
        return 0

    lax.fori_loop(0, chunks(x), second, 0)

    done = range(3, n - 3)
    done_inline = range(3, n - 4)
    loads = [rows.load for rows in (g_rows, bg_rows, b2g_rows)]
    loads += [lambda i, lanes: d_ref[i + 1, :, lanes], bd_rows.load, b2d_rows.load]

    def third(c, _):
        products(
            at_chunk(c), [i for i in range(n) if i not in done], [i for i in range(n) if i not in done_inline],
            loads, known4, si_ref, sc_ref, sums,
        )
        return 0

    lax.fori_loop(0, chunks(x), third, 0)
    for k in range(N_MOMENTS):
        moments_ref[pl.ds(k, 1), :] = jnp.sum(sums[k], axis=0, keepdims=True)
    moments_ref[pl.ds(N_MOMENTS, 24 - N_MOMENTS), :] = jnp.zeros((24 - N_MOMENTS, LANES), f32)


def add_terms(terms):
    total = None
    for term in terms:
        total = term if total is None else total + term
    return total


def solve(moments):
    mu, nu, xi = moments[:6], moments[6:12], moments[12:]

    def entry(a, b, i, j):
        if a == 0 and b == 0:
            return mu[i + j]
        if a == 1 and b == 1:
            return xi[i + j]
        return nu[i + j]

    shifted = {}

    def entry_a(a, b, i, j):
        which = a + b
        if (which, i + j) not in shifted:
            if i + j == 4:
                value = entry(a, b, 2, 3)
            else:
                value = entry(a, b, i, j + 1) + SHIFT * entry(a, b, i, j)
            shifted[which, i + j] = value * 0.25
        return shifted[which, i + j]

    def form(get, u, v):
        rows = []
        for (a, i), left in u.items():
            inner = add_terms(right * get(a, b, i, j) for (b, j), right in v.items())
            rows.append(left * inner)
        return add_terms(rows)

    def axpy(scale, u, v):
        out = dict(v)
        for key, value in u.items():
            term = scale * value
            out[key] = out[key] + term if key in out else term
        return out

    one = jnp.ones_like(mu[0])
    gradient = {(0, 0): 0.25 * one}
    direction = {(1, 0): one}
    model = {}
    for iteration in range(ITERS):
        mixing = -form(entry_a, gradient, direction) / form(entry_a, direction, direction)
        direction = axpy(mixing, direction, gradient)
        step = form(entry, gradient, direction) / form(entry_a, direction, direction)
        model = axpy(step, direction, model)
        if iteration < ITERS - 1:
            image = {key: value * (0.25 * SHIFT) for key, value in direction.items()}
            image = axpy(0.25, {(a, i + 1): value for (a, i), value in direction.items()}, image)
            gradient = axpy(-step, image, gradient)
    return model, direction


def last_kernel(
    n, x, moments_ref, m_ref, d_ref, g_in, bg_in, b2g_in, bd_in, b2d_in, g_end, bg_end, b2g_end, bd_end, b2d_end,
    model_hbm, dir_hbm, mo_ref, do_ref, sems,
):
    moments = [
        jnp.broadcast_to(jnp.sum(moments_ref[pl.ds(k, 1), :], axis=1, keepdims=True), (NT, LANES))
        for k in range(N_MOMENTS)
    ]
    model, direction = solve(moments)
    rows = mended(n, (g_in, bg_in, b2g_in, bd_in, b2d_in), (g_end, bg_end, b2g_end, bd_end, b2d_end))
    keys = ((0, 0), (0, 1), (0, 2), (1, 1), (1, 2))
    copies = []
    for i in range(n):
        def step(c, _):
            x0 = pl.multiple_of(c * LANES, LANES)
            here = pl.ds(x0, LANES)
            values = {key: vector.load(i, here) for key, vector in zip(keys, rows)}
            values[1, 0] = d_ref[i + 1, :, here]
            mo_ref[i, :, here] = m_ref[i + 1, :, here] + add_terms(
                model[key] * value for key, value in values.items())
            do_ref[i, :, here] = add_terms(direction[key] * value for key, value in values.items())
            return 0

        lax.fori_loop(0, x // LANES, step, 0, unroll=4)
        for k, (src, dst) in enumerate(((mo_ref, model_hbm), (do_ref, dir_hbm))):
            copy = pltpu.make_async_copy(src.at[i], dst.at[i], sems.at[2 * i + k])
            copy.start()
            copies.append(copy)
    for copy in copies:
        copy.wait()


def in_vmem(values):
    return [pltpu.with_memory_space_constraint(v, pltpu.VMEM) for v in values]


def kept(shape, dtype=f32):
    return pltpu.VMEM(shape, dtype)


def on_device(*args):
    n, _, x = args[0].shape
    peers = lax.axis_size("inline")
    vmem = pl.BlockSpec(memory_space=pltpu.VMEM)
    hbm = pl.BlockSpec(memory_space=pl.ANY)
    params = pltpu.CompilerParams(vmem_limit_bytes=VMEM_LIMIT)
    wide = kept((n + 2, NT, x + LANES))
    share = x // NT

    args = [pltpu.with_memory_space_constraint(v, pltpu.HBM) for v in args]
    up, down = pl.pallas_call(
        functools.partial(edge_kernel, n, x),
        out_shape=[kept((NT, 9 * x + share)), kept((NT, 8 * x + share))],
        in_specs=[hbm] * 6,
        out_specs=[vmem] * 2,
        scratch_shapes=[
            pltpu.VMEM((n, NT, x), f32),
            pltpu.VMEM((n, x), jnp.int32),
            pltpu.VMEM((n, NT, x), f32),
            pltpu.VMEM((n, NT, x), f32),
        ] + [pltpu.VMEM((n, NT, x + LANES), f32)] * 5 + [
            pltpu.VMEM((8, 2, NT, LANES), f32),
            pltpu.SemaphoreType.DMA((11,)),
        ],
        compiler_params=params,
        name="edges",
    )(*args)
    up = lax.ppermute(up, "inline", [(i, i - 1) for i in range(1, peers)])
    down = lax.ppermute(down, "inline", [(i, i + 1) for i in range(peers - 1)])

    local = pl.pallas_call(
        functools.partial(local_kernel, n, x),
        out_shape=[
            wide, wide, kept((n + 2, NT, x)), kept((n, NT, x)), kept((n, x), jnp.int32),
            wide, wide, wide, wide, wide, kept((N_MOMENTS, NT, LANES)),
        ],
        in_specs=[hbm] * 6,
        out_specs=[vmem] * 11,
        scratch_shapes=[
            pltpu.VMEM((n, NT, x), f32),
            pltpu.VMEM((2 * n, 2, NT, LANES), f32),
            pltpu.SemaphoreType.DMA((6,)),
        ],
        compiler_params=params,
        name="local",
    )(*args)
    m, d, _, _, _, g, bg, b2g, bd, b2d, _ = local

    out = pl.pallas_call(
        functools.partial(join_kernel, n, x),
        out_shape=[kept((2 * depth + 2, NT, x + LANES)) for depth in (1, 2, 3, 1, 2)]
        + [jax.ShapeDtypeStruct((24, LANES), f32)],
        in_specs=[vmem] * 13,
        out_specs=[vmem] * 6,
        scratch_shapes=[
            pltpu.VMEM((3, NT, x + LANES), f32),
            pltpu.VMEM((NT, x + LANES), f32),
            pltpu.VMEM((NT, x + LANES), f32),
            pltpu.VMEM((1, x), f32),
            pltpu.VMEM((1, x), f32),
            pltpu.VMEM((12, 2, NT, LANES), f32),
            pltpu.VMEM((N_MOMENTS, NT, LANES), f32),
        ],
        compiler_params=params,
        name="join",
    )(*in_vmem(local), up, down)
    *ends_out, moments = out

    reach = 1
    while reach < peers:
        moments = moments + lax.ppermute(moments, "inline", [(i, i ^ reach) for i in range(peers)])
        reach *= 2

    return pl.pallas_call(
        functools.partial(last_kernel, n, x),
        out_shape=[jax.ShapeDtypeStruct((n, NT, x), f32)] * 2,
        in_specs=[vmem] * 13,
        out_specs=[hbm] * 2,
        scratch_shapes=[
            pltpu.VMEM((n, NT, x), f32),
            pltpu.VMEM((n, NT, x), f32),
            pltpu.SemaphoreType.DMA((2 * n,)),
        ],
        compiler_params=params,
        name="last",
    )(moments, *in_vmem([m, d, g, bg, b2g, bd, b2d, *ends_out]))


def solution(mesh):
    rows = P(("groups", "inline"), None, None)
    return jax.shard_map(
        on_device,
        mesh=mesh,
        in_specs=(rows, P(("groups", "inline"), None), rows, rows, rows, rows),
        out_specs=(rows, rows),
        check_vma=False,
    )
```

time: 333 us -> 65.9 us (0.20)
  blocking collectives: 193 us -> 0 us
  other arithmetic: 44.1 us -> 0.01 us
  Pallas kernels: 0 us -> 37 us
  between operations: 32.2 us -> 0.69 us
  local copies, waits for them, and re-layouts: 18 us -> 0 us
  starting transfers between devices: 35.1 us -> 21.4 us
    psum x6 -> x0, blocking collectives: 193 us -> none  [the longest x3 103 us: on_device(): lax.psum((inner_sum(grad_image, dir_image), inner_sum(dir_image, dir_imag...]
    pallas_call x0 -> x4, Pallas kernels: none -> 37 us  [the longest x1 16.1 us: on_device(): pl.pallas_call(functools.partial(local_kernel, n, x), out_shape=[wide, wi...]
    reduce_sum x14 -> x0, other arithmetic: 34 us -> none  [the longest x6 16.6 us: inner_sum(): return total + jnp.sum(left_terms[2] * right_terms[2])]
    ppermute x15 -> x6, starting transfers between devices: 35.1 us -> 21.4 us  [the longest x4 17 us: on_device(): lax.ppermute(moments, 'inline', [(i, i ^ reach) for i in range(peers)])]
    slice x60 -> x0, local copies, waits for them, and re-layouts: 9.82 us -> none  [the longest x27 5.94 us: shift_ahead(): remaining = lax.slice_in_dim(values, 1, length_along, axis=along)]
    unnamed x76 -> x0, local copies, waits for them, and re-layouts: 8.23 us -> none
    add x3 -> x4, other arithmetic: 5.58 us -> 0.01 us  [on_device(): moments + lax.ppermute(moments, 'inline', [(i, i ^ reach) for i in range(...]
    mul x9 -> x0, other arithmetic: 3.64 us -> none  [the longest x3 2.58 us: on_device(): lower_inline = coefficients[0] * residual[1]]
  transfers between devices with their start and end apart: 15 -> 6, of which waited for: 7 -> 4; matrix products, arithmetic and copies ran while one was open for 3% -> 0% of each run, Pallas kernels for 0% -> 25%
where the time goes in v1:
time: 65.9 us; the launch traced here: 65.7 us
  Pallas kernels  37 us (56%)
  starting transfers between devices  21.4 us (32%)
  waiting for transfers between devices  6.63 us (10%)
  between operations  0.69 us (1%)
    ppermute x4, starting transfers between devices, on_device(): lax.ppermute(moments, 'inline', [(i, i ^ reach) for i in range(peers)])  17 us
    pallas_call x1, Pallas kernels, on_device(): pl.pallas_call(functools.partial(local_kernel, n, x), out_shape=[wide, wi...  16.1 us
    pallas_call x1, Pallas kernels, on_device(): pl.pallas_call(functools.partial(join_kernel, n, x), out_shape=[kept((2 *...  10.4 us
    pallas_call x1, Pallas kernels, on_device(): pl.pallas_call(functools.partial(edge_kernel, n, x), out_shape=[kept((NT,...  8.08 us
    ppermute x4, waiting for transfers between devices, on_device(): lax.ppermute(moments, 'inline', [(i, i ^ reach) for i in range(peers)])  6.63 us
    ppermute x1, starting transfers between devices, on_device(): down = lax.ppermute(down, 'inline', [(i, i + 1) for i in range(peers - 1)])  3.1 us
    pallas_call x1, Pallas kernels, on_device(): pl.pallas_call(functools.partial(last_kernel, n, x), out_shape=[jax.Shape...  2.37 us
  transfers between devices with their start and end apart: 6, of which 4 were waited for; matrix products, arithmetic and copies ran while one was open for 0% of the time, Pallas kernels for 25%

profile of v1, /device:TPU:0, one launch (start us, length us, event | category | flops | bytes accessed | tf_op | source)
XLA Modules:
  0.0 65.7 jit_solution(15352078127327036263)
XLA Ops:
  0.6 8.1 %edges.1 = (f32[8,37376]{1,0:T(8,128)S(1)}, f32[8,33280]{1,0:T(8,128)S(1)}) custom-call(f32[8,8,4096]{2,1,0:T(8,128)} %data_hbm.3, s32[8,4096]{1,0:T(8,128)} %mask_hbm.3, f32[8,8,4096]{2,1,0:T(8,128)} %si_hbm.3, f32[8,8,4096]{2,1,0:T(8,128)} %sc_hbm.3, f32[8,8,4096]{2,1,0:T(8,128)} %model_hbm.3, f32[8,8,4096]{2,1,0:T(8,128)} %dir_hbm.3), custom_call_target="tpu_custom_call" | custom-call | tf_op jit(solution)/shard_map/edges/pallas_call | solution.py:646
  8.7 1.3 %collective-permute-start = (f32[8,37376]{1,0:T(8,128)S(1)}, f32[8,37376]{1,0:T(8,128)S(1)}, u32[]{:S(2)}, u32[]{:S(2)}) collective-permute-start(f32[8,37376]{1,0:T(8,128)S(1)} %get-tuple-element.32), channel_id=1, source_target_pairs={{1,0},{2,1},{3,2},{4,3},{5,4},{6,5},{7,6},{8,7},{9,8},{10,9},{11,1... | collective-permute-start | bytes 3588104 | tf_op jit(solution)/shard_map/ppermute | solution.py:663
  10.0 3.1 %collective-permute-start.1 = (f32[8,33280]{1,0:T(8,128)S(1)}, f32[8,33280]{1,0:T(8,128)S(1)}, u32[]{:S(2)}, u32[]{:S(2)}) collective-permute-start(f32[8,33280]{1,0:T(8,128)S(1)} %get-tuple-element.33), channel_id=1, source_target_pairs={{0,1},{1,2},{2,3},{3,4},{4,5},{5,6},{6,7},{7,8},{8,9},{9,10},{10,1... | collective-permute-start | bytes 3194888 | tf_op jit(solution)/shard_map/ppermute | solution.py:664
  13.1 16.1 %local.1 = (f32[10,8,4224]{2,1,0:T(8,128)S(1)}, f32[10,8,4224]{2,1,0:T(8,128)S(1)}, f32[10,8,4096]{2,1,0:T(8,128)S(1)}, f32[8,8,4096]{2,1,0:T(8,128)S(1)}, s32[8...) custom-call(f32[8,8,4096]{2,1,0:T(8,128)} %data_hbm.3, ...), custom_call_target="tpu_custom_call" | custom-call | tf_op jit(solution)/shard_map/local/pallas_call | solution.py:666
  29.3 0.0 collective-permute-done.1.down_ref
  29.3 0.0 collective-permute-done.up_ref
  29.3 10.4 %join.1 = (f32[4,8,4224]{2,1,0:T(8,128)S(1)}, f32[6,8,4224]{2,1,0:T(8,128)S(1)}, f32[8,8,4224]{2,1,0:T(8,128)S(1)}, f32[4,8,4224]{2,1,0:T(8,128)S(1)}, f32[6,8,4224]{2,1,0:T(8,128)S(1)}, /*index=5*/f32[24,128]{1,0:T(8,128)S(1)}) custom-call(f32[10,8,4224]{2,1,0:T(8,128)S(1)} %get-tuple-element.21.m_ref, f32[10,8,4224]{2,1,0:T(8,128)S(1)} %get-tuple-element.22.d_ref, ...), custom_call_target="tpu_custom_call" | custom-call | tf_op jit(solution)/shard_map/join/pallas_call | solution.py:684
  39.7 10.1 %collective-permute-start.2 = (f32[24,128]{1,0:T(8,128)S(1)}, f32[24,128]{1,0:T(8,128)S(1)}, u32[]{:S(2)}, u32[]{:S(2)}) collective-permute-start(f32[24,128]{1,0:T(8,128)S(1)} %get-tuple-element.34), channel_id=1, source_target_pairs={{0,1},{1,0},{2,3},{3,2},{4,5},{5,4},{6,7},{7,6},{8,9},{9,8},{10,11... | collective-permute-start | bytes 36872 | tf_op jit(solution)/shard_map/ppermute | solution.py:706
  49.8 0.8 %collective-permute-done.2 = f32[24,128]{1,0:T(8,128)S(1)} collective-permute-done((f32[24,128]{1,0:T(8,128)S(1)}, f32[24,128]{1,0:T(8,128)S(1)}, u32[]{:S(2)}, u32[]{:S(2)}) %collective-permute-start.2) | collective-permute-done | bytes 12320 | tf_op jit(solution)/shard_map/ppermute | solution.py:706
  50.7 2.7 %collective-permute-start.3 = (f32[24,128]{1,0:T(8,128)S(1)}, f32[24,128]{1,0:T(8,128)S(1)}, u32[]{:S(2)}, u32[]{:S(2)}) collective-permute-start(f32[24,128]{1,0:T(8,128)S(1)} %add.12), channel_id=1, source_target_pairs={{0,2},{1,3},{2,0},{3,1},{4,6},{5,7},{6,4},{7,5},{8,10},{9,11},{10,... | collective-permute-start | bytes 36872 | tf_op jit(solution)/shard_map/ppermute | solution.py:706
  53.4 1.7 %collective-permute-done.3 = f32[24,128]{1,0:T(8,128)S(1)} collective-permute-done((f32[24,128]{1,0:T(8,128)S(1)}, f32[24,128]{1,0:T(8,128)S(1)}, u32[]{:S(2)}, u32[]{:S(2)}) %collective-permute-start.3) | collective-permute-done | bytes 12320 | tf_op jit(solution)/shard_map/ppermute | solution.py:706
  55.1 1.6 %collective-permute-start.4 = (f32[24,128]{1,0:T(8,128)S(1)}, f32[24,128]{1,0:T(8,128)S(1)}, u32[]{:S(2)}, u32[]{:S(2)}) collective-permute-start(f32[24,128]{1,0:T(8,128)S(1)} %add.13), channel_id=1, source_target_pairs={{0,4},{1,5},{2,6},{3,7},{4,0},{5,1},{6,2},{7,3},{8,12},{9,13},{10,... | collective-permute-start | bytes 36872 | tf_op jit(solution)/shard_map/ppermute | solution.py:706
  56.6 2.1 %collective-permute-done.4 = f32[24,128]{1,0:T(8,128)S(1)} collective-permute-done((f32[24,128]{1,0:T(8,128)S(1)}, f32[24,128]{1,0:T(8,128)S(1)}, u32[]{:S(2)}, u32[]{:S(2)}) %collective-permute-start.4) | collective-permute-done | bytes 12320 | tf_op jit(solution)/shard_map/ppermute | solution.py:706
  58.8 2.6 %collective-permute-start.5 = (f32[24,128]{1,0:T(8,128)S(1)}, f32[24,128]{1,0:T(8,128)S(1)}, u32[]{:S(2)}, u32[]{:S(2)}) collective-permute-start(f32[24,128]{1,0:T(8,128)S(1)} %add.14), channel_id=1, source_target_pairs={{0,8},{1,9},{2,10},{3,11},{4,12},{5,13},{6,14},{7,15},{8,0},{9,1},... | collective-permute-start | bytes 36872 | tf_op jit(solution)/shard_map/ppermute | solution.py:706
  61.4 2.0 %collective-permute-done.5 = f32[24,128]{1,0:T(8,128)S(1)} collective-permute-done((f32[24,128]{1,0:T(8,128)S(1)}, f32[24,128]{1,0:T(8,128)S(1)}, u32[]{:S(2)}, u32[]{:S(2)}) %collective-permute-start.5) | collective-permute-done | bytes 12320 | tf_op jit(solution)/shard_map/ppermute | solution.py:706
  63.4 2.4 %last.1 = (f32[8,8,4096]{2,1,0:T(8,128)}, f32[8,8,4096]{2,1,0:T(8,128)}) custom-call(f32[24,128]{1,0:T(8,128)S(1)} %add.15.moments_ref, f32[10,8,4224]{2,1,0:T(8,128)S(1)} %get-tuple-element.21.m_ref, f32[10,8,4224]{2,1,0:T(8,128)S(1)} %get-tuple-element.22.d_ref, f32[10,8,4224]{2,1,0:T(8,128)S(1)} %get-tuple-element.26.g_in, ...), custom_call_target="tpu_custom_call" | custom-call | tf_op jit(solution)/shard_map/last/pallas_call | solution.py:709
  (4 shorter events, 0.0 us)
Async XLA Ops:
  8.7 20.6 %collective-permute-start = (f32[8,37376]{1,0:T(8,128)S(1)}, f32[8,37376]{1,0:T(8,128)S(1)}, u32[]{:S(2)}, u32[]{:S(2)}) collective-permute-start(f32[8,37376]{1,0:T(8,128)S(1)} %get-tuple-element.32), channel_id=1, source_target_pairs={{1,0},{2,1},{3,2},{4,3},{5,4},{6,5},{7,6},{8,7},{9,8},{10,9},{11,1... | collective-permute-start | bytes 3588104 | tf_op jit(solution)/shard_map/ppermute | solution.py:663
  10.0 19.3 %collective-permute-start.1 = (f32[8,33280]{1,0:T(8,128)S(1)}, f32[8,33280]{1,0:T(8,128)S(1)}, u32[]{:S(2)}, u32[]{:S(2)}) collective-permute-start(f32[8,33280]{1,0:T(8,128)S(1)} %get-tuple-element.33), channel_id=1, source_target_pairs={{0,1},{1,2},{2,3},{3,4},{4,5},{5,6},{6,7},{7,8},{8,9},{9,10},{10,1... | collective-permute-start | bytes 3194888 | tf_op jit(solution)/shard_map/ppermute | solution.py:664
  39.7 10.9 %collective-permute-start.2 = (f32[24,128]{1,0:T(8,128)S(1)}, f32[24,128]{1,0:T(8,128)S(1)}, u32[]{:S(2)}, u32[]{:S(2)}) collective-permute-start(f32[24,128]{1,0:T(8,128)S(1)} %get-tuple-element.34), channel_id=1, source_target_pairs={{0,1},{1,0},{2,3},{3,2},{4,5},{5,4},{6,7},{7,6},{8,9},{9,8},{10,11... | collective-permute-start | bytes 36872 | tf_op jit(solution)/shard_map/ppermute | solution.py:706
  50.7 4.4 %collective-permute-start.3 = (f32[24,128]{1,0:T(8,128)S(1)}, f32[24,128]{1,0:T(8,128)S(1)}, u32[]{:S(2)}, u32[]{:S(2)}) collective-permute-start(f32[24,128]{1,0:T(8,128)S(1)} %add.12), channel_id=1, source_target_pairs={{0,2},{1,3},{2,0},{3,1},{4,6},{5,7},{6,4},{7,5},{8,10},{9,11},{10,... | collective-permute-start | bytes 36872 | tf_op jit(solution)/shard_map/ppermute | solution.py:706
  55.1 3.7 %collective-permute-start.4 = (f32[24,128]{1,0:T(8,128)S(1)}, f32[24,128]{1,0:T(8,128)S(1)}, u32[]{:S(2)}, u32[]{:S(2)}) collective-permute-start(f32[24,128]{1,0:T(8,128)S(1)} %add.13), channel_id=1, source_target_pairs={{0,4},{1,5},{2,6},{3,7},{4,0},{5,1},{6,2},{7,3},{8,12},{9,13},{10,... | collective-permute-start | bytes 36872 | tf_op jit(solution)/shard_map/ppermute | solution.py:706
  58.8 4.6 %collective-permute-start.5 = (f32[24,128]{1,0:T(8,128)S(1)}, f32[24,128]{1,0:T(8,128)S(1)}, u32[]{:S(2)}, u32[]{:S(2)}) collective-permute-start(f32[24,128]{1,0:T(8,128)S(1)} %add.14), channel_id=1, source_target_pairs={{0,8},{1,9},{2,10},{3,11},{4,12},{5,13},{6,14},{7,15},{8,0},{9,1},... | collective-permute-start | bytes 36872 | tf_op jit(solution)/shard_map/ppermute | solution.py:706

commit v2 on v1

--- a/solution.py
+++ b/solution.py
@@ -10,7 +10,7 @@
 ITERS = 3
 NT = 8
 LANES = 128
-CHUNK = 512
+CHUNK = 4096
 SHIFT = 18.0
 M0, D0, SI0, SC0, G0, BG0, B2G0, BD0, B2D0 = range(9)
 M1, D1, SI1, SC1, G1, BG1, BD1, SJ1 = range(8)

time: 65.9 us -> 60.3 us (0.915)
  Pallas kernels: 37 us -> 23.9 us
  starting transfers between devices: 21.4 us -> 28.7 us
    pallas_call x1, Pallas kernels: 16.1 us -> 8.84 us  [on_device(): pl.pallas_call(functools.partial(local_kernel, n, x), out_shape=[wide, wi...]
    ppermute x4, starting transfers between devices: 17 us -> 24.1 us  [on_device(): lax.ppermute(moments, 'inline', [(i, i ^ reach) for i in range(peers)])]
    pallas_call x1, Pallas kernels: 10.4 us -> 7.33 us  [on_device(): pl.pallas_call(functools.partial(join_kernel, n, x), out_shape=[kept((2 *...]
    pallas_call x1, Pallas kernels: 8.08 us -> 5.37 us  [on_device(): pl.pallas_call(functools.partial(edge_kernel, n, x), out_shape=[kept((NT,...]
  transfers between devices with their start and end apart: 6 -> 6, of which waited for: 4 -> 4; matrix products, arithmetic and copies ran while one was open for 0% -> 0% of each run, Pallas kernels for 25% -> 15%
where the time goes in v2:
time: 60.3 us; the launch traced here: 60.1 us
  starting transfers between devices  28.7 us (48%)
  Pallas kernels  23.9 us (40%)
  waiting for transfers between devices  6.63 us (11%)
  between operations  0.84 us (1%)
    ppermute x4, starting transfers between devices, on_device(): lax.ppermute(moments, 'inline', [(i, i ^ reach) for i in range(peers)])  24.1 us
    pallas_call x1, Pallas kernels, on_device(): pl.pallas_call(functools.partial(local_kernel, n, x), out_shape=[wide, wi...  8.84 us
    pallas_call x1, Pallas kernels, on_device(): pl.pallas_call(functools.partial(join_kernel, n, x), out_shape=[kept((2 *...  7.33 us
    ppermute x4, waiting for transfers between devices, on_device(): lax.ppermute(moments, 'inline', [(i, i ^ reach) for i in range(peers)])  6.63 us
    pallas_call x1, Pallas kernels, on_device(): pl.pallas_call(functools.partial(edge_kernel, n, x), out_shape=[kept((NT,...  5.37 us
    ppermute x1, starting transfers between devices, on_device(): down = lax.ppermute(down, 'inline', [(i, i + 1) for i in range(peers - 1)])  3.28 us
    pallas_call x1, Pallas kernels, on_device(): pl.pallas_call(functools.partial(last_kernel, n, x), out_shape=[jax.Shape...  2.37 us
    ppermute x1, starting transfers between devices, on_device(): up = lax.ppermute(up, 'inline', [(i, i - 1) for i in range(1, peers)])  1.29 us
  transfers between devices with their start and end apart: 6, of which 4 were waited for; matrix products, arithmetic and copies ran while one was open for 0% of the time, Pallas kernels for 15%

profile of v2, /device:TPU:0, one launch (start us, length us, event | category | flops | bytes accessed | tf_op | source)
XLA Modules:
  0.0 60.1 jit_solution(847791391887101855)
XLA Ops:
  0.6 5.4 %edges.1 = (f32[8,37376]{1,0:T(8,128)S(1)}, f32[8,33280]{1,0:T(8,128)S(1)}) custom-call(f32[8,8,4096]{2,1,0:T(8,128)} %data_hbm.3, s32[8,4096]{1,0:T(8,128)} %mask_hbm.3, f32[8,8,4096]{2,1,0:T(8,128)} %si_hbm.3, f32[8,8,4096]{2,1,0:T(8,128)} %sc_hbm.3, f32[8,8,4096]{2,1,0:T(8,128)} %model_hbm.3, f32[8,8,4096]{2,1,0:T(8,128)} %dir_hbm.3), custom_call_target="tpu_custom_call" | custom-call | tf_op jit(solution)/shard_map/edges/pallas_call | solution.py:646
  6.0 1.3 %collective-permute-start = (f32[8,37376]{1,0:T(8,128)S(1)}, f32[8,37376]{1,0:T(8,128)S(1)}, u32[]{:S(2)}, u32[]{:S(2)}) collective-permute-start(f32[8,37376]{1,0:T(8,128)S(1)} %get-tuple-element.32), channel_id=1, source_target_pairs={{1,0},{2,1},{3,2},{4,3},{5,4},{6,5},{7,6},{8,7},{9,8},{10,9},{11,1... | collective-permute-start | bytes 3588104 | tf_op jit(solution)/shard_map/ppermute | solution.py:663
  7.3 3.3 %collective-permute-start.1 = (f32[8,33280]{1,0:T(8,128)S(1)}, f32[8,33280]{1,0:T(8,128)S(1)}, u32[]{:S(2)}, u32[]{:S(2)}) collective-permute-start(f32[8,33280]{1,0:T(8,128)S(1)} %get-tuple-element.33), channel_id=1, source_target_pairs={{0,1},{1,2},{2,3},{3,4},{4,5},{5,6},{6,7},{7,8},{8,9},{9,10},{10,1... | collective-permute-start | bytes 3194888 | tf_op jit(solution)/shard_map/ppermute | solution.py:664
  10.6 8.8 %local.1 = (f32[10,8,4224]{2,1,0:T(8,128)S(1)}, f32[10,8,4224]{2,1,0:T(8,128)S(1)}, f32[10,8,4096]{2,1,0:T(8,128)S(1)}, f32[8,8,4096]{2,1,0:T(8,128)S(1)}, s32[8...) custom-call(f32[8,8,4096]{2,1,0:T(8,128)} %data_hbm.3, ...), custom_call_target="tpu_custom_call" | custom-call | tf_op jit(solution)/shard_map/local/pallas_call | solution.py:666
  19.4 0.0 collective-permute-done.1.down_ref
  19.5 0.0 collective-permute-done.up_ref
  19.5 7.3 %join.1 = (f32[4,8,4224]{2,1,0:T(8,128)S(1)}, f32[6,8,4224]{2,1,0:T(8,128)S(1)}, f32[8,8,4224]{2,1,0:T(8,128)S(1)}, f32[4,8,4224]{2,1,0:T(8,128)S(1)}, f32[6,8,4224]{2,1,0:T(8,128)S(1)}, /*index=5*/f32[24,128]{1,0:T(8,128)S(1)}) custom-call(f32[10,8,4224]{2,1,0:T(8,128)S(1)} %get-tuple-element.21.m_ref, f32[10,8,4224]{2,1,0:T(8,128)S(1)} %get-tuple-element.22.d_ref, ...), custom_call_target="tpu_custom_call" | custom-call | tf_op jit(solution)/shard_map/join/pallas_call | solution.py:684
  26.8 17.2 %collective-permute-start.2 = (f32[24,128]{1,0:T(8,128)S(1)}, f32[24,128]{1,0:T(8,128)S(1)}, u32[]{:S(2)}, u32[]{:S(2)}) collective-permute-start(f32[24,128]{1,0:T(8,128)S(1)} %get-tuple-element.34), channel_id=1, source_target_pairs={{0,1},{1,0},{2,3},{3,2},{4,5},{5,4},{6,7},{7,6},{8,9},{9,8},{10,11... | collective-permute-start | bytes 36872 | tf_op jit(solution)/shard_map/ppermute | solution.py:706
  44.0 0.8 %collective-permute-done.2 = f32[24,128]{1,0:T(8,128)S(1)} collective-permute-done((f32[24,128]{1,0:T(8,128)S(1)}, f32[24,128]{1,0:T(8,128)S(1)}, u32[]{:S(2)}, u32[]{:S(2)}) %collective-permute-start.2) | collective-permute-done | bytes 12320 | tf_op jit(solution)/shard_map/ppermute | solution.py:706
  44.9 2.7 %collective-permute-start.3 = (f32[24,128]{1,0:T(8,128)S(1)}, f32[24,128]{1,0:T(8,128)S(1)}, u32[]{:S(2)}, u32[]{:S(2)}) collective-permute-start(f32[24,128]{1,0:T(8,128)S(1)} %add.12), channel_id=1, source_target_pairs={{0,2},{1,3},{2,0},{3,1},{4,6},{5,7},{6,4},{7,5},{8,10},{9,11},{10,... | collective-permute-start | bytes 36872 | tf_op jit(solution)/shard_map/ppermute | solution.py:706
  47.6 1.7 %collective-permute-done.3 = f32[24,128]{1,0:T(8,128)S(1)} collective-permute-done((f32[24,128]{1,0:T(8,128)S(1)}, f32[24,128]{1,0:T(8,128)S(1)}, u32[]{:S(2)}, u32[]{:S(2)}) %collective-permute-start.3) | collective-permute-done | bytes 12320 | tf_op jit(solution)/shard_map/ppermute | solution.py:706
  49.2 1.6 %collective-permute-start.4 = (f32[24,128]{1,0:T(8,128)S(1)}, f32[24,128]{1,0:T(8,128)S(1)}, u32[]{:S(2)}, u32[]{:S(2)}) collective-permute-start(f32[24,128]{1,0:T(8,128)S(1)} %add.13), channel_id=1, source_target_pairs={{0,4},{1,5},{2,6},{3,7},{4,0},{5,1},{6,2},{7,3},{8,12},{9,13},{10,... | collective-permute-start | bytes 36872 | tf_op jit(solution)/shard_map/ppermute | solution.py:706
  50.8 2.1 %collective-permute-done.4 = f32[24,128]{1,0:T(8,128)S(1)} collective-permute-done((f32[24,128]{1,0:T(8,128)S(1)}, f32[24,128]{1,0:T(8,128)S(1)}, u32[]{:S(2)}, u32[]{:S(2)}) %collective-permute-start.4) | collective-permute-done | bytes 12320 | tf_op jit(solution)/shard_map/ppermute | solution.py:706
  52.9 2.6 %collective-permute-start.5 = (f32[24,128]{1,0:T(8,128)S(1)}, f32[24,128]{1,0:T(8,128)S(1)}, u32[]{:S(2)}, u32[]{:S(2)}) collective-permute-start(f32[24,128]{1,0:T(8,128)S(1)} %add.14), channel_id=1, source_target_pairs={{0,8},{1,9},{2,10},{3,11},{4,12},{5,13},{6,14},{7,15},{8,0},{9,1},... | collective-permute-start | bytes 36872 | tf_op jit(solution)/shard_map/ppermute | solution.py:706
  55.5 2.0 %collective-permute-done.5 = f32[24,128]{1,0:T(8,128)S(1)} collective-permute-done((f32[24,128]{1,0:T(8,128)S(1)}, f32[24,128]{1,0:T(8,128)S(1)}, u32[]{:S(2)}, u32[]{:S(2)}) %collective-permute-start.5) | collective-permute-done | bytes 12320 | tf_op jit(solution)/shard_map/ppermute | solution.py:706
  57.5 2.4 %last.1 = (f32[8,8,4096]{2,1,0:T(8,128)}, f32[8,8,4096]{2,1,0:T(8,128)}) custom-call(f32[24,128]{1,0:T(8,128)S(1)} %add.15.moments_ref, f32[10,8,4224]{2,1,0:T(8,128)S(1)} %get-tuple-element.21.m_ref, f32[10,8,4224]{2,1,0:T(8,128)S(1)} %get-tuple-element.22.d_ref, f32[10,8,4224]{2,1,0:T(8,128)S(1)} %get-tuple-element.26.g_in, ...), custom_call_target="tpu_custom_call" | custom-call | tf_op jit(solution)/shard_map/last/pallas_call | solution.py:709
  (4 shorter events, 0.0 us)
Async XLA Ops:
  6.0 13.5 %collective-permute-start = (f32[8,37376]{1,0:T(8,128)S(1)}, f32[8,37376]{1,0:T(8,128)S(1)}, u32[]{:S(2)}, u32[]{:S(2)}) collective-permute-start(f32[8,37376]{1,0:T(8,128)S(1)} %get-tuple-element.32), channel_id=1, source_target_pairs={{1,0},{2,1},{3,2},{4,3},{5,4},{6,5},{7,6},{8,7},{9,8},{10,9},{11,1... | collective-permute-start | bytes 3588104 | tf_op jit(solution)/shard_map/ppermute | solution.py:663
  7.3 12.1 %collective-permute-start.1 = (f32[8,33280]{1,0:T(8,128)S(1)}, f32[8,33280]{1,0:T(8,128)S(1)}, u32[]{:S(2)}, u32[]{:S(2)}) collective-permute-start(f32[8,33280]{1,0:T(8,128)S(1)} %get-tuple-element.33), channel_id=1, source_target_pairs={{0,1},{1,2},{2,3},{3,4},{4,5},{5,6},{6,7},{7,8},{8,9},{9,10},{10,1... | collective-permute-start | bytes 3194888 | tf_op jit(solution)/shard_map/ppermute | solution.py:664
  26.8 18.1 %collective-permute-start.2 = (f32[24,128]{1,0:T(8,128)S(1)}, f32[24,128]{1,0:T(8,128)S(1)}, u32[]{:S(2)}, u32[]{:S(2)}) collective-permute-start(f32[24,128]{1,0:T(8,128)S(1)} %get-tuple-element.34), channel_id=1, source_target_pairs={{0,1},{1,0},{2,3},{3,2},{4,5},{5,4},{6,7},{7,6},{8,9},{9,8},{10,11... | collective-permute-start | bytes 36872 | tf_op jit(solution)/shard_map/ppermute | solution.py:706
  44.9 4.4 %collective-permute-start.3 = (f32[24,128]{1,0:T(8,128)S(1)}, f32[24,128]{1,0:T(8,128)S(1)}, u32[]{:S(2)}, u32[]{:S(2)}) collective-permute-start(f32[24,128]{1,0:T(8,128)S(1)} %add.12), channel_id=1, source_target_pairs={{0,2},{1,3},{2,0},{3,1},{4,6},{5,7},{6,4},{7,5},{8,10},{9,11},{10,... | collective-permute-start | bytes 36872 | tf_op jit(solution)/shard_map/ppermute | solution.py:706
  49.2 3.7 %collective-permute-start.4 = (f32[24,128]{1,0:T(8,128)S(1)}, f32[24,128]{1,0:T(8,128)S(1)}, u32[]{:S(2)}, u32[]{:S(2)}) collective-permute-start(f32[24,128]{1,0:T(8,128)S(1)} %add.13), channel_id=1, source_target_pairs={{0,4},{1,5},{2,6},{3,7},{4,0},{5,1},{6,2},{7,3},{8,12},{9,13},{10,... | collective-permute-start | bytes 36872 | tf_op jit(solution)/shard_map/ppermute | solution.py:706
  52.9 4.6 %collective-permute-start.5 = (f32[24,128]{1,0:T(8,128)S(1)}, f32[24,128]{1,0:T(8,128)S(1)}, u32[]{:S(2)}, u32[]{:S(2)}) collective-permute-start(f32[24,128]{1,0:T(8,128)S(1)} %add.14), channel_id=1, source_target_pairs={{0,8},{1,9},{2,10},{3,11},{4,12},{5,13},{6,14},{7,15},{8,0},{9,1},... | collective-permute-start | bytes 36872 | tf_op jit(solution)/shard_map/ppermute | solution.py:706

commit v3 on v2

v3 whole, which is shorter than its diff:
```python
import functools

import jax
import jax.numpy as jnp
from jax import lax
from jax.experimental import pallas as pl
from jax.experimental.pallas import tpu as pltpu
from jax.sharding import PartitionSpec as P

ITERS = 3
NT = 8
LANES = 128
CHUNK = 4096
SHIFT = 18.0
M0, D0, SI0, SC0, G0, BD0, FIRST0 = range(7)
BG0, B2D0, B2G0, LATE0 = range(4)
M1, D1, SI1, SC1, SJ1, G1, BD1, FIRST1 = range(8)
BG1, LATE1 = range(2)
N_MOMENTS = 18
VMEM_LIMIT = 16 * 1024 * 1024

f32 = jnp.float32


def time_ahead(v):
    rolled = pltpu.roll(v, NT - 1, 0)
    return jnp.where(lax.broadcasted_iota(jnp.int32, v.shape, 0) == NT - 1, 0.0, rolled)


def time_behind(v):
    rolled = pltpu.roll(v, 1, 0)
    return jnp.where(lax.broadcasted_iota(jnp.int32, v.shape, 0) == 0, 0.0, rolled)


def sum_diff(v):
    ahead = time_ahead(v)
    return ahead + v, ahead - v


def head(pair, width):
    return pair[0][:, :width], pair[1][:, :width]


def inline_res(here, after, slope):
    return (after[0] - here[0]) + slope * (after[1] + here[1])


def parts(res, slope):
    scaled = slope * res
    return res - scaled, res + scaled


def to_next(ef):
    return ef[0] + time_behind(ef[1])


def to_self(ef):
    return -(ef[1] + time_behind(ef[0]))


def lane_ahead(v):
    width = v.shape[1]
    return pltpu.roll(v, width - 1, 1)[:, : width - LANES]


def lane_behind(before, v):
    joined = jnp.concatenate([before, v], axis=1)
    return pltpu.roll(joined, 1, 1)[:, LANES:]


def cross_res(sd, slope):
    width = sd[0].shape[1] - LANES
    here = head(sd, width)
    return (lane_ahead(sd[0]) - here[0]) + slope * (lane_ahead(sd[1]) + here[1])


def cross_terms(sd, slope, carry, slot):
    e, f = parts(cross_res(sd, slope), slope)
    e_behind = lane_behind(carry[slot, 0], e)
    f_behind = lane_behind(carry[slot, 1], f)
    carry[slot, 0] = e[:, -LANES:]
    carry[slot, 1] = f[:, -LANES:]
    return e_behind - f, f_behind - e


def stencil(load, slope_in, slope_cr, lo, hi, res_lo, res_hi, carry, slot, scale_lo=None):
    out = {}
    sd = {}

    def pair(i):
        if i not in sd:
            sd[i] = sum_diff(load(i))
        return sd[i]

    before = None
    for i in range(lo - 1, hi + 1):
        here = None
        if res_lo <= i <= res_hi:
            first = pair(i)
            second = pair(i + 1)
            width = first[0].shape[1] - LANES
            slope = slope_in(i)
            res = inline_res(head(first, width), head(second, width), slope)
            if i == -1 and scale_lo is not None:
                res = res * scale_lo
            here = parts(res, slope)
        if i >= lo:
            same, later = cross_terms(pair(i), slope_cr(i), carry, slot + i - lo)
            if before is not None:
                same = same + before[0]
                later = later + before[1]
            if here is not None:
                same = same - here[1]
                later = later - here[0]
            out[i] = same + time_behind(later)
        before = here
    return out


class Mended:
    def __init__(self, n, depth, whole, ends, before=None, after=None):
        self.n, self.depth, self.whole, self.ends, self.before, self.after = n, depth, whole, ends, before, after

    def at(self, i):
        if i < 0:
            return self.before
        if i >= self.n:
            return self.after
        if i < self.depth:
            return self.ends, i
        if i >= self.n - self.depth:
            return self.ends, i - self.n + 2 * self.depth
        return self.whole, i + 1

    def load(self, i, lanes):
        ref, row = self.at(i)
        return ref[row, :, lanes]

    def store(self, i, lanes, value):
        ref, row = self.at(i)
        ref[row, :, lanes] = value


def chunks(x):
    return x // CHUNK


def at_chunk(c):
    return pl.multiple_of(c * CHUNK, CHUNK)


class Own:
    def __init__(self, n, x0, si_ref, sc_ref, mask_ref, carry):
        self.n, self.x0, self.here = n, x0, pl.ds(x0, CHUNK)
        self.si_ref, self.sc_ref, self.mask_ref, self.carry = si_ref, sc_ref, mask_ref, carry

    def known4(self, i):
        return self.mask_ref[pl.ds(i, 1), self.here].astype(f32) * 4.0

    def level(self, src, lo, hi, slot):
        return stencil(
            lambda i: src[i + 1, :, pl.ds(self.x0, CHUNK + LANES)],
            lambda i: self.si_ref[i + 1, :, self.here],
            lambda i: self.sc_ref[i, :, self.here],
            lo, hi, 0, self.n - 2, self.carry, slot,
        )

    def applied(self, src, lo, hi, slot):
        out = self.level(src, lo, hi, slot)
        return {i: (self.known4(i) - SHIFT) * src[i + 1, :, self.here] + out[i] for i in out}

    def gradient(self, data_ref, m_ref, lo, hi, slot):
        out = self.level(m_ref, lo, hi, slot)
        return {i: self.known4(i) * (data_ref[i, :, self.here] - m_ref[i + 1, :, self.here]) - out[i] for i in out}


def put(ref, slot, x, x0, value):
    ref[:, pl.ds(pl.multiple_of(x0 + slot * x, CHUNK), CHUNK)] = value


def first_kernel(
    n, x,
    data_hbm, mask_hbm, si_hbm, sc_hbm, model_hbm, dir_hbm,
    data_ref, mask_ref, si_ref, sc_ref, m_ref, d_ref, up_ref, down_ref,
    carry, sems,
):
    body = (pl.ds(1, n), slice(None), pl.ds(0, x))
    copies = [
        pltpu.make_async_copy(source, target, sems.at[k])
        for k, (source, target) in enumerate((
            (model_hbm, m_ref.at[body]), (dir_hbm, d_ref.at[body]), (si_hbm, si_ref.at[pl.ds(1, n)]), (sc_hbm, sc_ref),
            (mask_hbm, mask_ref), (data_hbm, data_ref),
        ))
    ]
    for copy in copies:
        copy.start()
    clear_pads(x, (m_ref, d_ref))
    carry[...] = jnp.zeros(carry.shape, f32)
    for copy in copies:
        copy.wait()
    share = x // NT
    for s in range(NT):
        up_ref[pl.ds(s, 1), pl.ds(FIRST0 * x, share)] = mask_ref[pl.ds(0, 1), pl.ds(s * share, share)].astype(f32)
        down_ref[pl.ds(s, 1), pl.ds(FIRST1 * x, share)] = mask_ref[pl.ds(n - 1, 1), pl.ds(s * share, share)].astype(f32)

    def rows(c, _):
        x0 = at_chunk(c)
        here = pl.ds(x0, CHUNK)
        own = Own(n, x0, si_ref, sc_ref, mask_ref, carry)
        put(up_ref, G0, x, x0, own.gradient(data_ref, m_ref, 0, 0, 0)[0])
        put(up_ref, BD0, x, x0, own.applied(d_ref, 0, 0, 1)[0])
        put(down_ref, G1, x, x0, own.gradient(data_ref, m_ref, n - 1, n - 1, 2)[n - 1])
        put(down_ref, BD1, x, x0, own.applied(d_ref, n - 1, n - 1, 3)[n - 1])
        put(up_ref, M0, x, x0, m_ref[1, :, here])
        put(up_ref, D0, x, x0, d_ref[1, :, here])
        put(up_ref, SI0, x, x0, si_ref[1, :, here])
        put(up_ref, SC0, x, x0, sc_ref[0, :, here])
        put(down_ref, M1, x, x0, m_ref[n, :, here])
        put(down_ref, D1, x, x0, d_ref[n, :, here])
        put(down_ref, SI1, x, x0, si_ref[n, :, here])
        put(down_ref, SC1, x, x0, sc_ref[n - 1, :, here])
        put(down_ref, SJ1, x, x0, si_ref[n - 1, :, here])
        return 0

    lax.fori_loop(0, chunks(x), rows, 0)


def edge_kernel(
    n, x, data_ref, mask_ref, si_ref, sc_ref, m_ref, d_ref, up_first, down_first, up_ref, down_ref,
    g_ref, bg_ref, bd_ref, carry,
):
    clear_pads(x, (g_ref, bg_ref, bd_ref))
    carry[...] = jnp.zeros(carry.shape, f32)

    def first(c, _):
        x0 = at_chunk(c)
        here = pl.ds(x0, CHUNK)
        own = Own(n, x0, si_ref, sc_ref, mask_ref, carry)
        for i, value in {**own.gradient(data_ref, m_ref, 1, 2, 0), **own.gradient(data_ref, m_ref, n - 2, n - 2, 2)}.items():
            g_ref[i + 1, :, here] = value
        g_ref[1, :, here] = row_of(up_first, G0, x, x0)
        g_ref[n, :, here] = row_of(down_first, G1, x, x0)
        bd_ref[1, :, here] = row_of(up_first, BD0, x, x0)
        bd_ref[2, :, here] = own.applied(d_ref, 1, 1, 3)[1]
        return 0

    lax.fori_loop(0, chunks(x), first, 0)
    carry[...] = jnp.zeros(carry.shape, f32)

    def second(c, _):
        x0 = at_chunk(c)
        here = pl.ds(x0, CHUNK)
        own = Own(n, x0, si_ref, sc_ref, mask_ref, carry)
        out = own.applied(g_ref, 0, 1, 0)
        for i in (0, 1):
            bg_ref[i + 1, :, here] = out[i]
        put(up_ref, BG0, x, x0, out[0])
        put(down_ref, BG1, x, x0, own.applied(g_ref, n - 1, n - 1, 2)[n - 1])
        put(up_ref, B2D0, x, x0, own.applied(bd_ref, 0, 0, 3)[0])
        return 0

    lax.fori_loop(0, chunks(x), second, 0)
    carry[...] = jnp.zeros(carry.shape, f32)

    def third(c, _):
        x0 = at_chunk(c)
        put(up_ref, B2G0, x, x0, Own(n, x0, si_ref, sc_ref, mask_ref, carry).applied(bg_ref, 0, 0, 0)[0])
        return 0

    lax.fori_loop(0, chunks(x), third, 0)


def local_kernel(
    n, x, data_ref, mask_ref, si_ref, sc_ref, m_ref, d_ref,
    g_ref, bg_ref, b2g_ref, bd_ref, b2d_ref, sums_ref, carry,
):
    clear_pads(x, (g_ref, bg_ref, b2g_ref, bd_ref, b2d_ref))
    carry[...] = jnp.zeros(carry.shape, f32)
    sums_ref[...] = jnp.zeros(sums_ref.shape, f32)

    def first(c, _):
        x0 = at_chunk(c)
        own = Own(n, x0, si_ref, sc_ref, mask_ref, carry)
        for i, value in own.gradient(data_ref, m_ref, 0, n - 1, 0).items():
            g_ref[i + 1, :, own.here] = value
        for i, value in own.applied(d_ref, 0, n - 1, n).items():
            bd_ref[i + 1, :, own.here] = value
        return 0

    lax.fori_loop(0, chunks(x), first, 0)
    carry[...] = jnp.zeros(carry.shape, f32)

    def second(c, _):
        x0 = at_chunk(c)
        own = Own(n, x0, si_ref, sc_ref, mask_ref, carry)
        for i, value in own.applied(g_ref, 2, n - 3, 0).items():
            bg_ref[i + 1, :, own.here] = value
        for i, value in own.applied(bd_ref, 2, n - 3, n).items():
            b2d_ref[i + 1, :, own.here] = value
        return 0

    lax.fori_loop(0, chunks(x), second, 0)
    carry[...] = jnp.zeros(carry.shape, f32)

    def third(c, _):
        x0 = at_chunk(c)
        own = Own(n, x0, si_ref, sc_ref, mask_ref, carry)
        for i, value in own.applied(bg_ref, 3, n - 4, 0).items():
            b2g_ref[i + 1, :, own.here] = value
        return 0

    lax.fori_loop(0, chunks(x), third, 0)

    def fourth(c, _):
        x0 = at_chunk(c)
        here = pl.ds(x0, CHUNK)
        own = Own(n, x0, si_ref, sc_ref, mask_ref, carry)
        refs = (g_ref, bg_ref, b2g_ref, d_ref, bd_ref, b2d_ref)
        totals = Totals()
        pairs = [Pairs(lambda i, lanes, ref=ref: ref[i + 1, :, lanes], x0) for ref in (b2g_ref, b2d_ref)]
        for i in range(3, n - 3):
            values = [ref[i + 1, :, here] for ref in refs]
            for k, which in enumerate(PAIRS):
                if which is not None:
                    totals.add(k, values[which[0]], values[which[1]])
            known = own.known4(i)
            members = [(values[2], values[5], known * values[2], known * values[5])]
            members.append(tuple(pair.cross(i, sc_ref[i, :, here]) for pair in pairs) * 2)
            if i < n - 4:
                members.append(tuple(pair.inline(i, si_ref[i + 1, :, here]) for pair in pairs) * 2)
            for u, v, also_u, also_v in members:
                totals.add(5, u, also_u)
                totals.add(11, v, also_u)
                totals.add(17, v, also_v)
        totals.put(sums_ref)
        return 0

    lax.fori_loop(0, chunks(x), fourth, 0)


PAIRS = ((0, 0), (0, 1), (1, 1), (1, 2), (2, 2), None, (0, 3), (0, 4), (1, 4), (1, 5), (2, 5), None,
         (3, 3), (3, 4), (4, 4), (4, 5), (5, 5), None)


class Totals:
    def __init__(self):
        self.of = {}

    def add(self, k, left, right):
        product = left * right
        acc = product[:, :LANES]
        for j in range(1, CHUNK // LANES):
            acc = acc + product[:, j * LANES:(j + 1) * LANES]
        self.of[k] = self.of[k] + acc if k in self.of else acc

    def put(self, sums):
        for k, value in self.of.items():
            sums[k] = sums[k] + value


class Pairs:
    def __init__(self, load, x0):
        self.load, self.lanes, self.of = load, pl.ds(x0, CHUNK + LANES), {}

    def at(self, i):
        if i not in self.of:
            self.of[i] = sum_diff(self.load(i, self.lanes))
        return self.of[i]

    def inline(self, i, slope):
        return inline_res(head(self.at(i), CHUNK), head(self.at(i + 1), CHUNK), slope)

    def cross(self, i, slope):
        return cross_res(self.at(i), slope)


def place_flags():
    place = lax.axis_index("inline")
    return (place > 0).astype(f32), (place < lax.axis_size("inline") - 1).astype(f32)


def row_of(ref, slot, x, x0):
    return ref[:, pl.ds(pl.multiple_of(x0 + slot * x, CHUNK), CHUNK)]


def boundary(rows, i, slope, here, scale=None):
    res = inline_res(sum_diff(rows.load(i, here)), sum_diff(rows.load(i + 1, here)), slope)
    if scale is not None:
        res = res * scale
    return parts(res, slope)


def clear_pads(x, refs):
    for ref in refs:
        for i in range(ref.shape[0]):
            ref[i, :, pl.ds(x, LANES)] = jnp.zeros((NT, LANES), f32)


def end_rows(n, x0, src, dst, depth, slope_before, si_ref, sc_ref, known4, scale, carry, slot):
    here = pl.ds(x0, CHUNK)
    for lo, hi in ((0, depth), (n - 1 - depth, n - 1)):
        out = stencil(
            lambda i: src.load(i, pl.ds(x0, CHUNK + LANES)),
            lambda i: slope_before if i == -1 else si_ref[i + 1, :, here],
            lambda i: sc_ref[i, :, here],
            lo, hi, -1, n - 1, carry, slot, scale,
        )
        for i in range(lo, hi + 1):
            dst.store(i, here, (known4(i, x0) - SHIFT) * src.load(i, here) + out[i])
        slot += hi - lo + 1
    return slot


def beyond(rows_ref, row, wide, width, diagonal, cross, slope_inner, carry, slot, after, further=None):
    here = pl.ds(wide.start, width)
    sd = sum_diff(rows_ref[row, :, wide])
    near = head(sd, width)
    same, later = cross_terms(sd, cross, carry, slot)
    if after:
        if further is None:
            inner = parts(slope_inner * near[1] - near[0], slope_inner)
        else:
            inner = parts(inline_res(near, sum_diff(further), slope_inner), slope_inner)
        same, later = same - inner[1], later - inner[0]
    else:
        inner = parts(near[0] + slope_inner * near[1], slope_inner)
        same, later = same + inner[0], later + inner[1]
    return diagonal * rows_ref[row, :, here] + same + time_behind(later), inner


def join_kernel(
    n, x,
    m_ref, d_ref, si_ref, sc_ref, mask_ref, g_in, bg_in, bd_in, b2d_in, sums_in, up_ref, down_ref,
    g_out, bg_out, bd_out, b2d_out, sums, eps_out, res_out, mask_up,
    eps_ref, ghosts, mask_down, carry,
):
    not_first, not_last = place_flags()
    share = x // NT
    clear_pads(x, (eps_ref, eps_out, ghosts, g_out, bg_out, bd_out, b2d_out))
    carry[...] = jnp.zeros(carry.shape, f32)
    sums[...] = sums_in[...]
    for s in range(NT):
        mask_up[:, pl.ds(s * share, share)] = up_ref[pl.ds(s, 1), pl.ds(FIRST0 * x, share)] * 4.0 - SHIFT
        mask_down[:, pl.ds(s * share, share)] = down_ref[pl.ds(s, 1), pl.ds(FIRST1 * x, share)] * 4.0 - SHIFT
    g_rows = Mended(n, 1, g_in, g_out, (ghosts, 0), (ghosts, 1))
    bd_rows = Mended(n, 1, bd_in, bd_out, (ghosts, 2), (ghosts, 3))
    bg_rows = Mended(n, 2, bg_in, bg_out)
    b2d_rows = Mended(n, 2, b2d_in, b2d_out)

    def known4(i, x0):
        return mask_ref[pl.ds(i, 1), pl.ds(x0, CHUNK)].astype(f32) * 4.0

    def zeroth(c, _):
        x0 = at_chunk(c)
        here = pl.ds(x0, CHUNK)
        slope = si_ref[n, :, here]
        ef = parts(inline_res(sum_diff(m_ref[n, :, here]), sum_diff(row_of(up_ref, M0, x, x0)), slope), slope)
        eps = -to_next(ef)
        eps_ref[0, :, here] = eps
        g_rows.store(n, here, (row_of(up_ref, G0, x, x0) + eps) * not_last)
        g_rows.store(n - 1, here, g_in[n, :, here] - to_self(ef))
        ef = parts(inline_res(sum_diff(d_ref[n, :, here]), sum_diff(row_of(up_ref, D0, x, x0)), slope), slope)
        eps = to_next(ef)
        eps_ref[1, :, here] = eps
        bd_rows.store(n, here, (row_of(up_ref, BD0, x, x0) + eps) * not_last)
        bd_rows.store(n - 1, here, bd_in[n, :, here] + to_self(ef))

        slope = row_of(down_ref, SI1, x, x0)
        res = inline_res(sum_diff(row_of(down_ref, M1, x, x0)), sum_diff(m_ref[1, :, here]), slope) * not_first
        ef = parts(res, slope)
        eps = -to_self(ef)
        eps_ref[2, :, here] = eps
        g_rows.store(-1, here, row_of(down_ref, G1, x, x0) + eps)
        g_rows.store(0, here, g_in[1, :, here] - to_next(ef))
        res = inline_res(sum_diff(row_of(down_ref, D1, x, x0)), sum_diff(d_ref[1, :, here]), slope) * not_first
        ef = parts(res, slope)
        bd_rows.store(-1, here, row_of(down_ref, BD1, x, x0) + to_self(ef))
        bd_rows.store(0, here, bd_in[1, :, here] + to_next(ef))
        return 0

    lax.fori_loop(0, chunks(x), zeroth, 0)

    def first(c, _):
        x0 = at_chunk(c)
        here = pl.ds(x0, CHUNK)
        wide = pl.ds(x0, CHUNK + LANES)
        before = row_of(down_ref, SI1, x, x0)
        slot = end_rows(n, x0, g_rows, bg_rows, 1, before, si_ref, sc_ref, known4, not_first, carry, 0)
        slot = end_rows(n, x0, bd_rows, b2d_rows, 1, before, si_ref, sc_ref, known4, not_first, carry, slot)
        slope = si_ref[n, :, here]
        slope_up = row_of(up_ref, SI0, x, x0)
        cross_up = row_of(up_ref, SC0, x, x0)
        diagonal = mask_up[:, here]
        own, inner = beyond(eps_ref, 0, wide, CHUNK, diagonal, cross_up, slope_up, carry, slot, True)
        eps_out[0, :, here] = own + to_next(boundary(g_rows, n - 1, slope, here))
        eps_out[1, :, here] = to_next(inner)
        own, _ = beyond(eps_ref, 1, wide, CHUNK, diagonal, cross_up, slope_up, carry, slot + 1, True)
        eps_out[2, :, here] = own + to_next(boundary(bd_rows, n - 1, slope, here))
        own, _ = beyond(
            eps_ref, 2, wide, CHUNK, mask_down[:, here], row_of(down_ref, SC1, x, x0), row_of(down_ref, SJ1, x, x0),
            carry, slot + 2, False)
        eps_out[3, :, here] = own + to_self(boundary(g_rows, -1, before, here, not_first))
        return 0

    lax.fori_loop(0, chunks(x), first, 0)

    def second(c, _):
        x0 = at_chunk(c)
        here = pl.ds(x0, CHUNK)
        totals = Totals()
        pair = Pairs(b2d_rows.load, x0)
        for i in range(n):
            if not 3 <= i < n - 3:
                values = [g_rows.load(i, here), bg_rows.load(i, here), None, d_ref[i + 1, :, here],
                          bd_rows.load(i, here), b2d_rows.load(i, here)]
                for k, which in enumerate(PAIRS):
                    if which is not None and 2 not in which:
                        totals.add(k, values[which[0]], values[which[1]])
                totals.add(17, values[5], known4(i, x0) * values[5])
                res = pair.cross(i, sc_ref[i, :, here])
                res_out[n + i, :, here] = res
                totals.add(17, res, res)
            if not 3 <= i < n - 4 and i < n - 1:
                res = pair.inline(i, si_ref[i + 1, :, here])
                res_out[i, :, here] = res
                totals.add(17, res, res)
        totals.put(sums)
        return 0

    lax.fori_loop(0, chunks(x), second, 0)


def close_kernel(
    n, x,
    si_ref, sc_ref, mask_ref, bg_in, b2g_in, b2d_in, bg_end, b2d_end, sums_in, eps_ref, res_ref, mask_up, up_first, down_first,
    up_ref, down_ref,
    b2g_out, moments_ref,
    ghosts, carry, sums,
):
    not_first, not_last = place_flags()
    clear_pads(x, (ghosts, b2g_out))
    carry[...] = jnp.zeros(carry.shape, f32)
    sums[...] = sums_in[...]
    bg_rows = Mended(n, 2, bg_in, bg_end, (ghosts, 0), (ghosts, 1))
    b2g_rows = Mended(n, 3, b2g_in, b2g_out, None, (ghosts, 2))
    b2d_rows = Mended(n, 2, b2d_in, b2d_end)

    def known4(i, x0):
        return mask_ref[pl.ds(i, 1), pl.ds(x0, CHUNK)].astype(f32) * 4.0

    def first(c, _):
        x0 = at_chunk(c)
        here = pl.ds(x0, CHUNK)
        bg_rows.store(-1, here, row_of(down_ref, BG1, x, x0) + eps_ref[3, :, here])
        bg_rows.store(n, here, (row_of(up_ref, BG0, x, x0) + eps_ref[0, :, here]) * not_last)
        return 0

    lax.fori_loop(0, chunks(x), first, 0)

    def second(c, _):
        x0 = at_chunk(c)
        here = pl.ds(x0, CHUNK)
        wide = pl.ds(x0, CHUNK + LANES)
        slot = end_rows(n, x0, bg_rows, b2g_rows, 2, row_of(down_first, SI1, x, x0), si_ref, sc_ref, known4, not_first, carry, 0)
        own, _ = beyond(
            eps_ref, 0, wide, CHUNK, mask_up[:, here], row_of(up_first, SC0, x, x0), row_of(up_first, SI0, x, x0),
            carry, slot, True, eps_ref[1, :, here])
        edge = to_next(boundary(bg_rows, n - 1, si_ref[n, :, here], here))
        b2g_rows.store(n, here, (row_of(up_ref, B2G0, x, x0) + own + edge) * not_last)
        return 0

    lax.fori_loop(0, chunks(x), second, 0)

    def third(c, _):
        x0 = at_chunk(c)
        here = pl.ds(x0, CHUNK)
        totals = Totals()
        pair = Pairs(b2g_rows.load, x0)
        for i in range(n):
            if not 3 <= i < n - 3:
                bg, b2g, b2d = (rows.load(i, here) for rows in (bg_rows, b2g_rows, b2d_rows))
                totals.add(3, bg, b2g)
                totals.add(4, b2g, b2g)
                totals.add(10, b2g, b2d)
                weighed = known4(i, x0) * b2g
                totals.add(5, b2g, weighed)
                totals.add(11, b2d, weighed)
                res = pair.cross(i, sc_ref[i, :, here])
                totals.add(5, res, res)
                totals.add(11, res, res_ref[n + i, :, here])
            if not 3 <= i < n - 4:
                slope = si_ref[i + 1, :, here]
                res = pair.inline(i, slope)
                if i < n - 1:
                    other = res_ref[i, :, here]
                else:
                    after = (row_of(up_ref, B2D0, x, x0) + eps_ref[2, :, here]) * not_last
                    other = inline_res(sum_diff(b2d_rows.load(i, here)), sum_diff(after), slope)
                    totals.add(17, other, other)
                totals.add(5, res, res)
                totals.add(11, res, other)
        totals.put(sums)
        return 0

    lax.fori_loop(0, chunks(x), third, 0)
    for k in range(N_MOMENTS):
        moments_ref[pl.ds(k, 1), :] = jnp.sum(sums[k], axis=0, keepdims=True)
    moments_ref[pl.ds(N_MOMENTS, 24 - N_MOMENTS), :] = jnp.zeros((24 - N_MOMENTS, LANES), f32)


def add_terms(terms):
    total = None
    for term in terms:
        total = term if total is None else total + term
    return total


def solve(moments):
    mu, nu, xi = moments[:6], moments[6:12], moments[12:]

    def entry(a, b, i, j):
        if a == 0 and b == 0:
            return mu[i + j]
        if a == 1 and b == 1:
            return xi[i + j]
        return nu[i + j]

    shifted = {}

    def entry_a(a, b, i, j):
        which = a + b
        if (which, i + j) not in shifted:
            if i + j == 4:
                value = entry(a, b, 2, 3)
            else:
                value = entry(a, b, i, j + 1) + SHIFT * entry(a, b, i, j)
            shifted[which, i + j] = value * 0.25
        return shifted[which, i + j]

    def form(get, u, v):
        rows = []
        for (a, i), left in u.items():
            inner = add_terms(right * get(a, b, i, j) for (b, j), right in v.items())
            rows.append(left * inner)
        return add_terms(rows)

    def axpy(scale, u, v):
        out = dict(v)
        for key, value in u.items():
            term = scale * value
            out[key] = out[key] + term if key in out else term
        return out

    one = jnp.ones_like(mu[0])
    gradient = {(0, 0): 0.25 * one}
    direction = {(1, 0): one}
    model = {}
    for iteration in range(ITERS):
        mixing = -form(entry_a, gradient, direction) / form(entry_a, direction, direction)
        direction = axpy(mixing, direction, gradient)
        step = form(entry, gradient, direction) / form(entry_a, direction, direction)
        model = axpy(step, direction, model)
        if iteration < ITERS - 1:
            image = {key: value * (0.25 * SHIFT) for key, value in direction.items()}
            image = axpy(0.25, {(a, i + 1): value for (a, i), value in direction.items()}, image)
            gradient = axpy(-step, image, gradient)
    return model, direction


def last_kernel(
    n, x, moments_ref, m_ref, d_ref, g_in, bg_in, b2g_in, bd_in, b2d_in, g_end, bg_end, b2g_end, bd_end, b2d_end,
    model_hbm, dir_hbm, mo_ref, do_ref, sems,
):
    moments = [
        jnp.broadcast_to(jnp.sum(moments_ref[pl.ds(k, 1), :], axis=1, keepdims=True), (NT, LANES))
        for k in range(N_MOMENTS)
    ]
    model, direction = solve(moments)
    rows = [
        Mended(n, depth, whole, ends)
        for depth, whole, ends in ((1, g_in, g_end), (2, bg_in, bg_end), (3, b2g_in, b2g_end), (1, bd_in, bd_end), (2, b2d_in, b2d_end))
    ]
    keys = ((0, 0), (0, 1), (0, 2), (1, 1), (1, 2))
    copies = []
    for i in range(n):
        def step(c, _):
            x0 = pl.multiple_of(c * LANES, LANES)
            here = pl.ds(x0, LANES)
            values = {key: vector.load(i, here) for key, vector in zip(keys, rows)}
            values[1, 0] = d_ref[i + 1, :, here]
            mo_ref[i, :, here] = m_ref[i + 1, :, here] + add_terms(
                model[key] * value for key, value in values.items())
            do_ref[i, :, here] = add_terms(direction[key] * value for key, value in values.items())
            return 0

        lax.fori_loop(0, x // LANES, step, 0, unroll=4)
        for k, (src, dst) in enumerate(((mo_ref, model_hbm), (do_ref, dir_hbm))):
            copy = pltpu.make_async_copy(src.at[i], dst.at[i], sems.at[2 * i + k])
            copy.start()
            copies.append(copy)
    for copy in copies:
        copy.wait()


def in_vmem(values):
    return [pltpu.with_memory_space_constraint(v, pltpu.VMEM) for v in values]


def kept(shape, dtype=f32):
    return pltpu.VMEM(shape, dtype)


def on_device(*args):
    n, _, x = args[0].shape
    peers = lax.axis_size("inline")
    vmem = pl.BlockSpec(memory_space=pltpu.VMEM)
    hbm = pl.BlockSpec(memory_space=pl.ANY)
    params = pltpu.CompilerParams(vmem_limit_bytes=VMEM_LIMIT)
    wide = kept((n + 2, NT, x + LANES))
    share = x // NT

    args = [pltpu.with_memory_space_constraint(v, pltpu.HBM) for v in args]
    def exchange(up, down):
        return (
            lax.ppermute(up, "inline", [(i, i - 1) for i in range(1, peers)]),
            lax.ppermute(down, "inline", [(i, i + 1) for i in range(peers - 1)]),
        )

    *loaded, up, down = pl.pallas_call(
        functools.partial(first_kernel, n, x),
        out_shape=[
            kept((n, NT, x)), kept((n, x), jnp.int32), kept((n + 2, NT, x)), kept((n, NT, x)), wide, wide,
            kept((NT, FIRST0 * x + share)), kept((NT, FIRST1 * x + share)),
        ],
        in_specs=[hbm] * 6,
        out_specs=[vmem] * 8,
        scratch_shapes=[pltpu.VMEM((4, 2, NT, LANES), f32), pltpu.SemaphoreType.DMA((6,))],
        compiler_params=params,
        name="first",
    )(*args)
    loaded = in_vmem(loaded)
    _, mask, si, sc, m, d = loaded
    first = exchange(up, down)

    late = exchange(*pl.pallas_call(
        functools.partial(edge_kernel, n, x),
        out_shape=[kept((NT, LATE0 * x)), kept((NT, LATE1 * x))],
        in_specs=[vmem] * 8,
        out_specs=[vmem] * 2,
        scratch_shapes=[pltpu.VMEM((n + 2, NT, x + LANES), f32)] * 3 + [pltpu.VMEM((4, 2, NT, LANES), f32)],
        compiler_params=params,
        name="edges",
    )(*loaded, up, down))

    g, bg, b2g, bd, b2d, sums = in_vmem(pl.pallas_call(
        functools.partial(local_kernel, n, x),
        out_shape=[wide, wide, wide, wide, wide, kept((N_MOMENTS, NT, LANES))],
        in_specs=[vmem] * 6,
        out_specs=[vmem] * 6,
        scratch_shapes=[pltpu.VMEM((2 * n, 2, NT, LANES), f32)],
        compiler_params=params,
        name="local",
    )(*loaded))

    def ends(rows):
        return kept((rows, NT, x + LANES))

    out = pl.pallas_call(
        functools.partial(join_kernel, n, x),
        out_shape=[
            ends(2), ends(4), ends(2), ends(4), kept((N_MOMENTS, NT, LANES)), ends(4), kept((2 * n, NT, x)), kept((1, x)),
        ],
        in_specs=[vmem] * 12,
        out_specs=[vmem] * 8,
        scratch_shapes=[
            pltpu.VMEM((3, NT, x + LANES), f32),
            pltpu.VMEM((4, NT, x + LANES), f32),
            pltpu.VMEM((1, x), f32),
            pltpu.VMEM((11, 2, NT, LANES), f32),
        ],
        compiler_params=params,
        name="join",
    )(m, d, si, sc, mask, g, bg, bd, b2d, sums, *first)
    g_end, bg_end, bd_end, b2d_end, sums, eps, res, mask_up = in_vmem(out)

    b2g_end, moments = pl.pallas_call(
        functools.partial(close_kernel, n, x),
        out_shape=[ends(6), jax.ShapeDtypeStruct((24, LANES), f32)],
        in_specs=[vmem] * 16,
        out_specs=[vmem] * 2,
        scratch_shapes=[
            pltpu.VMEM((3, NT, x + LANES), f32),
            pltpu.VMEM((7, 2, NT, LANES), f32),
            pltpu.VMEM((N_MOMENTS, NT, LANES), f32),
        ],
        compiler_params=params,
        name="close",
    )(si, sc, mask, bg, b2g, b2d, bg_end, b2d_end, sums, eps, res, mask_up, *first, *late)

    reach = 1
    while reach < peers:
        moments = moments + lax.ppermute(moments, "inline", [(i, i ^ reach) for i in range(peers)])
        reach *= 2

    return pl.pallas_call(
        functools.partial(last_kernel, n, x),
        out_shape=[jax.ShapeDtypeStruct((n, NT, x), f32)] * 2,
        in_specs=[vmem] * 13,
        out_specs=[hbm] * 2,
        scratch_shapes=[
            pltpu.VMEM((n, NT, x), f32),
            pltpu.VMEM((n, NT, x), f32),
            pltpu.SemaphoreType.DMA((2 * n,)),
        ],
        compiler_params=params,
        name="last",
    )(
        moments, m, d, g, bg, b2g, bd, b2d, g_end, bg_end, *in_vmem([b2g_end]), bd_end, b2d_end)


def solution(mesh):
    rows = P(("groups", "inline"), None, None)
    return jax.shard_map(
        on_device,
        mesh=mesh,
        in_specs=(rows, P(("groups", "inline"), None), rows, rows, rows, rows),
        out_specs=(rows, rows),
        check_vma=False,
    )
```

time: 60.3 us -> 55.9 us (0.927)
  Pallas kernels: 23.9 us -> 21.3 us
  starting transfers between devices: 28.7 us -> 26.8 us
    ppermute x4, starting transfers between devices: 24.1 us -> 15.9 us  [on_device(): lax.ppermute(moments, 'inline', [(i, i ^ reach) for i in range(peers)])]
    ppermute x2 -> x4, starting transfers between devices: 4.57 us -> 10.9 us  [the longest x2 8.34 us: exchange(): lax.ppermute(down, 'inline', [(i, i + 1) for i in range(peers - 1)])]
    pallas_call x1 -> x3, Pallas kernels: 7.33 us -> 10.6 us  [the longest x1 4.28 us: on_device(): pl.pallas_call(functools.partial(join_kernel, n, x), out_shape=[ends(2),...]
    pallas_call x1, Pallas kernels: 5.37 us -> 2.16 us  [on_device(): pl.pallas_call(functools.partial(edge_kernel, n, x), out_shape=[kept((NT,...]
    pallas_call x1, Pallas kernels: 8.84 us -> 6.17 us  [on_device(): pl.pallas_call(functools.partial(local_kernel, n, x), out_shape=[wide, wi...]
  transfers between devices with their start and end apart: 6 -> 8, of which waited for: 4 -> 4; matrix products, arithmetic and copies ran while one was open for 0% -> 0% of each run, Pallas kernels for 15% -> 23%
where the time goes in v3:
time: 55.9 us; the launch traced here: 55.7 us
  starting transfers between devices  26.8 us (48%)
  Pallas kernels  21.3 us (38%)
  waiting for transfers between devices  6.64 us (12%)
  between operations  0.9 us (2%)
    ppermute x4, starting transfers between devices, on_device(): lax.ppermute(moments, 'inline', [(i, i ^ reach) for i in range(peers)])  15.9 us
    ppermute x2, starting transfers between devices, exchange(): lax.ppermute(down, 'inline', [(i, i + 1) for i in range(peers - 1)])  8.34 us
    ppermute x4, waiting for transfers between devices, on_device(): lax.ppermute(moments, 'inline', [(i, i ^ reach) for i in range(peers)])  6.63 us
    pallas_call x1, Pallas kernels, on_device(): pl.pallas_call(functools.partial(local_kernel, n, x), out_shape=[wide, wi...  6.17 us
    pallas_call x1, Pallas kernels, on_device(): pl.pallas_call(functools.partial(join_kernel, n, x), out_shape=[ends(2),...  4.28 us
    pallas_call x1, Pallas kernels, on_device(): pl.pallas_call(functools.partial(first_kernel, n, x), out_shape=[kept((n,...  3.63 us
    pallas_call x1, Pallas kernels, on_device(): pl.pallas_call(functools.partial(close_kernel, n, x), out_shape=[ends(6),...  2.69 us
    ppermute x2, starting transfers between devices, exchange(): lax.ppermute(up, 'inline', [(i, i - 1) for i in range(1, peers)])  2.58 us
  transfers between devices with their start and end apart: 8, of which 4 were waited for; matrix products, arithmetic and copies ran while one was open for 0% of the time, Pallas kernels for 23%

profile of v3, /device:TPU:0, one launch (start us, length us, event | category | flops | bytes accessed | tf_op | source)
XLA Modules:
  0.0 55.7 jit_solution(5470727358352001780)
XLA Ops:
  0.6 3.6 %first.1 = (f32[8,8,4096]{2,1,0:T(8,128)S(1)}, s32[8,4096]{1,0:T(8,128)S(1)}, f32[10,8,4096]{2,1,0:T(8,128)S(1)}, f32[8,8,4096]{2,1,0:T(8,128)S(1)}, f32[10,8,42...) custom-call(f32[8,8,4096]{2,1,0:T(8,128)} %data_hbm.1, ...), custom_call_target="tpu_custom_call" | custom-call | tf_op jit(solution)/shard_map/first/pallas_call | solution.py:729
  4.3 2.4 %collective-permute-start.1 = (f32[8,29184]{1,0:T(8,128)S(1)}, f32[8,29184]{1,0:T(8,128)S(1)}, u32[]{:S(2)}, u32[]{:S(2)}) collective-permute-start(f32[8,29184]{1,0:T(8,128)S(1)} %get-tuple-element.41.down_first), channel_id=1, source_target_pairs={{0,1},{1,2},{2,3},{3,4},{4,5},{5,6},{6,7},{7,8},{8,9},{9,10},{10,1... | collective-permute-start | bytes 2801672 | tf_op jit(solution)/shard_map/ppermute | solution.py:726
  6.7 1.3 %collective-permute-start = (f32[8,25088]{1,0:T(8,128)S(1)}, f32[8,25088]{1,0:T(8,128)S(1)}, u32[]{:S(2)}, u32[]{:S(2)}) collective-permute-start(f32[8,25088]{1,0:T(8,128)S(1)} %get-tuple-element.40.up_first), channel_id=1, source_target_pairs={{1,0},{2,1},{3,2},{4,3},{5,4},{6,5},{7,6},{8,7},{9,8},{10,9},{11,1... | collective-permute-start | bytes 2408456 | tf_op jit(solution)/shard_map/ppermute | solution.py:725
  8.0 2.2 %edges.1 = (f32[8,12288]{1,0:T(8,128)S(1)}, f32[8,4096]{1,0:T(8,128)S(1)}) custom-call(f32[8,8,4096]{2,1,0:T(8,128)S(1)} %get-tuple-element.31.data_ref, s32[8,4096]{1,0:T(8,128)S(1)} %get-tuple-element.30.mask_ref, f32[10,8,4096]{2,1,0:T(8,128)S(1)} %get-tuple-element.28.si_ref, f32[8,8,4096]{2,1,0:T(8,128)S(1)} %get-tuple-element.29.sc_ref, ...), custom_call_target="tpu_custom_call" | custom-call | tf_op jit(solution)/shard_map/edges/pallas_call | solution.py:745
  10.2 1.3 %collective-permute-start.2 = (f32[8,12288]{1,0:T(8,128)S(1)}, f32[8,12288]{1,0:T(8,128)S(1)}, u32[]{:S(2)}, u32[]{:S(2)}) collective-permute-start(f32[8,12288]{1,0:T(8,128)S(1)} %get-tuple-element.48), channel_id=1, source_target_pairs={{1,0},{2,1},{3,2},{4,3},{5,4},{6,5},{7,6},{8,7},{9,8},{10,9},{11,1... | collective-permute-start | bytes 1179656 | tf_op jit(solution)/shard_map/ppermute | solution.py:725
  11.5 5.9 %collective-permute-start.3 = (f32[8,4096]{1,0:T(8,128)S(1)}, f32[8,4096]{1,0:T(8,128)S(1)}, u32[]{:S(2)}, u32[]{:S(2)}) collective-permute-start(f32[8,4096]{1,0:T(8,128)S(1)} %get-tuple-element.49), channel_id=1, source_target_pairs={{0,1},{1,2},{2,3},{3,4},{4,5},{5,6},{6,7},{7,8},{8,9},{9,10},{10,1... | collective-permute-start | bytes 393224 | tf_op jit(solution)/shard_map/ppermute | solution.py:726
  17.4 6.2 %local.1 = (f32[10,8,4224]{2,1,0:T(8,128)S(1)}, f32[10,8,4224]{2,1,0:T(8,128)S(1)}, f32[10,8,4224]{2,1,0:T(8,128)S(1)}, f32[10,8,4224]{2,1,0:T(8,128)S(1)}, f32[...) custom-call(f32[8,8,4096]{2,1,0:T(8,128)S(1)} %get-tuple-element.31.data_ref, ...), custom_call_target="tpu_custom_call" | custom-call | tf_op jit(solution)/shard_map/local/pallas_call | solution.py:755
  23.6 0.0 collective-permute-done.up_ref.up_first
  23.6 0.0 collective-permute-done.1.down_ref.down_first
  23.6 4.3 %join.1 = (f32[2,8,4224]{2,1,0:T(8,128)S(1)}, f32[4,8,4224]{2,1,0:T(8,128)S(1)}, f32[2,8,4224]{2,1,0:T(8,128)S(1)}, f32[4,8,4224]{2,1,0:T(8,128)S(1)}, f32[18,8,...) custom-call(f32[10,8,4224]{2,1,0:T(8,128)S(1)} %get-tuple-element.32.m_ref, ...), custom_call_target="tpu_custom_call" | custom-call | tf_op jit(solution)/shard_map/join/pallas_call | solution.py:768
  27.9 0.0 collective-permute-done.3.down_ref
  27.9 0.0 collective-permute-done.2.up_ref
  27.9 2.7 %close.1 = (f32[6,8,4224]{2,1,0:T(8,128)S(1)}, f32[24,128]{1,0:T(8,128)S(1)}) custom-call(f32[10,8,4096]{2,1,0:T(8,128)S(1)} %get-tuple-element.28.si_ref, f32[8,8,4096]{2,1,0:T(8,128)S(1)} %get-tuple-element.29.sc_ref, s32[8,4096]{1,0:T(8,128)S(1)} %get-tuple-element.30.mask_ref, f32[10,8,4224]{2,1,0:T(8,128)S(1)} %get-tuple-element.34.bg_in, ...), custom_call_target="tpu_custom_call" | custom-call | tf_op jit(solution)/shard_map/close/pallas_call | solution.py:786
  30.6 9.0 %collective-permute-start.4 = (f32[24,128]{1,0:T(8,128)S(1)}, f32[24,128]{1,0:T(8,128)S(1)}, u32[]{:S(2)}, u32[]{:S(2)}) collective-permute-start(f32[24,128]{1,0:T(8,128)S(1)} %get-tuple-element.50), channel_id=1, source_target_pairs={{0,1},{1,0},{2,3},{3,2},{4,5},{5,4},{6,7},{7,6},{8,9},{9,8},{10,11... | collective-permute-start | bytes 36872 | tf_op jit(solution)/shard_map/ppermute | solution.py:802
  39.6 0.8 %collective-permute-done.4 = f32[24,128]{1,0:T(8,128)S(1)} collective-permute-done((f32[24,128]{1,0:T(8,128)S(1)}, f32[24,128]{1,0:T(8,128)S(1)}, u32[]{:S(2)}, u32[]{:S(2)}) %collective-permute-start.4) | collective-permute-done | bytes 12320 | tf_op jit(solution)/shard_map/ppermute | solution.py:802
  40.5 2.7 %collective-permute-start.5 = (f32[24,128]{1,0:T(8,128)S(1)}, f32[24,128]{1,0:T(8,128)S(1)}, u32[]{:S(2)}, u32[]{:S(2)}) collective-permute-start(f32[24,128]{1,0:T(8,128)S(1)} %add.12), channel_id=1, source_target_pairs={{0,2},{1,3},{2,0},{3,1},{4,6},{5,7},{6,4},{7,5},{8,10},{9,11},{10,... | collective-permute-start | bytes 36872 | tf_op jit(solution)/shard_map/ppermute | solution.py:802
  43.2 1.7 %collective-permute-done.5 = f32[24,128]{1,0:T(8,128)S(1)} collective-permute-done((f32[24,128]{1,0:T(8,128)S(1)}, f32[24,128]{1,0:T(8,128)S(1)}, u32[]{:S(2)}, u32[]{:S(2)}) %collective-permute-start.5) | collective-permute-done | bytes 12320 | tf_op jit(solution)/shard_map/ppermute | solution.py:802
  44.9 1.6 %collective-permute-start.6 = (f32[24,128]{1,0:T(8,128)S(1)}, f32[24,128]{1,0:T(8,128)S(1)}, u32[]{:S(2)}, u32[]{:S(2)}) collective-permute-start(f32[24,128]{1,0:T(8,128)S(1)} %add.13), channel_id=1, source_target_pairs={{0,4},{1,5},{2,6},{3,7},{4,0},{5,1},{6,2},{7,3},{8,12},{9,13},{10,... | collective-permute-start | bytes 36872 | tf_op jit(solution)/shard_map/ppermute | solution.py:802
  46.4 2.1 %collective-permute-done.6 = f32[24,128]{1,0:T(8,128)S(1)} collective-permute-done((f32[24,128]{1,0:T(8,128)S(1)}, f32[24,128]{1,0:T(8,128)S(1)}, u32[]{:S(2)}, u32[]{:S(2)}) %collective-permute-start.6) | collective-permute-done | bytes 12320 | tf_op jit(solution)/shard_map/ppermute | solution.py:802
  48.6 2.6 %collective-permute-start.7 = (f32[24,128]{1,0:T(8,128)S(1)}, f32[24,128]{1,0:T(8,128)S(1)}, u32[]{:S(2)}, u32[]{:S(2)}) collective-permute-start(f32[24,128]{1,0:T(8,128)S(1)} %add.14), channel_id=1, source_target_pairs={{0,8},{1,9},{2,10},{3,11},{4,12},{5,13},{6,14},{7,15},{8,0},{9,1},... | collective-permute-start | bytes 36872 | tf_op jit(solution)/shard_map/ppermute | solution.py:802
  51.2 2.0 %collective-permute-done.7 = f32[24,128]{1,0:T(8,128)S(1)} collective-permute-done((f32[24,128]{1,0:T(8,128)S(1)}, f32[24,128]{1,0:T(8,128)S(1)}, u32[]{:S(2)}, u32[]{:S(2)}) %collective-permute-start.7) | collective-permute-done | bytes 12320 | tf_op jit(solution)/shard_map/ppermute | solution.py:802
  53.2 2.3 %last.1 = (f32[8,8,4096]{2,1,0:T(8,128)}, f32[8,8,4096]{2,1,0:T(8,128)}) custom-call(f32[24,128]{1,0:T(8,128)S(1)} %add.15.moments_ref, f32[10,8,4224]{2,1,0:T(8,128)S(1)} %get-tuple-element.32.m_ref, f32[10,8,4224]{2,1,0:T(8,128)S(1)} %get-tuple-element.33.d_ref, f32[10,8,4224]{2,1,0:T(8,128)S(1)} %get-tuple-element.37.g_in, ...), custom_call_target="tpu_custom_call" | custom-call | tf_op jit(solution)/shard_map/last/pallas_call | solution.py:805
  (4 shorter events, 0.0 us)
Async XLA Ops:
  4.3 19.3 %collective-permute-start.1 = (f32[8,29184]{1,0:T(8,128)S(1)}, f32[8,29184]{1,0:T(8,128)S(1)}, u32[]{:S(2)}, u32[]{:S(2)}) collective-permute-start(f32[8,29184]{1,0:T(8,128)S(1)} %get-tuple-element.41.down_first), channel_id=1, source_target_pairs={{0,1},{1,2},{2,3},{3,4},{4,5},{5,6},{6,7},{7,8},{8,9},{9,10},{10,1... | collective-permute-start | bytes 2801672 | tf_op jit(solution)/shard_map/ppermute | solution.py:726
  6.7 16.9 %collective-permute-start = (f32[8,25088]{1,0:T(8,128)S(1)}, f32[8,25088]{1,0:T(8,128)S(1)}, u32[]{:S(2)}, u32[]{:S(2)}) collective-permute-start(f32[8,25088]{1,0:T(8,128)S(1)} %get-tuple-element.40.up_first), channel_id=1, source_target_pairs={{1,0},{2,1},{3,2},{4,3},{5,4},{6,5},{7,6},{8,7},{9,8},{10,9},{11,1... | collective-permute-start | bytes 2408456 | tf_op jit(solution)/shard_map/ppermute | solution.py:725
  10.2 17.7 %collective-permute-start.2 = (f32[8,12288]{1,0:T(8,128)S(1)}, f32[8,12288]{1,0:T(8,128)S(1)}, u32[]{:S(2)}, u32[]{:S(2)}) collective-permute-start(f32[8,12288]{1,0:T(8,128)S(1)} %get-tuple-element.48), channel_id=1, source_target_pairs={{1,0},{2,1},{3,2},{4,3},{5,4},{6,5},{7,6},{8,7},{9,8},{10,9},{11,1... | collective-permute-start | bytes 1179656 | tf_op jit(solution)/shard_map/ppermute | solution.py:725
  11.5 16.4 %collective-permute-start.3 = (f32[8,4096]{1,0:T(8,128)S(1)}, f32[8,4096]{1,0:T(8,128)S(1)}, u32[]{:S(2)}, u32[]{:S(2)}) collective-permute-start(f32[8,4096]{1,0:T(8,128)S(1)} %get-tuple-element.49), channel_id=1, source_target_pairs={{0,1},{1,2},{2,3},{3,4},{4,5},{5,6},{6,7},{7,8},{8,9},{9,10},{10,1... | collective-permute-start | bytes 393224 | tf_op jit(solution)/shard_map/ppermute | solution.py:726
  30.6 9.9 %collective-permute-start.4 = (f32[24,128]{1,0:T(8,128)S(1)}, f32[24,128]{1,0:T(8,128)S(1)}, u32[]{:S(2)}, u32[]{:S(2)}) collective-permute-start(f32[24,128]{1,0:T(8,128)S(1)} %get-tuple-element.50), channel_id=1, source_target_pairs={{0,1},{1,0},{2,3},{3,2},{4,5},{5,4},{6,7},{7,6},{8,9},{9,8},{10,11... | collective-permute-start | bytes 36872 | tf_op jit(solution)/shard_map/ppermute | solution.py:802
  40.5 4.4 %collective-permute-start.5 = (f32[24,128]{1,0:T(8,128)S(1)}, f32[24,128]{1,0:T(8,128)S(1)}, u32[]{:S(2)}, u32[]{:S(2)}) collective-permute-start(f32[24,128]{1,0:T(8,128)S(1)} %add.12), channel_id=1, source_target_pairs={{0,2},{1,3},{2,0},{3,1},{4,6},{5,7},{6,4},{7,5},{8,10},{9,11},{10,... | collective-permute-start | bytes 36872 | tf_op jit(solution)/shard_map/ppermute | solution.py:802
  44.9 3.7 %collective-permute-start.6 = (f32[24,128]{1,0:T(8,128)S(1)}, f32[24,128]{1,0:T(8,128)S(1)}, u32[]{:S(2)}, u32[]{:S(2)}) collective-permute-start(f32[24,128]{1,0:T(8,128)S(1)} %add.13), channel_id=1, source_target_pairs={{0,4},{1,5},{2,6},{3,7},{4,0},{5,1},{6,2},{7,3},{8,12},{9,13},{10,... | collective-permute-start | bytes 36872 | tf_op jit(solution)/shard_map/ppermute | solution.py:802
  48.6 4.6 %collective-permute-start.7 = (f32[24,128]{1,0:T(8,128)S(1)}, f32[24,128]{1,0:T(8,128)S(1)}, u32[]{:S(2)}, u32[]{:S(2)}) collective-permute-start(f32[24,128]{1,0:T(8,128)S(1)} %add.14), channel_id=1, source_target_pairs={{0,8},{1,9},{2,10},{3,11},{4,12},{5,13},{6,14},{7,15},{8,0},{9,1},... | collective-permute-start | bytes 36872 | tf_op jit(solution)/shard_map/ppermute | solution.py:802

commit v4 on v3

v4 whole, which is shorter than its diff:
```python
import functools

import jax
import jax.numpy as jnp
from jax import lax
from jax.experimental import pallas as pl
from jax.experimental.pallas import tpu as pltpu
from jax.sharding import PartitionSpec as P

ITERS = 3
NT = 8
LANES = 128
CHUNK = 4096
SHIFT = 18.0
M0, D0, SI0, FIRST0 = range(4)
SC0, G0, BD0, BG0, B2D0, B2G0, LATE0 = range(7)
WM1, WD1, SI1, G1, BD1, BG1, DOWN1 = range(7)
N_MOMENTS = 18
VMEM_LIMIT = 16 * 1024 * 1024

f32 = jnp.float32


def time_ahead(v):
    rolled = pltpu.roll(v, NT - 1, 0)
    return jnp.where(lax.broadcasted_iota(jnp.int32, v.shape, 0) == NT - 1, 0.0, rolled)


def time_behind(v):
    rolled = pltpu.roll(v, 1, 0)
    return jnp.where(lax.broadcasted_iota(jnp.int32, v.shape, 0) == 0, 0.0, rolled)


def sum_diff(v):
    ahead = time_ahead(v)
    return ahead + v, ahead - v


def head(pair, width):
    return pair[0][:, :width], pair[1][:, :width]


def inline_res(here, after, slope):
    return (after[0] - here[0]) + slope * (after[1] + here[1])


def parts(res, slope):
    scaled = slope * res
    return res - scaled, res + scaled


def to_next(ef):
    return ef[0] + time_behind(ef[1])


def to_self(ef):
    return -(ef[1] + time_behind(ef[0]))


def lane_ahead(v):
    width = v.shape[1]
    return pltpu.roll(v, width - 1, 1)[:, : width - LANES]


def lane_behind(before, v):
    joined = jnp.concatenate([before, v], axis=1)
    return pltpu.roll(joined, 1, 1)[:, LANES:]


def cross_res(sd, slope):
    width = sd[0].shape[1] - LANES
    here = head(sd, width)
    return (lane_ahead(sd[0]) - here[0]) + slope * (lane_ahead(sd[1]) + here[1])


def cross_terms(sd, slope, carry, slot):
    e, f = parts(cross_res(sd, slope), slope)
    e_behind = lane_behind(carry[slot, 0], e)
    f_behind = lane_behind(carry[slot, 1], f)
    carry[slot, 0] = e[:, -LANES:]
    carry[slot, 1] = f[:, -LANES:]
    return e_behind - f, f_behind - e


def stencil(load, slope_in, slope_cr, lo, hi, res_lo, res_hi, carry, slot, scale_lo=None):
    out = {}
    sd = {}

    def pair(i):
        if i not in sd:
            sd[i] = sum_diff(load(i))
        return sd[i]

    before = None
    for i in range(lo - 1, hi + 1):
        here = None
        if res_lo <= i <= res_hi:
            first = pair(i)
            second = pair(i + 1)
            width = first[0].shape[1] - LANES
            slope = slope_in(i)
            res = inline_res(head(first, width), head(second, width), slope)
            if i == -1 and scale_lo is not None:
                res = res * scale_lo
            here = parts(res, slope)
        if i >= lo:
            same, later = cross_terms(pair(i), slope_cr(i), carry, slot + i - lo)
            if before is not None:
                same = same + before[0]
                later = later + before[1]
            if here is not None:
                same = same - here[1]
                later = later - here[0]
            out[i] = same + time_behind(later)
        before = here
    return out


class Mended:
    def __init__(self, n, low, high, whole, ends, before=None, after=None):
        self.n, self.low, self.high, self.whole, self.ends, self.before, self.after = n, low, high, whole, ends, before, after

    def at(self, i):
        if i < 0:
            return self.before
        if i >= self.n:
            return self.after
        if i < self.low:
            return self.ends, i
        if i >= self.n - self.high:
            return self.ends, self.low + i - self.n + self.high
        return self.whole, i + 1

    def load(self, i, lanes):
        ref, row = self.at(i)
        return ref[row, :, lanes]

    def store(self, i, lanes, value):
        ref, row = self.at(i)
        ref[row, :, lanes] = value


def chunks(x):
    return x // CHUNK


def at_chunk(c):
    return pl.multiple_of(c * CHUNK, CHUNK)


class Own:
    def __init__(self, n, x0, si_ref, sc_ref, mask_ref, carry):
        self.n, self.x0, self.here = n, x0, pl.ds(x0, CHUNK)
        self.si_ref, self.sc_ref, self.mask_ref, self.carry = si_ref, sc_ref, mask_ref, carry

    def known4(self, i):
        return self.mask_ref[pl.ds(i, 1), self.here].astype(f32) * 4.0

    def level(self, src, lo, hi, slot):
        return stencil(
            lambda i: src[i + 1, :, pl.ds(self.x0, CHUNK + LANES)],
            lambda i: self.si_ref[i + 1, :, self.here],
            lambda i: self.sc_ref[i, :, self.here],
            lo, hi, 0, self.n - 2, self.carry, slot,
        )

    def applied(self, src, lo, hi, slot):
        out = self.level(src, lo, hi, slot)
        return {i: (self.known4(i) - SHIFT) * src[i + 1, :, self.here] + out[i] for i in out}

    def gradient(self, data_ref, m_ref, lo, hi, slot):
        out = self.level(m_ref, lo, hi, slot)
        return {i: self.known4(i) * (data_ref[i, :, self.here] - m_ref[i + 1, :, self.here]) - out[i] for i in out}


def put(ref, slot, x, x0, value):
    ref[:, pl.ds(pl.multiple_of(x0 + slot * x, CHUNK), CHUNK)] = value


def pack_kernel(n, x, si_hbm, model_hbm, dir_hbm, up_ref, sems):
    copies = [
        pltpu.make_async_copy(source.at[0], up_ref.at[:, pl.ds(slot * x, x)], sems.at[slot])
        for source, slot in ((model_hbm, M0), (dir_hbm, D0), (si_hbm, SI0))
    ]
    for copy in copies:
        copy.start()
    for copy in copies:
        copy.wait()


def first_kernel(
    n, x,
    data_hbm, mask_hbm, si_hbm, sc_hbm, model_hbm, dir_hbm,
    data_ref, mask_ref, si_ref, sc_ref, m_ref, d_ref, up_ref,
    g_ref, bg_ref, bd_ref, carry, sems,
):
    body = (pl.ds(1, n), slice(None), pl.ds(0, x))
    copies = [
        pltpu.make_async_copy(source, target, sems.at[k])
        for k, (source, target) in enumerate((
            (model_hbm, m_ref.at[body]), (dir_hbm, d_ref.at[body]), (si_hbm, si_ref.at[pl.ds(1, n)]), (sc_hbm, sc_ref),
            (mask_hbm, mask_ref), (data_hbm, data_ref),
        ))
    ]
    for copy in copies:
        copy.start()
    clear_pads(x, (m_ref, d_ref, g_ref, bg_ref, bd_ref))
    carry[...] = jnp.zeros(carry.shape, f32)
    for copy in copies:
        copy.wait()
    share = x // NT
    for s in range(NT):
        up_ref[pl.ds(s, 1), pl.ds(LATE0 * x, share)] = mask_ref[pl.ds(0, 1), pl.ds(s * share, share)].astype(f32)

    def first(c, _):
        x0 = at_chunk(c)
        own = Own(n, x0, si_ref, sc_ref, mask_ref, carry)
        put(up_ref, SC0, x, x0, sc_ref[0, :, own.here])
        out = own.gradient(data_ref, m_ref, 0, 2, 0)
        put(up_ref, G0, x, x0, out[0])
        for i, value in out.items():
            g_ref[i + 1, :, own.here] = value
        out = own.applied(d_ref, 0, 1, 3)
        put(up_ref, BD0, x, x0, out[0])
        for i, value in out.items():
            bd_ref[i + 1, :, own.here] = value
        return 0

    lax.fori_loop(0, chunks(x), first, 0)
    carry[...] = jnp.zeros(carry.shape, f32)

    def second(c, _):
        x0 = at_chunk(c)
        own = Own(n, x0, si_ref, sc_ref, mask_ref, carry)
        out = own.applied(g_ref, 0, 1, 0)
        put(up_ref, BG0, x, x0, out[0])
        for i, value in out.items():
            bg_ref[i + 1, :, own.here] = value
        put(up_ref, B2D0, x, x0, own.applied(bd_ref, 0, 0, 2)[0])
        return 0

    lax.fori_loop(0, chunks(x), second, 0)
    carry[...] = jnp.zeros(carry.shape, f32)

    def third(c, _):
        x0 = at_chunk(c)
        put(up_ref, B2G0, x, x0, Own(n, x0, si_ref, sc_ref, mask_ref, carry).applied(bg_ref, 0, 0, 0)[0])
        return 0

    lax.fori_loop(0, chunks(x), third, 0)


def down_kernel(
    n, x, data_ref, mask_ref, si_ref, sc_ref, m_ref, d_ref, up_first,
    down_ref, eps_ref,
    g_ref, carry,
):
    clear_pads(x, (g_ref, eps_ref))
    carry[...] = jnp.zeros(carry.shape, f32)

    def first(c, _):
        x0 = at_chunk(c)
        here = pl.ds(x0, CHUNK)
        own = Own(n, x0, si_ref, sc_ref, mask_ref, carry)
        slope = si_ref[n, :, here]
        out = own.gradient(data_ref, m_ref, n - 2, n - 1, 0)
        ef = parts(inline_res(sum_diff(m_ref[n, :, here]), sum_diff(row_of(up_first, M0, x, x0)), slope), slope)
        g_ref[n - 1, :, here] = out[n - 2]
        g_ref[n, :, here] = out[n - 1] - to_self(ef)
        put(down_ref, G1, x, x0, g_ref[n, :, here])
        eps_ref[0, :, here] = -to_next(ef)
        put(down_ref, WM1, x, x0, eps_ref[0, :, here])
        ef = parts(inline_res(sum_diff(d_ref[n, :, here]), sum_diff(row_of(up_first, D0, x, x0)), slope), slope)
        put(down_ref, BD1, x, x0, own.applied(d_ref, n - 1, n - 1, 2)[n - 1] + to_self(ef))
        eps_ref[1, :, here] = to_next(ef)
        put(down_ref, WD1, x, x0, eps_ref[1, :, here])
        put(down_ref, SI1, x, x0, slope)
        return 0

    lax.fori_loop(0, chunks(x), first, 0)
    carry[...] = jnp.zeros(carry.shape, f32)

    def second(c, _):
        x0 = at_chunk(c)
        own = Own(n, x0, si_ref, sc_ref, mask_ref, carry)
        put(down_ref, BG1, x, x0, own.applied(g_ref, n - 1, n - 1, 0)[n - 1])
        return 0

    lax.fori_loop(0, chunks(x), second, 0)


def local_kernel(
    n, x, data_ref, mask_ref, si_ref, sc_ref, m_ref, d_ref, down_ref,
    g_ref, bg_ref, b2g_ref, bd_ref, b2d_ref, sums_ref, carry,
):
    clear_pads(x, (g_ref, bg_ref, b2g_ref, bd_ref, b2d_ref))
    carry[...] = jnp.zeros(carry.shape, f32)
    sums_ref[...] = jnp.zeros(sums_ref.shape, f32)

    def first(c, _):
        x0 = at_chunk(c)
        here = pl.ds(x0, CHUNK)
        own = Own(n, x0, si_ref, sc_ref, mask_ref, carry)
        for i, value in own.gradient(data_ref, m_ref, 0, n - 2, 0).items():
            g_ref[i + 1, :, here] = value
        for i, value in own.applied(d_ref, 0, n - 2, n).items():
            bd_ref[i + 1, :, here] = value
        g_ref[n, :, here] = row_of(down_ref, G1, x, x0)
        bd_ref[n, :, here] = row_of(down_ref, BD1, x, x0)
        return 0

    lax.fori_loop(0, chunks(x), first, 0)
    carry[...] = jnp.zeros(carry.shape, f32)

    def second(c, _):
        x0 = at_chunk(c)
        own = Own(n, x0, si_ref, sc_ref, mask_ref, carry)
        for i, value in own.applied(g_ref, 2, n - 2, 0).items():
            bg_ref[i + 1, :, own.here] = value
        for i, value in own.applied(bd_ref, 2, n - 2, n).items():
            b2d_ref[i + 1, :, own.here] = value
        return 0

    lax.fori_loop(0, chunks(x), second, 0)
    carry[...] = jnp.zeros(carry.shape, f32)

    def third(c, _):
        x0 = at_chunk(c)
        own = Own(n, x0, si_ref, sc_ref, mask_ref, carry)
        for i, value in own.applied(bg_ref, 3, n - 3, 0).items():
            b2g_ref[i + 1, :, own.here] = value
        return 0

    lax.fori_loop(0, chunks(x), third, 0)

    def fourth(c, _):
        x0 = at_chunk(c)
        loads = [lambda i, lanes, ref=ref: ref[i + 1, :, lanes] for ref in (g_ref, bg_ref, b2g_ref, d_ref, bd_ref, b2d_ref)]
        products(n, x0, loads, mask_ref, si_ref, sc_ref, sums_ref, lambda done: done)
        return 0

    lax.fori_loop(0, chunks(x), fourth, 0)


PAIRS = ((0, 0), (0, 1), (1, 1), (1, 2), (2, 2), None, (0, 3), (0, 4), (1, 4), (1, 5), (2, 5), None,
         (3, 3), (3, 4), (4, 4), (4, 5), (5, 5), None)


class Totals:
    def __init__(self):
        self.of = {}

    def add(self, k, left, right):
        product = left * right
        acc = product[:, :LANES]
        for j in range(1, CHUNK // LANES):
            acc = acc + product[:, j * LANES:(j + 1) * LANES]
        self.of[k] = self.of[k] + acc if k in self.of else acc

    def put(self, sums):
        for k, value in self.of.items():
            sums[k] = sums[k] + value


class Pairs:
    def __init__(self, load, x0):
        self.load, self.lanes, self.of = load, pl.ds(x0, CHUNK + LANES), {}

    def at(self, i):
        if i not in self.of:
            self.of[i] = sum_diff(self.load(i, self.lanes))
        return self.of[i]

    def inline(self, i, slope):
        return inline_res(head(self.at(i), CHUNK), head(self.at(i + 1), CHUNK), slope)

    def cross(self, i, slope):
        return cross_res(self.at(i), slope)


LOW = (1, 2, 3, 0, 1, 2)
HIGH = (0, 1, 2, 0, 0, 1)


def products(n, x0, loads, mask_ref, si_ref, sc_ref, sums, take):
    here = pl.ds(x0, CHUNK)
    totals = Totals()
    pair_g, pair_d = Pairs(loads[2], x0), Pairs(loads[5], x0)

    def turn(i, *vectors):
        return take(all(LOW[v] <= i < n - HIGH[v] for v in vectors))

    for i in range(n):
        values = {}

        def row(v):
            if v not in values:
                values[v] = loads[v](i, here)
            return values[v]

        for k, which in enumerate(PAIRS):
            if which is not None and turn(i, *which):
                totals.add(k, row(which[0]), row(which[1]))
        res = {}
        for k, left, right in ((5, 2, 2), (11, 2, 5), (17, 5, 5)):
            if turn(i, left, right):
                known = mask_ref[pl.ds(i, 1), here].astype(f32) * 4.0
                totals.add(k, known * row(left), row(right))
                for v, pair in ((left, pair_g if left == 2 else pair_d), (right, pair_d if right == 5 else pair_g)):
                    if ("cross", v) not in res:
                        res["cross", v] = pair.cross(i, sc_ref[i, :, here])
                totals.add(k, res["cross", left], res["cross", right])
            if take(all(LOW[v] <= i < n - 1 - HIGH[v] for v in (left, right))):
                for v, pair in ((left, pair_g if left == 2 else pair_d), (right, pair_d if right == 5 else pair_g)):
                    if ("inline", v) not in res:
                        res["inline", v] = pair.inline(i, si_ref[i + 1, :, here])
                totals.add(k, res["inline", left], res["inline", right])
    totals.put(sums)


def place_flags():
    place = lax.axis_index("inline")
    return (place > 0).astype(f32), (place < lax.axis_size("inline") - 1).astype(f32)


def row_of(ref, slot, x, x0):
    return ref[:, pl.ds(pl.multiple_of(x0 + slot * x, CHUNK), CHUNK)]


def boundary(rows, i, slope, here, scale=None):
    res = inline_res(sum_diff(rows.load(i, here)), sum_diff(rows.load(i + 1, here)), slope)
    if scale is not None:
        res = res * scale
    return parts(res, slope)


def clear_pads(x, refs):
    for ref in refs:
        for i in range(ref.shape[0]):
            ref[i, :, pl.ds(x, LANES)] = jnp.zeros((NT, LANES), f32)


def end_rows(n, x0, src, dst, slope_before, si_ref, sc_ref, mask_ref, scale, carry, slot):
    here = pl.ds(x0, CHUNK)
    for lo, hi in ((0, dst.low - 1), (n - dst.high, n - 1)):
        out = stencil(
            lambda i: src.load(i, pl.ds(x0, CHUNK + LANES)),
            lambda i: slope_before if i == -1 else si_ref[i + 1, :, here],
            lambda i: sc_ref[i, :, here],
            lo, hi, -1, n - 1, carry, slot, scale,
        )
        for i in range(lo, hi + 1):
            known = mask_ref[pl.ds(i, 1), here].astype(f32) * 4.0
            dst.store(i, here, (known - SHIFT) * src.load(i, here) + out[i])
        slot += hi - lo + 1
    return slot


def beyond(rows_ref, row, wide, diagonal, cross, slope, carry, slot, further=None):
    here = pl.ds(wide.start, CHUNK)
    sd = sum_diff(rows_ref[row, :, wide])
    near = head(sd, CHUNK)
    same, later = cross_terms(sd, cross, carry, slot)
    if further is None:
        inner = parts(slope * near[1] - near[0], slope)
    else:
        inner = parts(inline_res(near, sum_diff(further), slope), slope)
    return diagonal * rows_ref[row, :, here] + (same - inner[1]) + time_behind(later - inner[0]), inner


def join_kernel(
    n, x,
    d_ref, si_ref, sc_ref, mask_ref, g_in, bg_in, b2g_in, bd_in, b2d_in, sums_in, eps_in,
    up_first, up_ref, down_ref,
    g_out, bg_out, b2g_out, bd_out, b2d_out, moments_ref,
    eps_ref, mask_up, ghosts, carry, sums,
):
    not_first, not_last = place_flags()
    clear_pads(x, (eps_ref, ghosts, g_out, bg_out, b2g_out, bd_out, b2d_out))
    carry[...] = jnp.zeros(carry.shape, f32)
    sums[...] = sums_in[...]
    share = x // NT
    for s in range(NT):
        mask_up[:, pl.ds(s * share, share)] = up_ref[pl.ds(s, 1), pl.ds(LATE0 * x, share)] * 4.0 - SHIFT
    g_rows, bg_rows, b2g_rows, d_rows, bd_rows, b2d_rows = (
        Mended(n, low, high, whole, ends, (ghosts, 2 * k), (ghosts, 2 * k + 1))
        for k, (low, high, whole, ends) in enumerate(zip(
            LOW, HIGH, (g_in, bg_in, b2g_in, d_ref, bd_in, b2d_in), (g_out, bg_out, b2g_out, None, bd_out, b2d_out)))
    )

    def zeroth(c, _):
        x0 = at_chunk(c)
        here = pl.ds(x0, CHUNK)
        g_rows.store(-1, here, row_of(down_ref, G1, x, x0))
        g_rows.store(0, here, g_in[1, :, here] + row_of(down_ref, WM1, x, x0))
        g_rows.store(n, here, (row_of(up_ref, G0, x, x0) + eps_in[0, :, here]) * not_last)
        bd_rows.store(-1, here, row_of(down_ref, BD1, x, x0))
        bd_rows.store(0, here, bd_in[1, :, here] + row_of(down_ref, WD1, x, x0))
        bd_rows.store(n, here, (row_of(up_ref, BD0, x, x0) + eps_in[1, :, here]) * not_last)
        return 0

    lax.fori_loop(0, chunks(x), zeroth, 0)

    def first(c, _):
        x0 = at_chunk(c)
        here = pl.ds(x0, CHUNK)
        before = row_of(down_ref, SI1, x, x0)
        slope = si_ref[n, :, here]
        slot = end_rows(n, x0, g_rows, bg_rows, before, si_ref, sc_ref, mask_ref, not_first, carry, 0)
        slot = end_rows(n, x0, bd_rows, b2d_rows, before, si_ref, sc_ref, mask_ref, not_first, carry, slot)
        wide = pl.ds(x0, CHUNK + LANES)
        slope_up, cross_up = row_of(up_first, SI0, x, x0), row_of(up_ref, SC0, x, x0)
        diagonal = mask_up[:, here]
        own, inner = beyond(eps_in, 0, wide, diagonal, cross_up, slope_up, carry, slot)
        eps = own + to_next(boundary(g_rows, n - 1, slope, here))
        eps_ref[0, :, here] = eps
        eps_ref[1, :, here] = to_next(inner)
        bg_rows.store(n, here, (row_of(up_ref, BG0, x, x0) + eps) * not_last)
        own, _ = beyond(eps_in, 1, wide, diagonal, cross_up, slope_up, carry, slot + 1)
        eps = own + to_next(boundary(bd_rows, n - 1, slope, here))
        b2d_rows.store(n, here, (row_of(up_ref, B2D0, x, x0) + eps) * not_last)
        bg_rows.store(-1, here, row_of(down_ref, BG1, x, x0) + to_self(boundary(g_rows, -1, before, here, not_first)))
        return 0

    lax.fori_loop(0, chunks(x), first, 0)
    carry[...] = jnp.zeros(carry.shape, f32)

    def second(c, _):
        x0 = at_chunk(c)
        here = pl.ds(x0, CHUNK)
        wide = pl.ds(x0, CHUNK + LANES)
        before = row_of(down_ref, SI1, x, x0)
        slot = end_rows(n, x0, bg_rows, b2g_rows, before, si_ref, sc_ref, mask_ref, not_first, carry, 0)
        own, _ = beyond(
            eps_ref, 0, wide, mask_up[:, here], row_of(up_ref, SC0, x, x0), row_of(up_first, SI0, x, x0),
            carry, slot, eps_ref[1, :, here])
        edge = to_next(boundary(bg_rows, n - 1, si_ref[n, :, here], here))
        b2g_rows.store(n, here, (row_of(up_ref, B2G0, x, x0) + own + edge) * not_last)
        return 0

    lax.fori_loop(0, chunks(x), second, 0)

    def third(c, _):
        loads = [rows.load for rows in (g_rows, bg_rows, b2g_rows, d_rows, bd_rows, b2d_rows)]
        products(n, at_chunk(c), loads, mask_ref, si_ref, sc_ref, sums, lambda done: not done)
        return 0

    lax.fori_loop(0, chunks(x), third, 0)
    for k in range(N_MOMENTS):
        moments_ref[pl.ds(k, 1), :] = jnp.sum(sums[k], axis=0, keepdims=True)
    moments_ref[pl.ds(N_MOMENTS, 24 - N_MOMENTS), :] = jnp.zeros((24 - N_MOMENTS, LANES), f32)


def add_terms(terms):
    total = None
    for term in terms:
        total = term if total is None else total + term
    return total


def solve(moments):
    mu, nu, xi = moments[:6], moments[6:12], moments[12:]

    def entry(a, b, i, j):
        if a == 0 and b == 0:
            return mu[i + j]
        if a == 1 and b == 1:
            return xi[i + j]
        return nu[i + j]

    shifted = {}

    def entry_a(a, b, i, j):
        which = a + b
        if (which, i + j) not in shifted:
            if i + j == 4:
                value = entry(a, b, 2, 3)
            else:
                value = entry(a, b, i, j + 1) + SHIFT * entry(a, b, i, j)
            shifted[which, i + j] = value * 0.25
        return shifted[which, i + j]

    def form(get, u, v):
        rows = []
        for (a, i), left in u.items():
            inner = add_terms(right * get(a, b, i, j) for (b, j), right in v.items())
            rows.append(left * inner)
        return add_terms(rows)

    def axpy(scale, u, v):
        out = dict(v)
        for key, value in u.items():
            term = scale * value
            out[key] = out[key] + term if key in out else term
        return out

    one = jnp.ones_like(mu[0])
    gradient = {(0, 0): 0.25 * one}
    direction = {(1, 0): one}
    model = {}
    for iteration in range(ITERS):
        mixing = -form(entry_a, gradient, direction) / form(entry_a, direction, direction)
        direction = axpy(mixing, direction, gradient)
        step = form(entry, gradient, direction) / form(entry_a, direction, direction)
        model = axpy(step, direction, model)
        if iteration < ITERS - 1:
            image = {key: value * (0.25 * SHIFT) for key, value in direction.items()}
            image = axpy(0.25, {(a, i + 1): value for (a, i), value in direction.items()}, image)
            gradient = axpy(-step, image, gradient)
    return model, direction


def last_kernel(
    n, x, moments_ref, m_ref, d_ref, g_in, bg_in, b2g_in, bd_in, b2d_in, g_end, bg_end, b2g_end, bd_end, b2d_end,
    model_hbm, dir_hbm, mo_ref, do_ref, sems,
):
    moments = [
        jnp.broadcast_to(jnp.sum(moments_ref[pl.ds(k, 1), :], axis=1, keepdims=True), (NT, LANES))
        for k in range(N_MOMENTS)
    ]
    model, direction = solve(moments)
    rows = [
        Mended(n, LOW[k], HIGH[k], whole, ends)
        for k, whole, ends in ((0, g_in, g_end), (1, bg_in, bg_end), (2, b2g_in, b2g_end), (4, bd_in, bd_end), (5, b2d_in, b2d_end))
    ]
    keys = ((0, 0), (0, 1), (0, 2), (1, 1), (1, 2))
    copies = []
    for i in range(n):
        def step(c, _):
            x0 = pl.multiple_of(c * LANES, LANES)
            here = pl.ds(x0, LANES)
            values = {key: vector.load(i, here) for key, vector in zip(keys, rows)}
            values[1, 0] = d_ref[i + 1, :, here]
            mo_ref[i, :, here] = m_ref[i + 1, :, here] + add_terms(
                model[key] * value for key, value in values.items())
            do_ref[i, :, here] = add_terms(direction[key] * value for key, value in values.items())
            return 0

        lax.fori_loop(0, x // LANES, step, 0, unroll=4)
        for k, (src, dst) in enumerate(((mo_ref, model_hbm), (do_ref, dir_hbm))):
            copy = pltpu.make_async_copy(src.at[i], dst.at[i], sems.at[2 * i + k])
            copy.start()
            copies.append(copy)
    for copy in copies:
        copy.wait()


def in_vmem(values):
    return [pltpu.with_memory_space_constraint(v, pltpu.VMEM) for v in values]


def kept(shape, dtype=f32):
    return pltpu.VMEM(shape, dtype)


def on_device(*args):
    n, _, x = args[0].shape
    peers = lax.axis_size("inline")
    assert peers & (peers - 1) == 0 and n >= 7 and x % CHUNK == 0
    vmem = pl.BlockSpec(memory_space=pltpu.VMEM)
    hbm = pl.BlockSpec(memory_space=pl.ANY)
    params = pltpu.CompilerParams(vmem_limit_bytes=VMEM_LIMIT)
    wide = kept((n + 2, NT, x + LANES))
    share = x // NT

    args = [pltpu.with_memory_space_constraint(v, pltpu.HBM) for v in args]

    def call(kernel, out_shape, in_specs, scratch_shapes, name):
        return pl.pallas_call(
            functools.partial(kernel, n, x),
            out_shape=out_shape,
            in_specs=in_specs,
            out_specs=[vmem] * len(out_shape),
            scratch_shapes=scratch_shapes,
            compiler_params=params,
            name=name,
        )

    def carry(slots):
        return pltpu.VMEM((slots, 2, NT, LANES), f32)

    def ends(rows):
        return kept((rows, NT, x + LANES))

    def to_before(value):
        return lax.ppermute(value, "inline", [(i, i - 1) for i in range(1, peers)])

    up_first, = call(
        pack_kernel, [kept((NT, FIRST0 * x))], [hbm] * 3, [pltpu.SemaphoreType.DMA((3,))], "pack",
    )(args[2], args[4], args[5])
    up_first = to_before(up_first)

    *loaded, up = call(
        first_kernel,
        [kept((n, NT, x)), kept((n, x), jnp.int32), kept((n + 2, NT, x)), kept((n, NT, x)), wide, wide,
         kept((NT, LATE0 * x + share))],
        [hbm] * 6,
        [pltpu.VMEM((4, NT, x + LANES), f32)] * 3 + [carry(5), pltpu.SemaphoreType.DMA((6,))], "first",
    )(*args)
    loaded = in_vmem(loaded)
    _, mask, si, sc, m, d = loaded
    up = to_before(up)

    down, eps = call(
        down_kernel, [kept((NT, DOWN1 * x)), ends(2)], [vmem] * 7,
        [pltpu.VMEM((n + 2, NT, x + LANES), f32), carry(3)], "down",
    )(*loaded, up_first)
    received = lax.ppermute(down, "inline", [(i, i + 1) for i in range(peers - 1)])

    made = call(
        local_kernel, [wide, wide, wide, wide, wide, kept((N_MOMENTS, NT, LANES))], [vmem] * 7,
        [carry(2 * n)], "local",
    )(*loaded, down)
    g, bg, b2g, bd, b2d, sums = in_vmem(made)

    out = call(
        join_kernel,
        [ends(LOW[k] + HIGH[k]) for k in (0, 1, 2, 4, 5)] + [jax.ShapeDtypeStruct((24, LANES), f32)], [vmem] * 14,
        [pltpu.VMEM((2, NT, x + LANES), f32), pltpu.VMEM((1, x), f32), pltpu.VMEM((12, NT, x + LANES), f32), carry(8),
         pltpu.VMEM((N_MOMENTS, NT, LANES), f32)], "join",
    )(d, si, sc, mask, g, bg, b2g, bd, b2d, sums, eps, up_first, up, received)
    moments = out[5]

    reach = 1
    while reach < peers:
        span = min(4, peers // reach)
        others = [lax.ppermute(moments, "inline", [(i, i ^ (k * reach)) for i in range(peers)]) for k in range(1, span)]
        moments = moments + add_terms(others)
        reach *= span

    return pl.pallas_call(
        functools.partial(last_kernel, n, x),
        out_shape=[jax.ShapeDtypeStruct((n, NT, x), f32)] * 2,
        in_specs=[vmem] * 13,
        out_specs=[hbm] * 2,
        scratch_shapes=[
            pltpu.VMEM((n, NT, x), f32),
            pltpu.VMEM((n, NT, x), f32),
            pltpu.SemaphoreType.DMA((2 * n,)),
        ],
        compiler_params=params,
        name="last",
    )(
        moments, m, d, g, bg, b2g, bd, b2d, *in_vmem(out[:5]))


def solution(mesh):
    rows = P(("groups", "inline"), None, None)
    return jax.shard_map(
        on_device,
        mesh=mesh,
        in_specs=(rows, P(("groups", "inline"), None), rows, rows, rows, rows),
        out_specs=(rows, rows),
        check_vma=False,
    )
```

time: 55.9 us -> 53.9 us (0.964)
  starting transfers between devices: 26.8 us -> 24.7 us
    ppermute x8 -> x9, starting transfers between devices: 26.8 us -> 24.7 us  [the longest x6 16.8 us: on_device(): lax.ppermute(moments, 'inline', [(i, i ^ k * reach) for i in range(peers)])]
    ppermute x8 -> x9, waiting for transfers between devices: 6.64 us -> 6.82 us  [the longest x6 6.81 us: on_device(): lax.ppermute(moments, 'inline', [(i, i ^ k * reach) for i in range(peers)])]
  transfers between devices with their start and end apart: 8 -> 9, of which waited for: 4 -> 4; matrix products, arithmetic and copies ran while one was open for 0% -> 0% of each run, Pallas kernels for 23% -> 24%
where the time goes in v4:
time: 53.9 us; the launch traced here: 53.7 us
  starting transfers between devices  24.7 us (46%)
  Pallas kernels  21.3 us (40%)
  waiting for transfers between devices  6.82 us (13%)
  between operations  0.88 us (2%)
    ppermute x6, starting transfers between devices, on_device(): lax.ppermute(moments, 'inline', [(i, i ^ k * reach) for i in range(peers)])  16.8 us
    pallas_call x1, Pallas kernels, on_device(): call(local_kernel, [wide, wide, wide, wide, wide, kept((N_MOMENTS, NT, LA...  7.16 us
    ppermute x6, waiting for transfers between devices, on_device(): lax.ppermute(moments, 'inline', [(i, i ^ k * reach) for i in range(peers)])  6.81 us
    ppermute x1, starting transfers between devices, on_device(): lax.ppermute(down, 'inline', [(i, i + 1) for i in range(peers - 1)])  5.32 us
    pallas_call x1, Pallas kernels, on_device(): call(join_kernel, [ends(LOW[k] + HIGH[k]) for k in (0, 1, 2, 4, 5)] + [ja...  5.07 us
    pallas_call x1, Pallas kernels, on_device(): call(first_kernel, [kept((n, NT, x)), kept((n, x), jnp.int32), kept((n +...  4.63 us
    ppermute x2, starting transfers between devices, to_before(): return lax.ppermute(value, 'inline', [(i, i - 1) for i in range(1, peers)])  2.58 us
    pallas_call x1, Pallas kernels, on_device(): pl.pallas_call(functools.partial(last_kernel, n, x), out_shape=[jax.Shape...  2.35 us
  transfers between devices with their start and end apart: 9, of which 4 were waited for; matrix products, arithmetic and copies ran while one was open for 0% of the time, Pallas kernels for 24%

profile of v4, /device:TPU:0, one launch (start us, length us, event | category | flops | bytes accessed | tf_op | source)
XLA Modules:
  0.0 53.7 jit_solution(6012218023687546722)
XLA Ops:
  0.6 1.1 %pack.1 = f32[8,12288]{1,0:T(8,128)S(1)} custom-call(f32[8,8,4096]{2,1,0:T(8,128)} %si_hbm.3, f32[8,8,4096]{2,1,0:T(8,128)} %model_hbm.3, f32[8,8,4096]{2,1,0:T(8,128)} %dir_hbm.3), custom_call_target="tpu_custom_call" | custom-call | tf_op jit(solution)/shard_map/pack/pallas_call | solution.py:688
  1.7 1.3 %collective-permute-start = (f32[8,12288]{1,0:T(8,128)S(1)}, f32[8,12288]{1,0:T(8,128)S(1)}, u32[]{:S(2)}, u32[]{:S(2)}) collective-permute-start(f32[8,12288]{1,0:T(8,128)S(1)} %pack.1), channel_id=1, source_target_pairs={{1,0},{2,1},{3,2},{4,3},{5,4},{6,5},{7,6},{8,7},{9,8},{10,9},{11,1... | collective-permute-start | bytes 1179656 | tf_op jit(solution)/shard_map/ppermute | solution.py:686
  3.0 4.6 %first.1 = (f32[8,8,4096]{2,1,0:T(8,128)S(1)}, s32[8,4096]{1,0:T(8,128)S(1)}, f32[10,8,4096]{2,1,0:T(8,128)S(1)}, f32[8,8,4096]{2,1,0:T(8,128)S(1)}, f32[10,8,42...) custom-call(f32[8,8,4096]{2,1,0:T(8,128)} %data_hbm.1, s32[8,4096]{1,0:T(8,128)} %mask_hbm.1, ...), custom_call_target="tpu_custom_call" | custom-call | tf_op jit(solution)/shard_map/first/pallas_call | solution.py:693
  7.6 1.3 %collective-permute-start.1 = (f32[8,25088]{1,0:T(8,128)S(1)}, f32[8,25088]{1,0:T(8,128)S(1)}, u32[]{:S(2)}, u32[]{:S(2)}) collective-permute-start(f32[8,25088]{1,0:T(8,128)S(1)} %get-tuple-element.37), channel_id=1, source_target_pairs={{1,0},{2,1},{3,2},{4,3},{5,4},{6,5},{7,6},{8,7},{9,8},{10,9},{11,1... | collective-permute-start | bytes 2408456 | tf_op jit(solution)/shard_map/ppermute | solution.py:686
  8.9 0.0 collective-permute-done.up_first
  8.9 1.0 %down.1 = (f32[8,24576]{1,0:T(8,128)S(1)}, f32[2,8,4224]{2,1,0:T(8,128)S(1)}) custom-call(f32[8,8,4096]{2,1,0:T(8,128)S(1)} %get-tuple-element.27.data_ref, s32[8,4096]{1,0:T(8,128)S(1)} %get-tuple-element.26.mask_ref, f32[10,8,4096]{2,1,0:T(8,128)S(1)} %get-tuple-element.24.si_ref, f32[8,8,4096]{2,1,0:T(8,128)S(1)} %get-tuple-element.25.sc_ref, ...), custom_call_target="tpu_custom_call" | custom-call | tf_op jit(solution)/shard_map/down/pallas_call | solution.py:704
  10.0 5.3 %collective-permute-start.2 = (f32[8,24576]{1,0:T(8,128)S(1)}, f32[8,24576]{1,0:T(8,128)S(1)}, u32[]{:S(2)}, u32[]{:S(2)}) collective-permute-start(f32[8,24576]{1,0:T(8,128)S(1)} %get-tuple-element.29.down_ref), channel_id=1, source_target_pairs={{0,1},{1,2},{2,3},{3,4},{4,5},{5,6},{6,7},{7,8},{8,9},{9,10},{10,1... | collective-permute-start | bytes 2359304 | tf_op jit(solution)/shard_map/ppermute | solution.py:708
  15.3 7.2 %local.1 = (f32[10,8,4224]{2,1,0:T(8,128)S(1)}, f32[10,8,4224]{2,1,0:T(8,128)S(1)}, f32[10,8,4224]{2,1,0:T(8,128)S(1)}, f32[10,8,4224]{2,1,0:T(8,128)S(1)}, f32[...) custom-call(f32[8,8,4096]{2,1,0:T(8,128)S(1)} %get-tuple-element.27.data_ref, ...), custom_call_target="tpu_custom_call" | custom-call | tf_op jit(solution)/shard_map/local/pallas_call | solution.py:710
  22.5 0.0 collective-permute-done.1.up_ref
  22.5 0.0 collective-permute-done.2.down_ref
  22.5 5.1 %join.1 = (f32[1,8,4224]{2,1,0:T(8,128)S(1)}, f32[3,8,4224]{2,1,0:T(8,128)S(1)}, f32[5,8,4224]{2,1,0:T(8,128)S(1)}, f32[1,8,4224]{2,1,0:T(8,128)S(1)}, f32[3,8,4224]{2,1,0:T(8,128)S(1)}, /*index=5*/f32[24,128]{1,0:T(8,128)S(1)}) custom-call(f32[10,8,4224]{2,1,0:T(8,128)S(1)} %get-tuple-element.23.d_ref, f32[10,8,4096]{2,1,0:T(8,128)S(1)} %get-tuple-element.24.si_ref, ...), custom_call_target="tpu_custom_call" | custom-call | tf_op jit(solution)/shard_map/join/pallas_call | solution.py:716
  27.6 9.9 %collective-permute-start.3 = (f32[24,128]{1,0:T(8,128)S(1)}, f32[24,128]{1,0:T(8,128)S(1)}, u32[]{:S(2)}, u32[]{:S(2)}) collective-permute-start(f32[24,128]{1,0:T(8,128)S(1)} %get-tuple-element.38), channel_id=1, source_target_pairs={{0,1},{1,0},{2,3},{3,2},{4,5},{5,4},{6,7},{7,6},{8,9},{9,8},{10,11... | collective-permute-start | bytes 36872 | tf_op jit(solution)/shard_map/ppermute | solution.py:727
  37.5 2.4 %collective-permute-start.4 = (f32[24,128]{1,0:T(8,128)S(1)}, f32[24,128]{1,0:T(8,128)S(1)}, u32[]{:S(2)}, u32[]{:S(2)}) collective-permute-start(f32[24,128]{1,0:T(8,128)S(1)} %get-tuple-element.38), channel_id=1, source_target_pairs={{0,2},{1,3},{2,0},{3,1},{4,6},{5,7},{6,4},{7,5},{8,10},{9,11},{10,... | collective-permute-start | bytes 36872 | tf_op jit(solution)/shard_map/ppermute | solution.py:727
  39.9 0.1 collective-permute-start.5
  40.0 0.0 collective-permute-done.3
  40.0 1.6 %collective-permute-done.4 = f32[24,128]{1,0:T(8,128)S(1)} collective-permute-done((f32[24,128]{1,0:T(8,128)S(1)}, f32[24,128]{1,0:T(8,128)S(1)}, u32[]{:S(2)}, u32[]{:S(2)}) %collective-permute-start.4) | collective-permute-done | bytes 12320 | tf_op jit(solution)/shard_map/ppermute | solution.py:727
  41.6 1.4 %collective-permute-done.5 = f32[24,128]{1,0:T(8,128)S(1)} collective-permute-done((f32[24,128]{1,0:T(8,128)S(1)}, f32[24,128]{1,0:T(8,128)S(1)}, u32[]{:S(2)}, u32[]{:S(2)}) %collective-permute-start.5) | collective-permute-done | bytes 12320 | tf_op jit(solution)/shard_map/ppermute | solution.py:727
  43.1 1.6 %collective-permute-start.6 = (f32[24,128]{1,0:T(8,128)S(1)}, f32[24,128]{1,0:T(8,128)S(1)}, u32[]{:S(2)}, u32[]{:S(2)}) collective-permute-start(f32[24,128]{1,0:T(8,128)S(1)} %add_add_fusion.1), channel_id=1, source_target_pairs={{0,4},{1,5},{2,6},{3,7},{4,0},{5,1},{6,2},{7,3},{8,12},{9,13},{10,... | collective-permute-start | bytes 36872 | tf_op jit(solution)/shard_map/ppermute | solution.py:727
  44.6 1.1 %collective-permute-start.7 = (f32[24,128]{1,0:T(8,128)S(1)}, f32[24,128]{1,0:T(8,128)S(1)}, u32[]{:S(2)}, u32[]{:S(2)}) collective-permute-start(f32[24,128]{1,0:T(8,128)S(1)} %add_add_fusion.1), channel_id=1, source_target_pairs={{0,8},{1,9},{2,10},{3,11},{4,12},{5,13},{6,14},{7,15},{8,0},{9,1},... | collective-permute-start | bytes 36872 | tf_op jit(solution)/shard_map/ppermute | solution.py:727
  45.7 1.7 %collective-permute-start.8 = (f32[24,128]{1,0:T(8,128)S(1)}, f32[24,128]{1,0:T(8,128)S(1)}, u32[]{:S(2)}, u32[]{:S(2)}) collective-permute-start(f32[24,128]{1,0:T(8,128)S(1)} %add_add_fusion.1), channel_id=1, source_target_pairs={{0,12},{1,13},{2,14},{3,15},{4,8},{5,9},{6,10},{7,11},{8,4},{9,5},... | collective-permute-start | bytes 36872 | tf_op jit(solution)/shard_map/ppermute | solution.py:727
  47.5 0.0 collective-permute-done.6
  47.5 1.8 %collective-permute-done.7 = f32[24,128]{1,0:T(8,128)S(1)} collective-permute-done((f32[24,128]{1,0:T(8,128)S(1)}, f32[24,128]{1,0:T(8,128)S(1)}, u32[]{:S(2)}, u32[]{:S(2)}) %collective-permute-start.7) | collective-permute-done | bytes 12320 | tf_op jit(solution)/shard_map/ppermute | solution.py:727
  49.3 2.0 %collective-permute-done.8 = f32[24,128]{1,0:T(8,128)S(1)} collective-permute-done((f32[24,128]{1,0:T(8,128)S(1)}, f32[24,128]{1,0:T(8,128)S(1)}, u32[]{:S(2)}, u32[]{:S(2)}) %collective-permute-start.8) | collective-permute-done | bytes 12320 | tf_op jit(solution)/shard_map/ppermute | solution.py:727
  51.2 2.4 %last.1 = (f32[8,8,4096]{2,1,0:T(8,128)}, f32[8,8,4096]{2,1,0:T(8,128)}) custom-call(f32[24,128]{1,0:T(8,128)S(1)} %add_add_fusion.moments_ref, f32[10,8,4224]{2,1,0:T(8,128)S(1)} %get-tuple-element.28.m_ref, f32[10,8,4224]{2,1,0:T(8,128)S(1)} %get-tuple-element.23.d_ref, f32[10,8,4224]{2,1,0:T(8,128)S(1)} %get-tuple-element.30.g_in, ...), custom_call_target="tpu_custom_call" | custom-call | tf_op jit(solution)/shard_map/last/pallas_call | solution.py:731
  (2 shorter events, 0.0 us)
Async XLA Ops:
  1.7 7.2 %collective-permute-start = (f32[8,12288]{1,0:T(8,128)S(1)}, f32[8,12288]{1,0:T(8,128)S(1)}, u32[]{:S(2)}, u32[]{:S(2)}) collective-permute-start(f32[8,12288]{1,0:T(8,128)S(1)} %pack.1), channel_id=1, source_target_pairs={{1,0},{2,1},{3,2},{4,3},{5,4},{6,5},{7,6},{8,7},{9,8},{10,9},{11,1... | collective-permute-start | bytes 1179656 | tf_op jit(solution)/shard_map/ppermute | solution.py:686
  7.6 14.9 %collective-permute-start.1 = (f32[8,25088]{1,0:T(8,128)S(1)}, f32[8,25088]{1,0:T(8,128)S(1)}, u32[]{:S(2)}, u32[]{:S(2)}) collective-permute-start(f32[8,25088]{1,0:T(8,128)S(1)} %get-tuple-element.37), channel_id=1, source_target_pairs={{1,0},{2,1},{3,2},{4,3},{5,4},{6,5},{7,6},{8,7},{9,8},{10,9},{11,1... | collective-permute-start | bytes 2408456 | tf_op jit(solution)/shard_map/ppermute | solution.py:686
  10.0 12.5 %collective-permute-start.2 = (f32[8,24576]{1,0:T(8,128)S(1)}, f32[8,24576]{1,0:T(8,128)S(1)}, u32[]{:S(2)}, u32[]{:S(2)}) collective-permute-start(f32[8,24576]{1,0:T(8,128)S(1)} %get-tuple-element.29.down_ref), channel_id=1, source_target_pairs={{0,1},{1,2},{2,3},{3,4},{4,5},{5,6},{6,7},{7,8},{8,9},{9,10},{10,1... | collective-permute-start | bytes 2359304 | tf_op jit(solution)/shard_map/ppermute | solution.py:708
  27.6 12.4 %collective-permute-start.3 = (f32[24,128]{1,0:T(8,128)S(1)}, f32[24,128]{1,0:T(8,128)S(1)}, u32[]{:S(2)}, u32[]{:S(2)}) collective-permute-start(f32[24,128]{1,0:T(8,128)S(1)} %get-tuple-element.38), channel_id=1, source_target_pairs={{0,1},{1,0},{2,3},{3,2},{4,5},{5,4},{6,7},{7,6},{8,9},{9,8},{10,11... | collective-permute-start | bytes 36872 | tf_op jit(solution)/shard_map/ppermute | solution.py:727
  37.5 4.1 %collective-permute-start.4 = (f32[24,128]{1,0:T(8,128)S(1)}, f32[24,128]{1,0:T(8,128)S(1)}, u32[]{:S(2)}, u32[]{:S(2)}) collective-permute-start(f32[24,128]{1,0:T(8,128)S(1)} %get-tuple-element.38), channel_id=1, source_target_pairs={{0,2},{1,3},{2,0},{3,1},{4,6},{5,7},{6,4},{7,5},{8,10},{9,11},{10,... | collective-permute-start | bytes 36872 | tf_op jit(solution)/shard_map/ppermute | solution.py:727
  39.9 3.1 %collective-permute-start.5 = (f32[24,128]{1,0:T(8,128)S(1)}, f32[24,128]{1,0:T(8,128)S(1)}, u32[]{:S(2)}, u32[]{:S(2)}) collective-permute-start(f32[24,128]{1,0:T(8,128)S(1)} %get-tuple-element.38), channel_id=1, source_target_pairs={{0,3},{1,2},{2,1},{3,0},{4,7},{5,6},{6,5},{7,4},{8,11},{9,10},{10,... | collective-permute-start | bytes 36872 | tf_op jit(solution)/shard_map/ppermute | solution.py:727
  43.1 4.4 %collective-permute-start.6 = (f32[24,128]{1,0:T(8,128)S(1)}, f32[24,128]{1,0:T(8,128)S(1)}, u32[]{:S(2)}, u32[]{:S(2)}) collective-permute-start(f32[24,128]{1,0:T(8,128)S(1)} %add_add_fusion.1), channel_id=1, source_target_pairs={{0,4},{1,5},{2,6},{3,7},{4,0},{5,1},{6,2},{7,3},{8,12},{9,13},{10,... | collective-permute-start | bytes 36872 | tf_op jit(solution)/shard_map/ppermute | solution.py:727
  44.6 4.6 %collective-permute-start.7 = (f32[24,128]{1,0:T(8,128)S(1)}, f32[24,128]{1,0:T(8,128)S(1)}, u32[]{:S(2)}, u32[]{:S(2)}) collective-permute-start(f32[24,128]{1,0:T(8,128)S(1)} %add_add_fusion.1), channel_id=1, source_target_pairs={{0,8},{1,9},{2,10},{3,11},{4,12},{5,13},{6,14},{7,15},{8,0},{9,1},... | collective-permute-start | bytes 36872 | tf_op jit(solution)/shard_map/ppermute | solution.py:727
  45.7 5.5 %collective-permute-start.8 = (f32[24,128]{1,0:T(8,128)S(1)}, f32[24,128]{1,0:T(8,128)S(1)}, u32[]{:S(2)}, u32[]{:S(2)}) collective-permute-start(f32[24,128]{1,0:T(8,128)S(1)} %add_add_fusion.1), channel_id=1, source_target_pairs={{0,12},{1,13},{2,14},{3,15},{4,8},{5,9},{6,10},{7,11},{8,4},{9,5},... | collective-permute-start | bytes 36872 | tf_op jit(solution)/shard_map/ppermute | solution.py:727

commit v5 on v4

--- a/solution.py
+++ b/solution.py
@@ -12,9 +12,9 @@
 LANES = 128
 CHUNK = 4096
 SHIFT = 18.0
-M0, D0, SI0, FIRST0 = range(4)
-SC0, G0, BD0, BG0, B2D0, B2G0, LATE0 = range(7)
-WM1, WD1, SI1, G1, BD1, BG1, DOWN1 = range(7)
+M0, D0, SI0, SC0, FIRST0 = range(5)
+G0, BD0, BG0, B2D0, B2G0, LATE0 = range(6)
+WM1, WD1, G1, BD1, BG1, DOWN1 = range(6)
 N_MOMENTS = 18
 VMEM_LIMIT = 16 * 1024 * 1024
 
@@ -177,10 +177,10 @@
     ref[:, pl.ds(pl.multiple_of(x0 + slot * x, CHUNK), CHUNK)] = value
 
 
-def pack_kernel(n, x, si_hbm, model_hbm, dir_hbm, up_ref, sems):
+def pack_kernel(n, x, si_hbm, sc_hbm, model_hbm, dir_hbm, up_ref, sems):
     copies = [
         pltpu.make_async_copy(source.at[0], up_ref.at[:, pl.ds(slot * x, x)], sems.at[slot])
-        for source, slot in ((model_hbm, M0), (dir_hbm, D0), (si_hbm, SI0))
+        for source, slot in ((model_hbm, M0), (dir_hbm, D0), (si_hbm, SI0), (sc_hbm, SC0))
     ]
     for copy in copies:
         copy.start()
@@ -191,22 +191,23 @@
 def first_kernel(
     n, x,
     data_hbm, mask_hbm, si_hbm, sc_hbm, model_hbm, dir_hbm,
-    data_ref, mask_ref, si_ref, sc_ref, m_ref, d_ref, up_ref,
+    data_ref, mask_ref, si_ref, sc_ref, m_ref, d_ref, up_ref, slope_ref,
     g_ref, bg_ref, bd_ref, carry, sems,
 ):
-    body = (pl.ds(1, n), slice(None), pl.ds(0, x))
-    copies = [
-        pltpu.make_async_copy(source, target, sems.at[k])
-        for k, (source, target) in enumerate((
-            (model_hbm, m_ref.at[body]), (dir_hbm, d_ref.at[body]), (si_hbm, si_ref.at[pl.ds(1, n)]), (sc_hbm, sc_ref),
-            (mask_hbm, mask_ref), (data_hbm, data_ref),
-        ))
-    ]
+    lanes = pl.ds(0, x)
+    copies = [pltpu.make_async_copy(mask_hbm, mask_ref, sems.at[0])]
+    for top in (True, False):
+        for source, target, skip in (
+            (model_hbm, m_ref, 1), (si_hbm, si_ref, 1), (sc_hbm, sc_ref, 0), (data_hbm, data_ref, 0), (dir_hbm, d_ref, 1),
+        ):
+            start, size = (0, 4) if top else (4, n - 4)
+            copies.append(pltpu.make_async_copy(
+                source.at[pl.ds(start, size)], target.at[pl.ds(start + skip, size), :, lanes], sems.at[len(copies)]))
     for copy in copies:
         copy.start()
     clear_pads(x, (m_ref, d_ref, g_ref, bg_ref, bd_ref))
     carry[...] = jnp.zeros(carry.shape, f32)
-    for copy in copies:
+    for copy in copies[:6]:
         copy.wait()
     share = x // NT
     for s in range(NT):
@@ -215,7 +216,6 @@
     def first(c, _):
         x0 = at_chunk(c)
         own = Own(n, x0, si_ref, sc_ref, mask_ref, carry)
-        put(up_ref, SC0, x, x0, sc_ref[0, :, own.here])
         out = own.gradient(data_ref, m_ref, 0, 2, 0)
         put(up_ref, G0, x, x0, out[0])
         for i, value in out.items():
@@ -248,6 +248,9 @@
         return 0
 
     lax.fori_loop(0, chunks(x), third, 0)
+    for copy in copies[6:]:
+        copy.wait()
+    slope_ref[...] = si_ref[n, :, lanes]
 
 
 def down_kernel(
@@ -274,7 +277,6 @@
         put(down_ref, BD1, x, x0, own.applied(d_ref, n - 1, n - 1, 2)[n - 1] + to_self(ef))
         eps_ref[1, :, here] = to_next(ef)
         put(down_ref, WD1, x, x0, eps_ref[1, :, here])
-        put(down_ref, SI1, x, x0, slope)
         return 0
 
     lax.fori_loop(0, chunks(x), first, 0)
@@ -471,7 +473,7 @@
 def join_kernel(
     n, x,
     d_ref, si_ref, sc_ref, mask_ref, g_in, bg_in, b2g_in, bd_in, b2d_in, sums_in, eps_in,
-    up_first, up_ref, down_ref,
+    up_first, up_ref, slope_ref, down_ref,
     g_out, bg_out, b2g_out, bd_out, b2d_out, moments_ref,
     eps_ref, mask_up, ghosts, carry, sums,
 ):
@@ -504,12 +506,12 @@
     def first(c, _):
         x0 = at_chunk(c)
         here = pl.ds(x0, CHUNK)
-        before = row_of(down_ref, SI1, x, x0)
+        before = slope_ref[:, here]
         slope = si_ref[n, :, here]
         slot = end_rows(n, x0, g_rows, bg_rows, before, si_ref, sc_ref, mask_ref, not_first, carry, 0)
         slot = end_rows(n, x0, bd_rows, b2d_rows, before, si_ref, sc_ref, mask_ref, not_first, carry, slot)
         wide = pl.ds(x0, CHUNK + LANES)
-        slope_up, cross_up = row_of(up_first, SI0, x, x0), row_of(up_ref, SC0, x, x0)
+        slope_up, cross_up = row_of(up_first, SI0, x, x0), row_of(up_first, SC0, x, x0)
         diagonal = mask_up[:, here]
         own, inner = beyond(eps_in, 0, wide, diagonal, cross_up, slope_up, carry, slot)
         eps = own + to_next(boundary(g_rows, n - 1, slope, here))
@@ -529,10 +531,10 @@
         x0 = at_chunk(c)
         here = pl.ds(x0, CHUNK)
         wide = pl.ds(x0, CHUNK + LANES)
-        before = row_of(down_ref, SI1, x, x0)
+        before = slope_ref[:, here]
         slot = end_rows(n, x0, bg_rows, b2g_rows, before, si_ref, sc_ref, mask_ref, not_first, carry, 0)
         own, _ = beyond(
-            eps_ref, 0, wide, mask_up[:, here], row_of(up_ref, SC0, x, x0), row_of(up_first, SI0, x, x0),
+            eps_ref, 0, wide, mask_up[:, here], row_of(up_first, SC0, x, x0), row_of(up_first, SI0, x, x0),
             carry, slot, eps_ref[1, :, here])
         edge = to_next(boundary(bg_rows, n - 1, si_ref[n, :, here], here))
         b2g_rows.store(n, here, (row_of(up_ref, B2G0, x, x0) + own + edge) * not_last)
@@ -685,27 +687,31 @@
     def to_before(value):
         return lax.ppermute(value, "inline", [(i, i - 1) for i in range(1, peers)])
 
+    def to_after(value):
+        return lax.ppermute(value, "inline", [(i, i + 1) for i in range(peers - 1)])
+
     up_first, = call(
-        pack_kernel, [kept((NT, FIRST0 * x))], [hbm] * 3, [pltpu.SemaphoreType.DMA((3,))], "pack",
-    )(args[2], args[4], args[5])
+        pack_kernel, [kept((NT, FIRST0 * x))], [hbm] * 4, [pltpu.SemaphoreType.DMA((4,))], "pack",
+    )(*args[2:])
     up_first = to_before(up_first)
 
-    *loaded, up = call(
+    *loaded, up, slope = call(
         first_kernel,
         [kept((n, NT, x)), kept((n, x), jnp.int32), kept((n + 2, NT, x)), kept((n, NT, x)), wide, wide,
-         kept((NT, LATE0 * x + share))],
+         kept((NT, LATE0 * x + share)), kept((NT, x))],
         [hbm] * 6,
-        [pltpu.VMEM((4, NT, x + LANES), f32)] * 3 + [carry(5), pltpu.SemaphoreType.DMA((6,))], "first",
+        [pltpu.VMEM((4, NT, x + LANES), f32)] * 3 + [carry(5), pltpu.SemaphoreType.DMA((11,))], "first",
     )(*args)
     loaded = in_vmem(loaded)
     _, mask, si, sc, m, d = loaded
     up = to_before(up)
+    slope = to_after(slope)
 
     down, eps = call(
         down_kernel, [kept((NT, DOWN1 * x)), ends(2)], [vmem] * 7,
         [pltpu.VMEM((n + 2, NT, x + LANES), f32), carry(3)], "down",
     )(*loaded, up_first)
-    received = lax.ppermute(down, "inline", [(i, i + 1) for i in range(peers - 1)])
+    received = to_after(down)
 
     made = call(
         local_kernel, [wide, wide, wide, wide, wide, kept((N_MOMENTS, NT, LANES))], [vmem] * 7,
@@ -715,10 +721,10 @@
 
     out = call(
         join_kernel,
-        [ends(LOW[k] + HIGH[k]) for k in (0, 1, 2, 4, 5)] + [jax.ShapeDtypeStruct((24, LANES), f32)], [vmem] * 14,
+        [ends(LOW[k] + HIGH[k]) for k in (0, 1, 2, 4, 5)] + [jax.ShapeDtypeStruct((24, LANES), f32)], [vmem] * 15,
         [pltpu.VMEM((2, NT, x + LANES), f32), pltpu.VMEM((1, x), f32), pltpu.VMEM((12, NT, x + LANES), f32), carry(8),
          pltpu.VMEM((N_MOMENTS, NT, LANES), f32)], "join",
-    )(d, si, sc, mask, g, bg, b2g, bd, b2d, sums, eps, up_first, up, received)
+    )(d, si, sc, mask, g, bg, b2g, bd, b2d, sums, eps, up_first, up, slope, received)
     moments = out[5]
 
     reach = 1

time: 53.9 us -> 49.8 us (0.924)
  waiting for transfers between devices: 6.82 us -> 4.63 us
  starting transfers between devices: 24.7 us -> 23.3 us
  Pallas kernels: 21.3 us -> 20.7 us
    ppermute x6, starting transfers between devices: 16.8 us -> 11.4 us  [on_device(): lax.ppermute(moments, 'inline', [(i, i ^ k * reach) for i in range(peers)])]
    ppermute x1 -> x2, starting transfers between devices: 5.32 us -> 9.34 us  [to_after(): return lax.ppermute(value, 'inline', [(i, i + 1) for i in range(peers - 1)])]
    ppermute x6, waiting for transfers between devices: 6.81 us -> 4.62 us  [on_device(): lax.ppermute(moments, 'inline', [(i, i ^ k * reach) for i in range(peers)])]
    pallas_call x1, Pallas kernels: 4.63 us -> 3.9 us  [on_device(): call(first_kernel, [kept((n, NT, x)), kept((n, x), jnp.int32), kept((n +...]
  transfers between devices with their start and end apart: 9 -> 10, of which waited for: 4 -> 3; matrix products, arithmetic and copies ran while one was open for 0% -> 0% of each run, Pallas kernels for 24% -> 24%
where the time goes in v5:
time: 49.8 us; the launch traced here: 49.5 us
  starting transfers between devices  23.3 us (47%)
  Pallas kernels  20.7 us (42%)
  waiting for transfers between devices  4.63 us (9%)
  between operations  0.9 us (2%)
    ppermute x6, starting transfers between devices, on_device(): lax.ppermute(moments, 'inline', [(i, i ^ k * reach) for i in range(peers)])  11.4 us
    ppermute x2, starting transfers between devices, to_after(): return lax.ppermute(value, 'inline', [(i, i + 1) for i in range(peers - 1)])  9.34 us
    pallas_call x1, Pallas kernels, on_device(): call(local_kernel, [wide, wide, wide, wide, wide, kept((N_MOMENTS, NT, LA...  7.16 us
    pallas_call x1, Pallas kernels, on_device(): call(join_kernel, [ends(LOW[k] + HIGH[k]) for k in (0, 1, 2, 4, 5)] + [ja...  5.08 us
    ppermute x6, waiting for transfers between devices, on_device(): lax.ppermute(moments, 'inline', [(i, i ^ k * reach) for i in range(peers)])  4.62 us
    pallas_call x1, Pallas kernels, on_device(): call(first_kernel, [kept((n, NT, x)), kept((n, x), jnp.int32), kept((n +...  3.9 us
    ppermute x2, starting transfers between devices, to_before(): return lax.ppermute(value, 'inline', [(i, i - 1) for i in range(1, peers)])  2.58 us
    pallas_call x1, Pallas kernels, on_device(): pl.pallas_call(functools.partial(last_kernel, n, x), out_shape=[jax.Shape...  2.36 us
  transfers between devices with their start and end apart: 10, of which 3 were waited for; matrix products, arithmetic and copies ran while one was open for 0% of the time, Pallas kernels for 24%

profile of v5, /device:TPU:0, one launch (start us, length us, event | category | flops | bytes accessed | tf_op | source)
XLA Modules:
  0.0 49.5 jit_solution(15646165782764734407)
XLA Ops:
  0.6 1.1 %pack.1 = f32[8,16384]{1,0:T(8,128)S(1)} custom-call(f32[8,8,4096]{2,1,0:T(8,128)} %si_hbm.3, f32[8,8,4096]{2,1,0:T(8,128)} %sc_hbm.3, f32[8,8,4096]{2,1,0:T(8,128)} %model_hbm.3, f32[8,8,4096]{2,1,0:T(8,128)} %dir_hbm.3), custom_call_target="tpu_custom_call" | custom-call | tf_op jit(solution)/shard_map/pack/pallas_call | solution.py:693
  1.8 1.3 %collective-permute-start = (f32[8,16384]{1,0:T(8,128)S(1)}, f32[8,16384]{1,0:T(8,128)S(1)}, u32[]{:S(2)}, u32[]{:S(2)}) collective-permute-start(f32[8,16384]{1,0:T(8,128)S(1)} %pack.1), channel_id=1, source_target_pairs={{1,0},{2,1},{3,2},{4,3},{5,4},{6,5},{7,6},{8,7},{9,8},{10,9},{11,1... | collective-permute-start | bytes 1572872 | tf_op jit(solution)/shard_map/ppermute | solution.py:688
  3.1 3.9 %first.1 = (f32[8,8,4096]{2,1,0:T(8,128)S(1)}, s32[8,4096]{1,0:T(8,128)S(1)}, f32[10,8,4096]{2,1,0:T(8,128)S(1)}, f32[8,8,4096]{2,1,0:T(8,128)S(1)}, f32[10,8,42...) custom-call(f32[8,8,4096]{2,1,0:T(8,128)} %data_hbm.1, ...), custom_call_target="tpu_custom_call" | custom-call | tf_op jit(solution)/shard_map/first/pallas_call | solution.py:698
  7.0 1.3 %collective-permute-start.1 = (f32[8,20992]{1,0:T(8,128)S(1)}, f32[8,20992]{1,0:T(8,128)S(1)}, u32[]{:S(2)}, u32[]{:S(2)}) collective-permute-start(f32[8,20992]{1,0:T(8,128)S(1)} %get-tuple-element.38), channel_id=1, source_target_pairs={{1,0},{2,1},{3,2},{4,3},{5,4},{6,5},{7,6},{8,7},{9,8},{10,9},{11,1... | collective-permute-start | bytes 2015240 | tf_op jit(solution)/shard_map/ppermute | solution.py:688
  8.3 0.0 collective-permute-done.up_first
  8.3 1.0 %down.1 = (f32[8,20480]{1,0:T(8,128)S(1)}, f32[2,8,4224]{2,1,0:T(8,128)S(1)}) custom-call(f32[8,8,4096]{2,1,0:T(8,128)S(1)} %get-tuple-element.28.data_ref, s32[8,4096]{1,0:T(8,128)S(1)} %get-tuple-element.27.mask_ref, f32[10,8,4096]{2,1,0:T(8,128)S(1)} %get-tuple-element.25.si_ref, f32[8,8,4096]{2,1,0:T(8,128)S(1)} %get-tuple-element.26.sc_ref, ...), custom_call_target="tpu_custom_call" | custom-call | tf_op jit(solution)/shard_map/down/pallas_call | solution.py:710
  9.3 7.3 %collective-permute-start.3 = (f32[8,20480]{1,0:T(8,128)S(1)}, f32[8,20480]{1,0:T(8,128)S(1)}, u32[]{:S(2)}, u32[]{:S(2)}) collective-permute-start(f32[8,20480]{1,0:T(8,128)S(1)} %get-tuple-element.30.down_ref), channel_id=1, source_target_pairs={{0,1},{1,2},{2,3},{3,4},{4,5},{5,6},{6,7},{7,8},{8,9},{9,10},{10,1... | collective-permute-start | bytes 1966088 | tf_op jit(solution)/shard_map/ppermute | solution.py:691
  16.6 2.1 %collective-permute-start.2 = (f32[8,4096]{1,0:T(8,128)S(1)}, f32[8,4096]{1,0:T(8,128)S(1)}, u32[]{:S(2)}, u32[]{:S(2)}) collective-permute-start(f32[8,4096]{1,0:T(8,128)S(1)} %get-tuple-element.39), channel_id=1, source_target_pairs={{0,1},{1,2},{2,3},{3,4},{4,5},{5,6},{6,7},{7,8},{8,9},{9,10},{10,1... | collective-permute-start | bytes 393224 | tf_op jit(solution)/shard_map/ppermute | solution.py:691
  18.7 7.2 %local.1 = (f32[10,8,4224]{2,1,0:T(8,128)S(1)}, f32[10,8,4224]{2,1,0:T(8,128)S(1)}, f32[10,8,4224]{2,1,0:T(8,128)S(1)}, f32[10,8,4224]{2,1,0:T(8,128)S(1)}, f32[...) custom-call(f32[8,8,4096]{2,1,0:T(8,128)S(1)} %get-tuple-element.28.data_ref, ...), custom_call_target="tpu_custom_call" | custom-call | tf_op jit(solution)/shard_map/local/pallas_call | solution.py:716
  25.9 0.0 collective-permute-done.2.slope_ref
  25.9 0.0 collective-permute-done.1.up_ref
  25.9 0.0 collective-permute-done.3.down_ref
  25.9 5.1 %join.1 = (f32[1,8,4224]{2,1,0:T(8,128)S(1)}, f32[3,8,4224]{2,1,0:T(8,128)S(1)}, f32[5,8,4224]{2,1,0:T(8,128)S(1)}, f32[1,8,4224]{2,1,0:T(8,128)S(1)}, f32[3,8,4224]{2,1,0:T(8,128)S(1)}, /*index=5*/f32[24,128]{1,0:T(8,128)S(1)}) custom-call(f32[10,8,4224]{2,1,0:T(8,128)S(1)} %get-tuple-element.24.d_ref, f32[10,8,4096]{2,1,0:T(8,128)S(1)} %get-tuple-element.25.si_ref, ...), custom_call_target="tpu_custom_call" | custom-call | tf_op jit(solution)/shard_map/join/pallas_call | solution.py:722
  31.0 2.8 %collective-permute-start.6 = (f32[24,128]{1,0:T(8,128)S(1)}, f32[24,128]{1,0:T(8,128)S(1)}, u32[]{:S(2)}, u32[]{:S(2)}) collective-permute-start(f32[24,128]{1,0:T(8,128)S(1)} %get-tuple-element.40), channel_id=1, source_target_pairs={{0,3},{1,2},{2,1},{3,0},{4,7},{5,6},{6,5},{7,4},{8,11},{9,10},{10,... | collective-permute-start | bytes 36872 | tf_op jit(solution)/shard_map/ppermute | solution.py:733
  33.8 4.1 %collective-permute-start.5 = (f32[24,128]{1,0:T(8,128)S(1)}, f32[24,128]{1,0:T(8,128)S(1)}, u32[]{:S(2)}, u32[]{:S(2)}) collective-permute-start(f32[24,128]{1,0:T(8,128)S(1)} %get-tuple-element.40), channel_id=1, source_target_pairs={{0,2},{1,3},{2,0},{3,1},{4,6},{5,7},{6,4},{7,5},{8,10},{9,11},{10,... | collective-permute-start | bytes 36872 | tf_op jit(solution)/shard_map/ppermute | solution.py:733
  37.9 0.0 collective-permute-start.4
  37.9 0.0 collective-permute-done.6
  37.9 1.7 %collective-permute-done.5 = f32[24,128]{1,0:T(8,128)S(1)} collective-permute-done((f32[24,128]{1,0:T(8,128)S(1)}, f32[24,128]{1,0:T(8,128)S(1)}, u32[]{:S(2)}, u32[]{:S(2)}) %collective-permute-start.5) | collective-permute-done | bytes 12320 | tf_op jit(solution)/shard_map/ppermute | solution.py:733
  39.6 0.0 collective-permute-done.4
  39.6 2.7 %collective-permute-start.9 = (f32[24,128]{1,0:T(8,128)S(1)}, f32[24,128]{1,0:T(8,128)S(1)}, u32[]{:S(2)}, u32[]{:S(2)}) collective-permute-start(f32[24,128]{1,0:T(8,128)S(1)} %add_add_fusion.1), channel_id=1, source_target_pairs={{0,12},{1,13},{2,14},{3,15},{4,8},{5,9},{6,10},{7,11},{8,4},{9,5},... | collective-permute-start | bytes 36872 | tf_op jit(solution)/shard_map/ppermute | solution.py:733
  42.3 0.4 collective-permute-start.8
  42.7 1.3 %collective-permute-start.7 = (f32[24,128]{1,0:T(8,128)S(1)}, f32[24,128]{1,0:T(8,128)S(1)}, u32[]{:S(2)}, u32[]{:S(2)}) collective-permute-start(f32[24,128]{1,0:T(8,128)S(1)} %add_add_fusion.1), channel_id=1, source_target_pairs={{0,4},{1,5},{2,6},{3,7},{4,0},{5,1},{6,2},{7,3},{8,12},{9,13},{10,... | collective-permute-start | bytes 36872 | tf_op jit(solution)/shard_map/ppermute | solution.py:733
  44.1 1.1 %collective-permute-done.9 = f32[24,128]{1,0:T(8,128)S(1)} collective-permute-done((f32[24,128]{1,0:T(8,128)S(1)}, f32[24,128]{1,0:T(8,128)S(1)}, u32[]{:S(2)}, u32[]{:S(2)}) %collective-permute-start.9) | collective-permute-done | bytes 12320 | tf_op jit(solution)/shard_map/ppermute | solution.py:733
  45.2 1.8 %collective-permute-done.8 = f32[24,128]{1,0:T(8,128)S(1)} collective-permute-done((f32[24,128]{1,0:T(8,128)S(1)}, f32[24,128]{1,0:T(8,128)S(1)}, u32[]{:S(2)}, u32[]{:S(2)}) %collective-permute-start.8) | collective-permute-done | bytes 12320 | tf_op jit(solution)/shard_map/ppermute | solution.py:733
  47.0 0.0 collective-permute-done.7
  47.0 2.4 %last.1 = (f32[8,8,4096]{2,1,0:T(8,128)}, f32[8,8,4096]{2,1,0:T(8,128)}) custom-call(f32[24,128]{1,0:T(8,128)S(1)} %add_add_fusion.moments_ref, f32[10,8,4224]{2,1,0:T(8,128)S(1)} %get-tuple-element.29.m_ref, f32[10,8,4224]{2,1,0:T(8,128)S(1)} %get-tuple-element.24.d_ref, f32[10,8,4224]{2,1,0:T(8,128)S(1)} %get-tuple-element.31.g_in, ...), custom_call_target="tpu_custom_call" | custom-call | tf_op jit(solution)/shard_map/last/pallas_call | solution.py:737
  (2 shorter events, 0.0 us)
Async XLA Ops:
  1.8 6.5 %collective-permute-start = (f32[8,16384]{1,0:T(8,128)S(1)}, f32[8,16384]{1,0:T(8,128)S(1)}, u32[]{:S(2)}, u32[]{:S(2)}) collective-permute-start(f32[8,16384]{1,0:T(8,128)S(1)} %pack.1), channel_id=1, source_target_pairs={{1,0},{2,1},{3,2},{4,3},{5,4},{6,5},{7,6},{8,7},{9,8},{10,9},{11,1... | collective-permute-start | bytes 1572872 | tf_op jit(solution)/shard_map/ppermute | solution.py:688
  7.0 18.9 %collective-permute-start.1 = (f32[8,20992]{1,0:T(8,128)S(1)}, f32[8,20992]{1,0:T(8,128)S(1)}, u32[]{:S(2)}, u32[]{:S(2)}) collective-permute-start(f32[8,20992]{1,0:T(8,128)S(1)} %get-tuple-element.38), channel_id=1, source_target_pairs={{1,0},{2,1},{3,2},{4,3},{5,4},{6,5},{7,6},{8,7},{9,8},{10,9},{11,1... | collective-permute-start | bytes 2015240 | tf_op jit(solution)/shard_map/ppermute | solution.py:688
  9.3 16.5 %collective-permute-start.3 = (f32[8,20480]{1,0:T(8,128)S(1)}, f32[8,20480]{1,0:T(8,128)S(1)}, u32[]{:S(2)}, u32[]{:S(2)}) collective-permute-start(f32[8,20480]{1,0:T(8,128)S(1)} %get-tuple-element.30.down_ref), channel_id=1, source_target_pairs={{0,1},{1,2},{2,3},{3,4},{4,5},{5,6},{6,7},{7,8},{8,9},{9,10},{10,1... | collective-permute-start | bytes 1966088 | tf_op jit(solution)/shard_map/ppermute | solution.py:691
  16.6 9.2 %collective-permute-start.2 = (f32[8,4096]{1,0:T(8,128)S(1)}, f32[8,4096]{1,0:T(8,128)S(1)}, u32[]{:S(2)}, u32[]{:S(2)}) collective-permute-start(f32[8,4096]{1,0:T(8,128)S(1)} %get-tuple-element.39), channel_id=1, source_target_pairs={{0,1},{1,2},{2,3},{3,4},{4,5},{5,6},{6,7},{7,8},{8,9},{9,10},{10,1... | collective-permute-start | bytes 393224 | tf_op jit(solution)/shard_map/ppermute | solution.py:691
  31.0 7.0 %collective-permute-start.6 = (f32[24,128]{1,0:T(8,128)S(1)}, f32[24,128]{1,0:T(8,128)S(1)}, u32[]{:S(2)}, u32[]{:S(2)}) collective-permute-start(f32[24,128]{1,0:T(8,128)S(1)} %get-tuple-element.40), channel_id=1, source_target_pairs={{0,3},{1,2},{2,1},{3,0},{4,7},{5,6},{6,5},{7,4},{8,11},{9,10},{10,... | collective-permute-start | bytes 36872 | tf_op jit(solution)/shard_map/ppermute | solution.py:733
  33.8 5.8 %collective-permute-start.5 = (f32[24,128]{1,0:T(8,128)S(1)}, f32[24,128]{1,0:T(8,128)S(1)}, u32[]{:S(2)}, u32[]{:S(2)}) collective-permute-start(f32[24,128]{1,0:T(8,128)S(1)} %get-tuple-element.40), channel_id=1, source_target_pairs={{0,2},{1,3},{2,0},{3,1},{4,6},{5,7},{6,4},{7,5},{8,10},{9,11},{10,... | collective-permute-start | bytes 36872 | tf_op jit(solution)/shard_map/ppermute | solution.py:733
  37.9 1.7 %collective-permute-start.4 = (f32[24,128]{1,0:T(8,128)S(1)}, f32[24,128]{1,0:T(8,128)S(1)}, u32[]{:S(2)}, u32[]{:S(2)}) collective-permute-start(f32[24,128]{1,0:T(8,128)S(1)} %get-tuple-element.40), channel_id=1, source_target_pairs={{0,1},{1,0},{2,3},{3,2},{4,5},{5,4},{6,7},{7,6},{8,9},{9,8},{10,11... | collective-permute-start | bytes 36872 | tf_op jit(solution)/shard_map/ppermute | solution.py:733
  39.6 5.6 %collective-permute-start.9 = (f32[24,128]{1,0:T(8,128)S(1)}, f32[24,128]{1,0:T(8,128)S(1)}, u32[]{:S(2)}, u32[]{:S(2)}) collective-permute-start(f32[24,128]{1,0:T(8,128)S(1)} %add_add_fusion.1), channel_id=1, source_target_pairs={{0,12},{1,13},{2,14},{3,15},{4,8},{5,9},{6,10},{7,11},{8,4},{9,5},... | collective-permute-start | bytes 36872 | tf_op jit(solution)/shard_map/ppermute | solution.py:733
  42.3 4.7 %collective-permute-start.8 = (f32[24,128]{1,0:T(8,128)S(1)}, f32[24,128]{1,0:T(8,128)S(1)}, u32[]{:S(2)}, u32[]{:S(2)}) collective-permute-start(f32[24,128]{1,0:T(8,128)S(1)} %add_add_fusion.1), channel_id=1, source_target_pairs={{0,8},{1,9},{2,10},{3,11},{4,12},{5,13},{6,14},{7,15},{8,0},{9,1},... | collective-permute-start | bytes 36872 | tf_op jit(solution)/shard_map/ppermute | solution.py:733
  42.7 4.3 %collective-permute-start.7 = (f32[24,128]{1,0:T(8,128)S(1)}, f32[24,128]{1,0:T(8,128)S(1)}, u32[]{:S(2)}, u32[]{:S(2)}) collective-permute-start(f32[24,128]{1,0:T(8,128)S(1)} %add_add_fusion.1), channel_id=1, source_target_pairs={{0,4},{1,5},{2,6},{3,7},{4,0},{5,1},{6,2},{7,3},{8,12},{9,13},{10,... | collective-permute-start | bytes 36872 | tf_op jit(solution)/shard_map/ppermute | solution.py:733

commit v6 on v5

--- a/solution.py
+++ b/solution.py
@@ -145,7 +145,18 @@
 
 
 def at_chunk(c):
-    return pl.multiple_of(c * CHUNK, CHUNK)
+    return multiple(c * CHUNK)
+
+
+def multiple(lane):
+    return lane if isinstance(lane, int) else pl.multiple_of(lane, CHUNK)
+
+
+def sweep(x, body):
+    if chunks(x) == 1:
+        body(0, 0)
+    else:
+        lax.fori_loop(0, chunks(x), body, 0)
 
 
 class Own:
@@ -174,7 +185,7 @@
 
 
 def put(ref, slot, x, x0, value):
-    ref[:, pl.ds(pl.multiple_of(x0 + slot * x, CHUNK), CHUNK)] = value
+    ref[:, pl.ds(multiple(x0 + slot * x), CHUNK)] = value
 
 
 def pack_kernel(n, x, si_hbm, sc_hbm, model_hbm, dir_hbm, up_ref, sems):
@@ -226,7 +237,7 @@
             bd_ref[i + 1, :, own.here] = value
         return 0
 
-    lax.fori_loop(0, chunks(x), first, 0)
+    sweep(x, first)
     carry[...] = jnp.zeros(carry.shape, f32)
 
     def second(c, _):
@@ -239,7 +250,7 @@
         put(up_ref, B2D0, x, x0, own.applied(bd_ref, 0, 0, 2)[0])
         return 0
 
-    lax.fori_loop(0, chunks(x), second, 0)
+    sweep(x, second)
     carry[...] = jnp.zeros(carry.shape, f32)
 
     def third(c, _):
@@ -247,7 +258,7 @@
         put(up_ref, B2G0, x, x0, Own(n, x0, si_ref, sc_ref, mask_ref, carry).applied(bg_ref, 0, 0, 0)[0])
         return 0
 
-    lax.fori_loop(0, chunks(x), third, 0)
+    sweep(x, third)
     for copy in copies[6:]:
         copy.wait()
     slope_ref[...] = si_ref[n, :, lanes]
@@ -279,7 +290,7 @@
         put(down_ref, WD1, x, x0, eps_ref[1, :, here])
         return 0
 
-    lax.fori_loop(0, chunks(x), first, 0)
+    sweep(x, first)
     carry[...] = jnp.zeros(carry.shape, f32)
 
     def second(c, _):
@@ -288,7 +299,7 @@
         put(down_ref, BG1, x, x0, own.applied(g_ref, n - 1, n - 1, 0)[n - 1])
         return 0
 
-    lax.fori_loop(0, chunks(x), second, 0)
+    sweep(x, second)
 
 
 def local_kernel(
@@ -311,7 +322,7 @@
         bd_ref[n, :, here] = row_of(down_ref, BD1, x, x0)
         return 0
 
-    lax.fori_loop(0, chunks(x), first, 0)
+    sweep(x, first)
     carry[...] = jnp.zeros(carry.shape, f32)
 
     def second(c, _):
@@ -323,7 +334,7 @@
             b2d_ref[i + 1, :, own.here] = value
         return 0
 
-    lax.fori_loop(0, chunks(x), second, 0)
+    sweep(x, second)
     carry[...] = jnp.zeros(carry.shape, f32)
 
     def third(c, _):
@@ -333,7 +344,7 @@
             b2g_ref[i + 1, :, own.here] = value
         return 0
 
-    lax.fori_loop(0, chunks(x), third, 0)
+    sweep(x, third)
 
     def fourth(c, _):
         x0 = at_chunk(c)
@@ -341,7 +352,7 @@
         products(n, x0, loads, mask_ref, si_ref, sc_ref, sums_ref, lambda done: done)
         return 0
 
-    lax.fori_loop(0, chunks(x), fourth, 0)
+    sweep(x, fourth)
 
 
 PAIRS = ((0, 0), (0, 1), (1, 1), (1, 2), (2, 2), None, (0, 3), (0, 4), (1, 4), (1, 5), (2, 5), None,
@@ -426,7 +437,7 @@
 
 
 def row_of(ref, slot, x, x0):
-    return ref[:, pl.ds(pl.multiple_of(x0 + slot * x, CHUNK), CHUNK)]
+    return ref[:, pl.ds(multiple(x0 + slot * x), CHUNK)]
 
 
 def boundary(rows, i, slope, here, scale=None):
@@ -501,7 +512,7 @@
         bd_rows.store(n, here, (row_of(up_ref, BD0, x, x0) + eps_in[1, :, here]) * not_last)
         return 0
 
-    lax.fori_loop(0, chunks(x), zeroth, 0)
+    sweep(x, zeroth)
 
     def first(c, _):
         x0 = at_chunk(c)
@@ -524,7 +535,7 @@
         bg_rows.store(-1, here, row_of(down_ref, BG1, x, x0) + to_self(boundary(g_rows, -1, before, here, not_first)))
         return 0
 
-    lax.fori_loop(0, chunks(x), first, 0)
+    sweep(x, first)
     carry[...] = jnp.zeros(carry.shape, f32)
 
     def second(c, _):
@@ -540,24 +551,25 @@
         b2g_rows.store(n, here, (row_of(up_ref, B2G0, x, x0) + own + edge) * not_last)
         return 0
 
-    lax.fori_loop(0, chunks(x), second, 0)
+    sweep(x, second)
 
     def third(c, _):
         loads = [rows.load for rows in (g_rows, bg_rows, b2g_rows, d_rows, bd_rows, b2d_rows)]
         products(n, at_chunk(c), loads, mask_ref, si_ref, sc_ref, sums, lambda done: not done)
         return 0
 
-    lax.fori_loop(0, chunks(x), third, 0)
+    sweep(x, third)
     for k in range(N_MOMENTS):
         moments_ref[pl.ds(k, 1), :] = jnp.sum(sums[k], axis=0, keepdims=True)
     moments_ref[pl.ds(N_MOMENTS, 24 - N_MOMENTS), :] = jnp.zeros((24 - N_MOMENTS, LANES), f32)
 
 
 def add_terms(terms):
-    total = None
-    for term in terms:
-        total = term if total is None else total + term
-    return total
+    terms = list(terms)
+    while len(terms) > 1:
+        pairs = [left + right for left, right in zip(terms[::2], terms[1::2])]
+        terms = pairs + terms[len(pairs) * 2:]
+    return terms[0]
 
 
 def solve(moments):
@@ -583,11 +595,8 @@
         return shifted[which, i + j]
 
     def form(get, u, v):
-        rows = []
-        for (a, i), left in u.items():
-            inner = add_terms(right * get(a, b, i, j) for (b, j), right in v.items())
-            rows.append(left * inner)
-        return add_terms(rows)
+        return add_terms(
+            left * add_terms(right * get(a, b, i, j) for (b, j), right in v.items()) for (a, i), left in u.items())
 
     def axpy(scale, u, v):
         out = dict(v)
@@ -628,17 +637,12 @@
     keys = ((0, 0), (0, 1), (0, 2), (1, 1), (1, 2))
     copies = []
     for i in range(n):
-        def step(c, _):
-            x0 = pl.multiple_of(c * LANES, LANES)
-            here = pl.ds(x0, LANES)
+        for c in range(x // LANES):
+            here = pl.ds(c * LANES, LANES)
             values = {key: vector.load(i, here) for key, vector in zip(keys, rows)}
             values[1, 0] = d_ref[i + 1, :, here]
-            mo_ref[i, :, here] = m_ref[i + 1, :, here] + add_terms(
-                model[key] * value for key, value in values.items())
+            mo_ref[i, :, here] = m_ref[i + 1, :, here] + add_terms(model[key] * value for key, value in values.items())
             do_ref[i, :, here] = add_terms(direction[key] * value for key, value in values.items())
-            return 0
-
-        lax.fori_loop(0, x // LANES, step, 0, unroll=4)
         for k, (src, dst) in enumerate(((mo_ref, model_hbm), (do_ref, dir_hbm))):
             copy = pltpu.make_async_copy(src.at[i], dst.at[i], sems.at[2 * i + k])
             copy.start()

time: 49.8 us -> 49.2 us (0.988)
  Pallas kernels: 20.7 us -> 20.1 us
    pallas_call x1, Pallas kernels: 2.36 us -> 1.81 us  [on_device(): pl.pallas_call(functools.partial(last_kernel, n, x), out_shape=[jax.Shape...]
  transfers between devices with their start and end apart: 10 -> 10, of which waited for: 3 -> 3; matrix products, arithmetic and copies ran while one was open for 0% -> 0% of each run, Pallas kernels for 24% -> 25%
where the time goes in v6:
time: 49.2 us; the launch traced here: 49 us
  starting transfers between devices  23.3 us (47%)
  Pallas kernels  20.1 us (41%)
  waiting for transfers between devices  4.63 us (9%)
  between operations  0.9 us (2%)
    ppermute x6, starting transfers between devices, on_device(): lax.ppermute(moments, 'inline', [(i, i ^ k * reach) for i in range(peers)])  11.4 us
    ppermute x2, starting transfers between devices, to_after(): return lax.ppermute(value, 'inline', [(i, i + 1) for i in range(peers - 1)])  9.34 us
    pallas_call x1, Pallas kernels, on_device(): call(local_kernel, [wide, wide, wide, wide, wide, kept((N_MOMENTS, NT, LA...  7.16 us
    pallas_call x1, Pallas kernels, on_device(): call(join_kernel, [ends(LOW[k] + HIGH[k]) for k in (0, 1, 2, 4, 5)] + [ja...  5.08 us
    ppermute x6, waiting for transfers between devices, on_device(): lax.ppermute(moments, 'inline', [(i, i ^ k * reach) for i in range(peers)])  4.62 us
    pallas_call x1, Pallas kernels, on_device(): call(first_kernel, [kept((n, NT, x)), kept((n, x), jnp.int32), kept((n +...  3.9 us
    ppermute x2, starting transfers between devices, to_before(): return lax.ppermute(value, 'inline', [(i, i - 1) for i in range(1, peers)])  2.58 us
    pallas_call x1, Pallas kernels, on_device(): pl.pallas_call(functools.partial(last_kernel, n, x), out_shape=[jax.Shape...  1.81 us
  transfers between devices with their start and end apart: 10, of which 3 were waited for; matrix products, arithmetic and copies ran while one was open for 0% of the time, Pallas kernels for 25%

profile of v6, /device:TPU:0, one launch (start us, length us, event | category | flops | bytes accessed | tf_op | source)
XLA Modules:
  0.0 49.0 jit_solution(12902555781499292391)
XLA Ops:
  0.6 1.1 %pack.1 = f32[8,16384]{1,0:T(8,128)S(1)} custom-call(f32[8,8,4096]{2,1,0:T(8,128)} %si_hbm.3, f32[8,8,4096]{2,1,0:T(8,128)} %sc_hbm.3, f32[8,8,4096]{2,1,0:T(8,128)} %model_hbm.3, f32[8,8,4096]{2,1,0:T(8,128)} %dir_hbm.3), custom_call_target="tpu_custom_call" | custom-call | tf_op jit(solution)/shard_map/pack/pallas_call | solution.py:697
  1.8 1.3 %collective-permute-start = (f32[8,16384]{1,0:T(8,128)S(1)}, f32[8,16384]{1,0:T(8,128)S(1)}, u32[]{:S(2)}, u32[]{:S(2)}) collective-permute-start(f32[8,16384]{1,0:T(8,128)S(1)} %pack.1), channel_id=1, source_target_pairs={{1,0},{2,1},{3,2},{4,3},{5,4},{6,5},{7,6},{8,7},{9,8},{10,9},{11,1... | collective-permute-start | bytes 1572872 | tf_op jit(solution)/shard_map/ppermute | solution.py:692
  3.1 3.9 %first.1 = (f32[8,8,4096]{2,1,0:T(8,128)S(1)}, s32[8,4096]{1,0:T(8,128)S(1)}, f32[10,8,4096]{2,1,0:T(8,128)S(1)}, f32[8,8,4096]{2,1,0:T(8,128)S(1)}, f32[10,8,42...) custom-call(f32[8,8,4096]{2,1,0:T(8,128)} %data_hbm.1, ...), custom_call_target="tpu_custom_call" | custom-call | tf_op jit(solution)/shard_map/first/pallas_call | solution.py:702
  7.0 1.3 %collective-permute-start.1 = (f32[8,20992]{1,0:T(8,128)S(1)}, f32[8,20992]{1,0:T(8,128)S(1)}, u32[]{:S(2)}, u32[]{:S(2)}) collective-permute-start(f32[8,20992]{1,0:T(8,128)S(1)} %get-tuple-element.38), channel_id=1, source_target_pairs={{1,0},{2,1},{3,2},{4,3},{5,4},{6,5},{7,6},{8,7},{9,8},{10,9},{11,1... | collective-permute-start | bytes 2015240 | tf_op jit(solution)/shard_map/ppermute | solution.py:692
  8.3 0.0 collective-permute-done.up_first
  8.3 1.0 %down.1 = (f32[8,20480]{1,0:T(8,128)S(1)}, f32[2,8,4224]{2,1,0:T(8,128)S(1)}) custom-call(f32[8,8,4096]{2,1,0:T(8,128)S(1)} %get-tuple-element.28.data_ref, s32[8,4096]{1,0:T(8,128)S(1)} %get-tuple-element.27.mask_ref, f32[10,8,4096]{2,1,0:T(8,128)S(1)} %get-tuple-element.25.si_ref, f32[8,8,4096]{2,1,0:T(8,128)S(1)} %get-tuple-element.26.sc_ref, ...), custom_call_target="tpu_custom_call" | custom-call | tf_op jit(solution)/shard_map/down/pallas_call | solution.py:714
  9.3 7.3 %collective-permute-start.3 = (f32[8,20480]{1,0:T(8,128)S(1)}, f32[8,20480]{1,0:T(8,128)S(1)}, u32[]{:S(2)}, u32[]{:S(2)}) collective-permute-start(f32[8,20480]{1,0:T(8,128)S(1)} %get-tuple-element.30.down_ref), channel_id=1, source_target_pairs={{0,1},{1,2},{2,3},{3,4},{4,5},{5,6},{6,7},{7,8},{8,9},{9,10},{10,1... | collective-permute-start | bytes 1966088 | tf_op jit(solution)/shard_map/ppermute | solution.py:695
  16.6 2.1 %collective-permute-start.2 = (f32[8,4096]{1,0:T(8,128)S(1)}, f32[8,4096]{1,0:T(8,128)S(1)}, u32[]{:S(2)}, u32[]{:S(2)}) collective-permute-start(f32[8,4096]{1,0:T(8,128)S(1)} %get-tuple-element.39), channel_id=1, source_target_pairs={{0,1},{1,2},{2,3},{3,4},{4,5},{5,6},{6,7},{7,8},{8,9},{9,10},{10,1... | collective-permute-start | bytes 393224 | tf_op jit(solution)/shard_map/ppermute | solution.py:695
  18.7 7.2 %local.1 = (f32[10,8,4224]{2,1,0:T(8,128)S(1)}, f32[10,8,4224]{2,1,0:T(8,128)S(1)}, f32[10,8,4224]{2,1,0:T(8,128)S(1)}, f32[10,8,4224]{2,1,0:T(8,128)S(1)}, f32[...) custom-call(f32[8,8,4096]{2,1,0:T(8,128)S(1)} %get-tuple-element.28.data_ref, ...), custom_call_target="tpu_custom_call" | custom-call | tf_op jit(solution)/shard_map/local/pallas_call | solution.py:720
  25.8 0.0 collective-permute-done.2.slope_ref
  25.9 0.0 collective-permute-done.1.up_ref
  25.9 0.0 collective-permute-done.3.down_ref
  25.9 5.1 %join.1 = (f32[1,8,4224]{2,1,0:T(8,128)S(1)}, f32[3,8,4224]{2,1,0:T(8,128)S(1)}, f32[5,8,4224]{2,1,0:T(8,128)S(1)}, f32[1,8,4224]{2,1,0:T(8,128)S(1)}, f32[3,8,4224]{2,1,0:T(8,128)S(1)}, /*index=5*/f32[24,128]{1,0:T(8,128)S(1)}) custom-call(f32[10,8,4224]{2,1,0:T(8,128)S(1)} %get-tuple-element.24.d_ref, f32[10,8,4096]{2,1,0:T(8,128)S(1)} %get-tuple-element.25.si_ref, ...), custom_call_target="tpu_custom_call" | custom-call | tf_op jit(solution)/shard_map/join/pallas_call | solution.py:726
  31.0 2.8 %collective-permute-start.6 = (f32[24,128]{1,0:T(8,128)S(1)}, f32[24,128]{1,0:T(8,128)S(1)}, u32[]{:S(2)}, u32[]{:S(2)}) collective-permute-start(f32[24,128]{1,0:T(8,128)S(1)} %get-tuple-element.40), channel_id=1, source_target_pairs={{0,3},{1,2},{2,1},{3,0},{4,7},{5,6},{6,5},{7,4},{8,11},{9,10},{10,... | collective-permute-start | bytes 36872 | tf_op jit(solution)/shard_map/ppermute | solution.py:737
  33.8 4.1 %collective-permute-start.5 = (f32[24,128]{1,0:T(8,128)S(1)}, f32[24,128]{1,0:T(8,128)S(1)}, u32[]{:S(2)}, u32[]{:S(2)}) collective-permute-start(f32[24,128]{1,0:T(8,128)S(1)} %get-tuple-element.40), channel_id=1, source_target_pairs={{0,2},{1,3},{2,0},{3,1},{4,6},{5,7},{6,4},{7,5},{8,10},{9,11},{10,... | collective-permute-start | bytes 36872 | tf_op jit(solution)/shard_map/ppermute | solution.py:737
  37.9 0.0 collective-permute-start.4
  37.9 0.0 collective-permute-done.6
  37.9 1.7 %collective-permute-done.5 = f32[24,128]{1,0:T(8,128)S(1)} collective-permute-done((f32[24,128]{1,0:T(8,128)S(1)}, f32[24,128]{1,0:T(8,128)S(1)}, u32[]{:S(2)}, u32[]{:S(2)}) %collective-permute-start.5) | collective-permute-done | bytes 12320 | tf_op jit(solution)/shard_map/ppermute | solution.py:737
  39.6 0.0 collective-permute-done.4
  39.6 2.7 %collective-permute-start.9 = (f32[24,128]{1,0:T(8,128)S(1)}, f32[24,128]{1,0:T(8,128)S(1)}, u32[]{:S(2)}, u32[]{:S(2)}) collective-permute-start(f32[24,128]{1,0:T(8,128)S(1)} %add_add_fusion.1), channel_id=1, source_target_pairs={{0,12},{1,13},{2,14},{3,15},{4,8},{5,9},{6,10},{7,11},{8,4},{9,5},... | collective-permute-start | bytes 36872 | tf_op jit(solution)/shard_map/ppermute | solution.py:737
  42.3 0.4 collective-permute-start.8
  42.7 1.3 %collective-permute-start.7 = (f32[24,128]{1,0:T(8,128)S(1)}, f32[24,128]{1,0:T(8,128)S(1)}, u32[]{:S(2)}, u32[]{:S(2)}) collective-permute-start(f32[24,128]{1,0:T(8,128)S(1)} %add_add_fusion.1), channel_id=1, source_target_pairs={{0,4},{1,5},{2,6},{3,7},{4,0},{5,1},{6,2},{7,3},{8,12},{9,13},{10,... | collective-permute-start | bytes 36872 | tf_op jit(solution)/shard_map/ppermute | solution.py:737
  44.1 1.1 %collective-permute-done.9 = f32[24,128]{1,0:T(8,128)S(1)} collective-permute-done((f32[24,128]{1,0:T(8,128)S(1)}, f32[24,128]{1,0:T(8,128)S(1)}, u32[]{:S(2)}, u32[]{:S(2)}) %collective-permute-start.9) | collective-permute-done | bytes 12320 | tf_op jit(solution)/shard_map/ppermute | solution.py:737
  45.2 1.8 %collective-permute-done.8 = f32[24,128]{1,0:T(8,128)S(1)} collective-permute-done((f32[24,128]{1,0:T(8,128)S(1)}, f32[24,128]{1,0:T(8,128)S(1)}, u32[]{:S(2)}, u32[]{:S(2)}) %collective-permute-start.8) | collective-permute-done | bytes 12320 | tf_op jit(solution)/shard_map/ppermute | solution.py:737
  47.0 0.0 collective-permute-done.7
  47.0 1.8 %last.1 = (f32[8,8,4096]{2,1,0:T(8,128)}, f32[8,8,4096]{2,1,0:T(8,128)}) custom-call(f32[24,128]{1,0:T(8,128)S(1)} %add_add_fusion.moments_ref, f32[10,8,4224]{2,1,0:T(8,128)S(1)} %get-tuple-element.29.m_ref, f32[10,8,4224]{2,1,0:T(8,128)S(1)} %get-tuple-element.24.d_ref, f32[10,8,4224]{2,1,0:T(8,128)S(1)} %get-tuple-element.31.g_in, ...), custom_call_target="tpu_custom_call" | custom-call | tf_op jit(solution)/shard_map/last/pallas_call | solution.py:741
  (2 shorter events, 0.0 us)
Async XLA Ops:
  1.8 6.5 %collective-permute-start = (f32[8,16384]{1,0:T(8,128)S(1)}, f32[8,16384]{1,0:T(8,128)S(1)}, u32[]{:S(2)}, u32[]{:S(2)}) collective-permute-start(f32[8,16384]{1,0:T(8,128)S(1)} %pack.1), channel_id=1, source_target_pairs={{1,0},{2,1},{3,2},{4,3},{5,4},{6,5},{7,6},{8,7},{9,8},{10,9},{11,1... | collective-permute-start | bytes 1572872 | tf_op jit(solution)/shard_map/ppermute | solution.py:692
  7.0 18.9 %collective-permute-start.1 = (f32[8,20992]{1,0:T(8,128)S(1)}, f32[8,20992]{1,0:T(8,128)S(1)}, u32[]{:S(2)}, u32[]{:S(2)}) collective-permute-start(f32[8,20992]{1,0:T(8,128)S(1)} %get-tuple-element.38), channel_id=1, source_target_pairs={{1,0},{2,1},{3,2},{4,3},{5,4},{6,5},{7,6},{8,7},{9,8},{10,9},{11,1... | collective-permute-start | bytes 2015240 | tf_op jit(solution)/shard_map/ppermute | solution.py:692
  9.3 16.5 %collective-permute-start.3 = (f32[8,20480]{1,0:T(8,128)S(1)}, f32[8,20480]{1,0:T(8,128)S(1)}, u32[]{:S(2)}, u32[]{:S(2)}) collective-permute-start(f32[8,20480]{1,0:T(8,128)S(1)} %get-tuple-element.30.down_ref), channel_id=1, source_target_pairs={{0,1},{1,2},{2,3},{3,4},{4,5},{5,6},{6,7},{7,8},{8,9},{9,10},{10,1... | collective-permute-start | bytes 1966088 | tf_op jit(solution)/shard_map/ppermute | solution.py:695
  16.6 9.2 %collective-permute-start.2 = (f32[8,4096]{1,0:T(8,128)S(1)}, f32[8,4096]{1,0:T(8,128)S(1)}, u32[]{:S(2)}, u32[]{:S(2)}) collective-permute-start(f32[8,4096]{1,0:T(8,128)S(1)} %get-tuple-element.39), channel_id=1, source_target_pairs={{0,1},{1,2},{2,3},{3,4},{4,5},{5,6},{6,7},{7,8},{8,9},{9,10},{10,1... | collective-permute-start | bytes 393224 | tf_op jit(solution)/shard_map/ppermute | solution.py:695
  31.0 7.0 %collective-permute-start.6 = (f32[24,128]{1,0:T(8,128)S(1)}, f32[24,128]{1,0:T(8,128)S(1)}, u32[]{:S(2)}, u32[]{:S(2)}) collective-permute-start(f32[24,128]{1,0:T(8,128)S(1)} %get-tuple-element.40), channel_id=1, source_target_pairs={{0,3},{1,2},{2,1},{3,0},{4,7},{5,6},{6,5},{7,4},{8,11},{9,10},{10,... | collective-permute-start | bytes 36872 | tf_op jit(solution)/shard_map/ppermute | solution.py:737
  33.8 5.8 %collective-permute-start.5 = (f32[24,128]{1,0:T(8,128)S(1)}, f32[24,128]{1,0:T(8,128)S(1)}, u32[]{:S(2)}, u32[]{:S(2)}) collective-permute-start(f32[24,128]{1,0:T(8,128)S(1)} %get-tuple-element.40), channel_id=1, source_target_pairs={{0,2},{1,3},{2,0},{3,1},{4,6},{5,7},{6,4},{7,5},{8,10},{9,11},{10,... | collective-permute-start | bytes 36872 | tf_op jit(solution)/shard_map/ppermute | solution.py:737
  37.9 1.7 %collective-permute-start.4 = (f32[24,128]{1,0:T(8,128)S(1)}, f32[24,128]{1,0:T(8,128)S(1)}, u32[]{:S(2)}, u32[]{:S(2)}) collective-permute-start(f32[24,128]{1,0:T(8,128)S(1)} %get-tuple-element.40), channel_id=1, source_target_pairs={{0,1},{1,0},{2,3},{3,2},{4,5},{5,4},{6,7},{7,6},{8,9},{9,8},{10,11... | collective-permute-start | bytes 36872 | tf_op jit(solution)/shard_map/ppermute | solution.py:737
  39.6 5.6 %collective-permute-start.9 = (f32[24,128]{1,0:T(8,128)S(1)}, f32[24,128]{1,0:T(8,128)S(1)}, u32[]{:S(2)}, u32[]{:S(2)}) collective-permute-start(f32[24,128]{1,0:T(8,128)S(1)} %add_add_fusion.1), channel_id=1, source_target_pairs={{0,12},{1,13},{2,14},{3,15},{4,8},{5,9},{6,10},{7,11},{8,4},{9,5},... | collective-permute-start | bytes 36872 | tf_op jit(solution)/shard_map/ppermute | solution.py:737
  42.3 4.7 %collective-permute-start.8 = (f32[24,128]{1,0:T(8,128)S(1)}, f32[24,128]{1,0:T(8,128)S(1)}, u32[]{:S(2)}, u32[]{:S(2)}) collective-permute-start(f32[24,128]{1,0:T(8,128)S(1)} %add_add_fusion.1), channel_id=1, source_target_pairs={{0,8},{1,9},{2,10},{3,11},{4,12},{5,13},{6,14},{7,15},{8,0},{9,1},... | collective-permute-start | bytes 36872 | tf_op jit(solution)/shard_map/ppermute | solution.py:737
  42.7 4.3 %collective-permute-start.7 = (f32[24,128]{1,0:T(8,128)S(1)}, f32[24,128]{1,0:T(8,128)S(1)}, u32[]{:S(2)}, u32[]{:S(2)}) collective-permute-start(f32[24,128]{1,0:T(8,128)S(1)} %add_add_fusion.1), channel_id=1, source_target_pairs={{0,4},{1,5},{2,6},{3,7},{4,0},{5,1},{6,2},{7,3},{8,12},{9,13},{10,... | collective-permute-start | bytes 36872 | tf_op jit(solution)/shard_map/ppermute | solution.py:737

commit v7 on v6

--- a/solution.py
+++ b/solution.py
@@ -486,7 +486,7 @@
     d_ref, si_ref, sc_ref, mask_ref, g_in, bg_in, b2g_in, bd_in, b2d_in, sums_in, eps_in,
     up_first, up_ref, slope_ref, down_ref,
     g_out, bg_out, b2g_out, bd_out, b2d_out, moments_ref,
-    eps_ref, mask_up, ghosts, carry, sums,
+    eps_ref, mask_up, ghosts, carry, sums, rows_ref,
 ):
     not_first, not_last = place_flags()
     clear_pads(x, (eps_ref, ghosts, g_out, bg_out, b2g_out, bd_out, b2d_out))
@@ -560,8 +560,13 @@
 
     sweep(x, third)
     for k in range(N_MOMENTS):
-        moments_ref[pl.ds(k, 1), :] = jnp.sum(sums[k], axis=0, keepdims=True)
-    moments_ref[pl.ds(N_MOMENTS, 24 - N_MOMENTS), :] = jnp.zeros((24 - N_MOMENTS, LANES), f32)
+        rows_ref[pl.ds(k, 1), :] = jnp.sum(sums[k], axis=0, keepdims=True)
+    rows_ref[pl.ds(N_MOMENTS, 24 - N_MOMENTS), :] = jnp.zeros((24 - N_MOMENTS, LANES), f32)
+    rows = rows_ref[...]
+    rows = rows + pltpu.roll(rows, LANES // 2, 1)
+    rows = rows + pltpu.roll(rows, LANES // 4, 1)
+    group = lax.broadcasted_iota(jnp.int32, (8, LANES), 1) // (LANES // 4)
+    moments_ref[...] = jnp.where(group == 0, rows[:8], jnp.where(group == 1, rows[8:16], rows[16:]))
 
 
 def add_terms(terms):
@@ -625,8 +630,10 @@
     n, x, moments_ref, m_ref, d_ref, g_in, bg_in, b2g_in, bd_in, b2d_in, g_end, bg_end, b2g_end, bd_end, b2d_end,
     model_hbm, dir_hbm, mo_ref, do_ref, sems,
 ):
+    group = lax.broadcasted_iota(jnp.int32, (1, LANES), 1) // (LANES // 4)
     moments = [
-        jnp.broadcast_to(jnp.sum(moments_ref[pl.ds(k, 1), :], axis=1, keepdims=True), (NT, LANES))
+        jnp.broadcast_to(
+            jnp.sum(jnp.where(group == k // 8, moments_ref[pl.ds(k % 8, 1), :], 0.0), axis=1, keepdims=True), (NT, LANES))
         for k in range(N_MOMENTS)
     ]
     model, direction = solve(moments)
@@ -725,9 +732,9 @@
 
     out = call(
         join_kernel,
-        [ends(LOW[k] + HIGH[k]) for k in (0, 1, 2, 4, 5)] + [jax.ShapeDtypeStruct((24, LANES), f32)], [vmem] * 15,
+        [ends(LOW[k] + HIGH[k]) for k in (0, 1, 2, 4, 5)] + [jax.ShapeDtypeStruct((8, LANES), f32)], [vmem] * 15,
         [pltpu.VMEM((2, NT, x + LANES), f32), pltpu.VMEM((1, x), f32), pltpu.VMEM((12, NT, x + LANES), f32), carry(8),
-         pltpu.VMEM((N_MOMENTS, NT, LANES), f32)], "join",
+         pltpu.VMEM((N_MOMENTS, NT, LANES), f32), pltpu.VMEM((24, LANES), f32)], "join",
     )(d, si, sc, mask, g, bg, b2g, bd, b2d, sums, eps, up_first, up, slope, received)
     moments = out[5]
 

time: 49.2 us -> 49.3 us (level)
  Pallas kernels: 20.1 us -> 21.2 us
  starting transfers between devices: 23.3 us -> 22.8 us
    ppermute x6, starting transfers between devices: 11.4 us -> 10.9 us  [on_device(): lax.ppermute(moments, 'inline', [(i, i ^ k * reach) for i in range(peers)])]
    pallas_call x1, Pallas kernels: 7.16 us -> 7.66 us  [on_device(): call(local_kernel, [wide, wide, wide, wide, wide, kept((N_MOMENTS, NT, LA...]
  transfers between devices with their start and end apart: 10 -> 10, of which waited for: 3 -> 3; matrix products, arithmetic and copies ran while one was open for 0% -> 0% of each run, Pallas kernels for 25% -> 26%
where the time goes in v7:
time: 49.3 us; the launch traced here: 49.1 us
  starting transfers between devices  22.8 us (46%)
  Pallas kernels  21.2 us (43%)
  waiting for transfers between devices  4.27 us (9%)
  between operations  0.89 us (2%)
    ppermute x6, starting transfers between devices, on_device(): lax.ppermute(moments, 'inline', [(i, i ^ k * reach) for i in range(peers)])  10.9 us
    ppermute x2, starting transfers between devices, to_after(): return lax.ppermute(value, 'inline', [(i, i + 1) for i in range(peers - 1)])  9.26 us
    pallas_call x1, Pallas kernels, on_device(): call(local_kernel, [wide, wide, wide, wide, wide, kept((N_MOMENTS, NT, LA...  7.66 us
    pallas_call x1, Pallas kernels, on_device(): call(join_kernel, [ends(LOW[k] + HIGH[k]) for k in (0, 1, 2, 4, 5)] + [ja...  5.53 us
    ppermute x6, waiting for transfers between devices, on_device(): lax.ppermute(moments, 'inline', [(i, i ^ k * reach) for i in range(peers)])  4.26 us
    pallas_call x1, Pallas kernels, on_device(): call(first_kernel, [kept((n, NT, x)), kept((n, x), jnp.int32), kept((n +...  3.98 us
    ppermute x2, starting transfers between devices, to_before(): return lax.ppermute(value, 'inline', [(i, i - 1) for i in range(1, peers)])  2.58 us
    pallas_call x1, Pallas kernels, on_device(): pl.pallas_call(functools.partial(last_kernel, n, x), out_shape=[jax.Shape...  1.8 us
  transfers between devices with their start and end apart: 10, of which 3 were waited for; matrix products, arithmetic and copies ran while one was open for 0% of the time, Pallas kernels for 26%

profile of v7, /device:TPU:0, one launch (start us, length us, event | category | flops | bytes accessed | tf_op | source)
XLA Modules:
  0.0 49.1 jit_solution(7577941106860446918)
XLA Ops:
  0.6 1.1 %pack.1 = f32[8,16384]{1,0:T(8,128)S(1)} custom-call(f32[8,8,4096]{2,1,0:T(8,128)} %si_hbm.3, f32[8,8,4096]{2,1,0:T(8,128)} %sc_hbm.3, f32[8,8,4096]{2,1,0:T(8,128)} %model_hbm.3, f32[8,8,4096]{2,1,0:T(8,128)} %dir_hbm.3), custom_call_target="tpu_custom_call" | custom-call | tf_op jit(solution)/shard_map/pack/pallas_call | solution.py:704
  1.8 1.3 %collective-permute-start = (f32[8,16384]{1,0:T(8,128)S(1)}, f32[8,16384]{1,0:T(8,128)S(1)}, u32[]{:S(2)}, u32[]{:S(2)}) collective-permute-start(f32[8,16384]{1,0:T(8,128)S(1)} %pack.1), channel_id=1, source_target_pairs={{1,0},{2,1},{3,2},{4,3},{5,4},{6,5},{7,6},{8,7},{9,8},{10,9},{11,1... | collective-permute-start | bytes 1572872 | tf_op jit(solution)/shard_map/ppermute | solution.py:699
  3.1 4.0 %first.1 = (f32[8,8,4096]{2,1,0:T(8,128)S(1)}, s32[8,4096]{1,0:T(8,128)S(1)}, f32[10,8,4096]{2,1,0:T(8,128)S(1)}, f32[8,8,4096]{2,1,0:T(8,128)S(1)}, f32[10,8,42...) custom-call(f32[8,8,4096]{2,1,0:T(8,128)} %data_hbm.1, ...), custom_call_target="tpu_custom_call" | custom-call | tf_op jit(solution)/shard_map/first/pallas_call | solution.py:709
  7.1 1.3 %collective-permute-start.1 = (f32[8,20992]{1,0:T(8,128)S(1)}, f32[8,20992]{1,0:T(8,128)S(1)}, u32[]{:S(2)}, u32[]{:S(2)}) collective-permute-start(f32[8,20992]{1,0:T(8,128)S(1)} %get-tuple-element.38), channel_id=1, source_target_pairs={{1,0},{2,1},{3,2},{4,3},{5,4},{6,5},{7,6},{8,7},{9,8},{10,9},{11,1... | collective-permute-start | bytes 2015240 | tf_op jit(solution)/shard_map/ppermute | solution.py:699
  8.4 0.0 collective-permute-done.up_first
  8.4 1.1 %down.1 = (f32[8,20480]{1,0:T(8,128)S(1)}, f32[2,8,4224]{2,1,0:T(8,128)S(1)}) custom-call(f32[8,8,4096]{2,1,0:T(8,128)S(1)} %get-tuple-element.28.data_ref, s32[8,4096]{1,0:T(8,128)S(1)} %get-tuple-element.27.mask_ref, f32[10,8,4096]{2,1,0:T(8,128)S(1)} %get-tuple-element.25.si_ref, f32[8,8,4096]{2,1,0:T(8,128)S(1)} %get-tuple-element.26.sc_ref, ...), custom_call_target="tpu_custom_call" | custom-call | tf_op jit(solution)/shard_map/down/pallas_call | solution.py:721
  9.4 7.2 %collective-permute-start.3 = (f32[8,20480]{1,0:T(8,128)S(1)}, f32[8,20480]{1,0:T(8,128)S(1)}, u32[]{:S(2)}, u32[]{:S(2)}) collective-permute-start(f32[8,20480]{1,0:T(8,128)S(1)} %get-tuple-element.30.down_ref), channel_id=1, source_target_pairs={{0,1},{1,2},{2,3},{3,4},{4,5},{5,6},{6,7},{7,8},{8,9},{9,10},{10,1... | collective-permute-start | bytes 1966088 | tf_op jit(solution)/shard_map/ppermute | solution.py:702
  16.6 2.1 %collective-permute-start.2 = (f32[8,4096]{1,0:T(8,128)S(1)}, f32[8,4096]{1,0:T(8,128)S(1)}, u32[]{:S(2)}, u32[]{:S(2)}) collective-permute-start(f32[8,4096]{1,0:T(8,128)S(1)} %get-tuple-element.39), channel_id=1, source_target_pairs={{0,1},{1,2},{2,3},{3,4},{4,5},{5,6},{6,7},{7,8},{8,9},{9,10},{10,1... | collective-permute-start | bytes 393224 | tf_op jit(solution)/shard_map/ppermute | solution.py:702
  18.7 7.7 %local.1 = (f32[10,8,4224]{2,1,0:T(8,128)S(1)}, f32[10,8,4224]{2,1,0:T(8,128)S(1)}, f32[10,8,4224]{2,1,0:T(8,128)S(1)}, f32[10,8,4224]{2,1,0:T(8,128)S(1)}, f32[...) custom-call(f32[8,8,4096]{2,1,0:T(8,128)S(1)} %get-tuple-element.28.data_ref, ...), custom_call_target="tpu_custom_call" | custom-call | tf_op jit(solution)/shard_map/local/pallas_call | solution.py:727
  26.4 0.0 collective-permute-done.2.slope_ref
  26.4 0.0 collective-permute-done.1.up_ref
  26.4 0.0 collective-permute-done.3.down_ref
  26.4 5.5 %join.1 = (f32[1,8,4224]{2,1,0:T(8,128)S(1)}, f32[3,8,4224]{2,1,0:T(8,128)S(1)}, f32[5,8,4224]{2,1,0:T(8,128)S(1)}, f32[1,8,4224]{2,1,0:T(8,128)S(1)}, f32[3,8,4224]{2,1,0:T(8,128)S(1)}, /*index=5*/f32[8,128]{1,0:T(8,128)S(1)}) custom-call(f32[10,8,4224]{2,1,0:T(8,128)S(1)} %get-tuple-element.24.d_ref, f32[10,8,4096]{2,1,0:T(8,128)S(1)} %get-tuple-element.25.si_ref, ...), custom_call_target="tpu_custom_call" | custom-call | tf_op jit(solution)/shard_map/join/pallas_call | solution.py:733
  31.9 2.7 %collective-permute-start.6 = (f32[8,128]{1,0:T(8,128)S(1)}, f32[8,128]{1,0:T(8,128)S(1)}, u32[]{:S(2)}, u32[]{:S(2)}) collective-permute-start(f32[8,128]{1,0:T(8,128)S(1)} %get-tuple-element.40), channel_id=1, source_target_pairs={{0,3},{1,2},{2,1},{3,0},{4,7},{5,6},{6,5},{7,4},{8,11},{9,10},{10,... | collective-permute-start | bytes 12296 | tf_op jit(solution)/shard_map/ppermute | solution.py:744
  34.7 3.6 %collective-permute-start.5 = (f32[8,128]{1,0:T(8,128)S(1)}, f32[8,128]{1,0:T(8,128)S(1)}, u32[]{:S(2)}, u32[]{:S(2)}) collective-permute-start(f32[8,128]{1,0:T(8,128)S(1)} %get-tuple-element.40), channel_id=1, source_target_pairs={{0,2},{1,3},{2,0},{3,1},{4,6},{5,7},{6,4},{7,5},{8,10},{9,11},{10,... | collective-permute-start | bytes 12296 | tf_op jit(solution)/shard_map/ppermute | solution.py:744
  38.3 0.1 collective-permute-start.4
  38.4 0.0 collective-permute-done.6
  38.4 1.5 %collective-permute-done.5 = f32[8,128]{1,0:T(8,128)S(1)} collective-permute-done((f32[8,128]{1,0:T(8,128)S(1)}, f32[8,128]{1,0:T(8,128)S(1)}, u32[]{:S(2)}, u32[]{:S(2)}) %collective-permute-start.5) | collective-permute-done | bytes 4128 | tf_op jit(solution)/shard_map/ppermute | solution.py:744
  39.9 0.0 collective-permute-done.4
  39.9 2.7 %collective-permute-start.9 = (f32[8,128]{1,0:T(8,128)S(1)}, f32[8,128]{1,0:T(8,128)S(1)}, u32[]{:S(2)}, u32[]{:S(2)}) collective-permute-start(f32[8,128]{1,0:T(8,128)S(1)} %add_add_fusion.1), channel_id=1, source_target_pairs={{0,12},{1,13},{2,14},{3,15},{4,8},{5,9},{6,10},{7,11},{8,4},{9,5},... | collective-permute-start | bytes 12296 | tf_op jit(solution)/shard_map/ppermute | solution.py:744
  42.6 0.4 collective-permute-start.8
  43.0 1.4 %collective-permute-start.7 = (f32[8,128]{1,0:T(8,128)S(1)}, f32[8,128]{1,0:T(8,128)S(1)}, u32[]{:S(2)}, u32[]{:S(2)}) collective-permute-start(f32[8,128]{1,0:T(8,128)S(1)} %add_add_fusion.1), channel_id=1, source_target_pairs={{0,4},{1,5},{2,6},{3,7},{4,0},{5,1},{6,2},{7,3},{8,12},{9,13},{10,... | collective-permute-start | bytes 12296 | tf_op jit(solution)/shard_map/ppermute | solution.py:744
  44.4 1.0 %collective-permute-done.9 = f32[8,128]{1,0:T(8,128)S(1)} collective-permute-done((f32[8,128]{1,0:T(8,128)S(1)}, f32[8,128]{1,0:T(8,128)S(1)}, u32[]{:S(2)}, u32[]{:S(2)}) %collective-permute-start.9) | collective-permute-done | bytes 4128 | tf_op jit(solution)/shard_map/ppermute | solution.py:744
  45.4 1.7 %collective-permute-done.8 = f32[8,128]{1,0:T(8,128)S(1)} collective-permute-done((f32[8,128]{1,0:T(8,128)S(1)}, f32[8,128]{1,0:T(8,128)S(1)}, u32[]{:S(2)}, u32[]{:S(2)}) %collective-permute-start.8) | collective-permute-done | bytes 4128 | tf_op jit(solution)/shard_map/ppermute | solution.py:744
  47.1 0.0 collective-permute-done.7
  47.1 1.8 %last.1 = (f32[8,8,4096]{2,1,0:T(8,128)}, f32[8,8,4096]{2,1,0:T(8,128)}) custom-call(f32[8,128]{1,0:T(8,128)S(1)} %add_add_fusion.moments_ref, f32[10,8,4224]{2,1,0:T(8,128)S(1)} %get-tuple-element.29.m_ref, f32[10,8,4224]{2,1,0:T(8,128)S(1)} %get-tuple-element.24.d_ref, f32[10,8,4224]{2,1,0:T(8,128)S(1)} %get-tuple-element.31.g_in, ...), custom_call_target="tpu_custom_call" | custom-call | tf_op jit(solution)/shard_map/last/pallas_call | solution.py:748
  (2 shorter events, 0.0 us)
Async XLA Ops:
  1.8 6.6 %collective-permute-start = (f32[8,16384]{1,0:T(8,128)S(1)}, f32[8,16384]{1,0:T(8,128)S(1)}, u32[]{:S(2)}, u32[]{:S(2)}) collective-permute-start(f32[8,16384]{1,0:T(8,128)S(1)} %pack.1), channel_id=1, source_target_pairs={{1,0},{2,1},{3,2},{4,3},{5,4},{6,5},{7,6},{8,7},{9,8},{10,9},{11,1... | collective-permute-start | bytes 1572872 | tf_op jit(solution)/shard_map/ppermute | solution.py:699
  7.1 19.3 %collective-permute-start.1 = (f32[8,20992]{1,0:T(8,128)S(1)}, f32[8,20992]{1,0:T(8,128)S(1)}, u32[]{:S(2)}, u32[]{:S(2)}) collective-permute-start(f32[8,20992]{1,0:T(8,128)S(1)} %get-tuple-element.38), channel_id=1, source_target_pairs={{1,0},{2,1},{3,2},{4,3},{5,4},{6,5},{7,6},{8,7},{9,8},{10,9},{11,1... | collective-permute-start | bytes 2015240 | tf_op jit(solution)/shard_map/ppermute | solution.py:699
  9.4 17.0 %collective-permute-start.3 = (f32[8,20480]{1,0:T(8,128)S(1)}, f32[8,20480]{1,0:T(8,128)S(1)}, u32[]{:S(2)}, u32[]{:S(2)}) collective-permute-start(f32[8,20480]{1,0:T(8,128)S(1)} %get-tuple-element.30.down_ref), channel_id=1, source_target_pairs={{0,1},{1,2},{2,3},{3,4},{4,5},{5,6},{6,7},{7,8},{8,9},{9,10},{10,1... | collective-permute-start | bytes 1966088 | tf_op jit(solution)/shard_map/ppermute | solution.py:702
  16.6 9.7 %collective-permute-start.2 = (f32[8,4096]{1,0:T(8,128)S(1)}, f32[8,4096]{1,0:T(8,128)S(1)}, u32[]{:S(2)}, u32[]{:S(2)}) collective-permute-start(f32[8,4096]{1,0:T(8,128)S(1)} %get-tuple-element.39), channel_id=1, source_target_pairs={{0,1},{1,2},{2,3},{3,4},{4,5},{5,6},{6,7},{7,8},{8,9},{9,10},{10,1... | collective-permute-start | bytes 393224 | tf_op jit(solution)/shard_map/ppermute | solution.py:702
  31.9 6.4 %collective-permute-start.6 = (f32[8,128]{1,0:T(8,128)S(1)}, f32[8,128]{1,0:T(8,128)S(1)}, u32[]{:S(2)}, u32[]{:S(2)}) collective-permute-start(f32[8,128]{1,0:T(8,128)S(1)} %get-tuple-element.40), channel_id=1, source_target_pairs={{0,3},{1,2},{2,1},{3,0},{4,7},{5,6},{6,5},{7,4},{8,11},{9,10},{10,... | collective-permute-start | bytes 12296 | tf_op jit(solution)/shard_map/ppermute | solution.py:744
  34.7 5.2 %collective-permute-start.5 = (f32[8,128]{1,0:T(8,128)S(1)}, f32[8,128]{1,0:T(8,128)S(1)}, u32[]{:S(2)}, u32[]{:S(2)}) collective-permute-start(f32[8,128]{1,0:T(8,128)S(1)} %get-tuple-element.40), channel_id=1, source_target_pairs={{0,2},{1,3},{2,0},{3,1},{4,6},{5,7},{6,4},{7,5},{8,10},{9,11},{10,... | collective-permute-start | bytes 12296 | tf_op jit(solution)/shard_map/ppermute | solution.py:744
  38.3 1.6 %collective-permute-start.4 = (f32[8,128]{1,0:T(8,128)S(1)}, f32[8,128]{1,0:T(8,128)S(1)}, u32[]{:S(2)}, u32[]{:S(2)}) collective-permute-start(f32[8,128]{1,0:T(8,128)S(1)} %get-tuple-element.40), channel_id=1, source_target_pairs={{0,1},{1,0},{2,3},{3,2},{4,5},{5,4},{6,7},{7,6},{8,9},{9,8},{10,11... | collective-permute-start | bytes 12296 | tf_op jit(solution)/shard_map/ppermute | solution.py:744
  39.9 5.5 %collective-permute-start.9 = (f32[8,128]{1,0:T(8,128)S(1)}, f32[8,128]{1,0:T(8,128)S(1)}, u32[]{:S(2)}, u32[]{:S(2)}) collective-permute-start(f32[8,128]{1,0:T(8,128)S(1)} %add_add_fusion.1), channel_id=1, source_target_pairs={{0,12},{1,13},{2,14},{3,15},{4,8},{5,9},{6,10},{7,11},{8,4},{9,5},... | collective-permute-start | bytes 12296 | tf_op jit(solution)/shard_map/ppermute | solution.py:744
  42.6 4.5 %collective-permute-start.8 = (f32[8,128]{1,0:T(8,128)S(1)}, f32[8,128]{1,0:T(8,128)S(1)}, u32[]{:S(2)}, u32[]{:S(2)}) collective-permute-start(f32[8,128]{1,0:T(8,128)S(1)} %add_add_fusion.1), channel_id=1, source_target_pairs={{0,8},{1,9},{2,10},{3,11},{4,12},{5,13},{6,14},{7,15},{8,0},{9,1},... | collective-permute-start | bytes 12296 | tf_op jit(solution)/shard_map/ppermute | solution.py:744
  43.0 4.1 %collective-permute-start.7 = (f32[8,128]{1,0:T(8,128)S(1)}, f32[8,128]{1,0:T(8,128)S(1)}, u32[]{:S(2)}, u32[]{:S(2)}) collective-permute-start(f32[8,128]{1,0:T(8,128)S(1)} %add_add_fusion.1), channel_id=1, source_target_pairs={{0,4},{1,5},{2,6},{3,7},{4,0},{5,1},{6,2},{7,3},{8,12},{9,13},{10,... | collective-permute-start | bytes 12296 | tf_op jit(solution)/shard_map/ppermute | solution.py:744

commit v8 on v6

--- a/solution.py
+++ b/solution.py
@@ -218,7 +218,7 @@
         copy.start()
     clear_pads(x, (m_ref, d_ref, g_ref, bg_ref, bd_ref))
     carry[...] = jnp.zeros(carry.shape, f32)
-    for copy in copies[:6]:
+    for copy in copies[:5]:
         copy.wait()
     share = x // NT
     for s in range(NT):
@@ -231,6 +231,11 @@
         put(up_ref, G0, x, x0, out[0])
         for i, value in out.items():
             g_ref[i + 1, :, own.here] = value
+        return 0
+
+    def first_of_direction(c, _):
+        x0 = at_chunk(c)
+        own = Own(n, x0, si_ref, sc_ref, mask_ref, carry)
         out = own.applied(d_ref, 0, 1, 3)
         put(up_ref, BD0, x, x0, out[0])
         for i, value in out.items():
@@ -238,6 +243,8 @@
         return 0
 
     sweep(x, first)
+    copies[5].wait()
+    sweep(x, first_of_direction)
     carry[...] = jnp.zeros(carry.shape, f32)
 
     def second(c, _):

time: 49.2 us -> 49.1 us (level)
  transfers between devices with their start and end apart: 10 -> 10, of which waited for: 3 -> 3; matrix products, arithmetic and copies ran while one was open for 0% -> 0% of each run, Pallas kernels for 25% -> 24%
where the time goes in v8:
time: 49.1 us; the launch traced here: 48.8 us
  starting transfers between devices  23.3 us (47%)
  Pallas kernels  20 us (41%)
  waiting for transfers between devices  4.63 us (9%)
  between operations  0.9 us (2%)
    ppermute x6, starting transfers between devices, on_device(): lax.ppermute(moments, 'inline', [(i, i ^ k * reach) for i in range(peers)])  11.3 us
    ppermute x2, starting transfers between devices, to_after(): return lax.ppermute(value, 'inline', [(i, i + 1) for i in range(peers - 1)])  9.49 us
    pallas_call x1, Pallas kernels, on_device(): call(local_kernel, [wide, wide, wide, wide, wide, kept((N_MOMENTS, NT, LA...  7.16 us
    pallas_call x1, Pallas kernels, on_device(): call(join_kernel, [ends(LOW[k] + HIGH[k]) for k in (0, 1, 2, 4, 5)] + [ja...  5.08 us
    ppermute x6, waiting for transfers between devices, on_device(): lax.ppermute(moments, 'inline', [(i, i ^ k * reach) for i in range(peers)])  4.62 us
    pallas_call x1, Pallas kernels, on_device(): call(first_kernel, [kept((n, NT, x)), kept((n, x), jnp.int32), kept((n +...  3.75 us
    ppermute x2, starting transfers between devices, to_before(): return lax.ppermute(value, 'inline', [(i, i - 1) for i in range(1, peers)])  2.58 us
    pallas_call x1, Pallas kernels, on_device(): pl.pallas_call(functools.partial(last_kernel, n, x), out_shape=[jax.Shape...  1.81 us
  transfers between devices with their start and end apart: 10, of which 3 were waited for; matrix products, arithmetic and copies ran while one was open for 0% of the time, Pallas kernels for 24%

profile of v8, /device:TPU:0, one launch (start us, length us, event | category | flops | bytes accessed | tf_op | source)
XLA Modules:
  0.0 48.8 jit_solution(9488488119281490878)
XLA Ops:
  0.6 1.1 %pack.1 = f32[8,16384]{1,0:T(8,128)S(1)} custom-call(f32[8,8,4096]{2,1,0:T(8,128)} %si_hbm.3, f32[8,8,4096]{2,1,0:T(8,128)} %sc_hbm.3, f32[8,8,4096]{2,1,0:T(8,128)} %model_hbm.3, f32[8,8,4096]{2,1,0:T(8,128)} %dir_hbm.3), custom_call_target="tpu_custom_call" | custom-call | tf_op jit(solution)/shard_map/pack/pallas_call | solution.py:704
  1.8 1.3 %collective-permute-start = (f32[8,16384]{1,0:T(8,128)S(1)}, f32[8,16384]{1,0:T(8,128)S(1)}, u32[]{:S(2)}, u32[]{:S(2)}) collective-permute-start(f32[8,16384]{1,0:T(8,128)S(1)} %pack.1), channel_id=1, source_target_pairs={{1,0},{2,1},{3,2},{4,3},{5,4},{6,5},{7,6},{8,7},{9,8},{10,9},{11,1... | collective-permute-start | bytes 1572872 | tf_op jit(solution)/shard_map/ppermute | solution.py:699
  3.1 3.8 %first.1 = (f32[8,8,4096]{2,1,0:T(8,128)S(1)}, s32[8,4096]{1,0:T(8,128)S(1)}, f32[10,8,4096]{2,1,0:T(8,128)S(1)}, f32[8,8,4096]{2,1,0:T(8,128)S(1)}, f32[10,8,42...) custom-call(f32[8,8,4096]{2,1,0:T(8,128)} %data_hbm.1, ...), custom_call_target="tpu_custom_call" | custom-call | tf_op jit(solution)/shard_map/first/pallas_call | solution.py:709
  6.8 1.3 %collective-permute-start.1 = (f32[8,20992]{1,0:T(8,128)S(1)}, f32[8,20992]{1,0:T(8,128)S(1)}, u32[]{:S(2)}, u32[]{:S(2)}) collective-permute-start(f32[8,20992]{1,0:T(8,128)S(1)} %get-tuple-element.38), channel_id=1, source_target_pairs={{1,0},{2,1},{3,2},{4,3},{5,4},{6,5},{7,6},{8,7},{9,8},{10,9},{11,1... | collective-permute-start | bytes 2015240 | tf_op jit(solution)/shard_map/ppermute | solution.py:699
  8.1 0.0 collective-permute-done.up_first
  8.1 1.0 %down.1 = (f32[8,20480]{1,0:T(8,128)S(1)}, f32[2,8,4224]{2,1,0:T(8,128)S(1)}) custom-call(f32[8,8,4096]{2,1,0:T(8,128)S(1)} %get-tuple-element.28.data_ref, s32[8,4096]{1,0:T(8,128)S(1)} %get-tuple-element.27.mask_ref, f32[10,8,4096]{2,1,0:T(8,128)S(1)} %get-tuple-element.25.si_ref, f32[8,8,4096]{2,1,0:T(8,128)S(1)} %get-tuple-element.26.sc_ref, ...), custom_call_target="tpu_custom_call" | custom-call | tf_op jit(solution)/shard_map/down/pallas_call | solution.py:721
  9.2 7.4 %collective-permute-start.3 = (f32[8,20480]{1,0:T(8,128)S(1)}, f32[8,20480]{1,0:T(8,128)S(1)}, u32[]{:S(2)}, u32[]{:S(2)}) collective-permute-start(f32[8,20480]{1,0:T(8,128)S(1)} %get-tuple-element.30.down_ref), channel_id=1, source_target_pairs={{0,1},{1,2},{2,3},{3,4},{4,5},{5,6},{6,7},{7,8},{8,9},{9,10},{10,1... | collective-permute-start | bytes 1966088 | tf_op jit(solution)/shard_map/ppermute | solution.py:702
  16.6 2.1 %collective-permute-start.2 = (f32[8,4096]{1,0:T(8,128)S(1)}, f32[8,4096]{1,0:T(8,128)S(1)}, u32[]{:S(2)}, u32[]{:S(2)}) collective-permute-start(f32[8,4096]{1,0:T(8,128)S(1)} %get-tuple-element.39), channel_id=1, source_target_pairs={{0,1},{1,2},{2,3},{3,4},{4,5},{5,6},{6,7},{7,8},{8,9},{9,10},{10,1... | collective-permute-start | bytes 393224 | tf_op jit(solution)/shard_map/ppermute | solution.py:702
  18.7 7.2 %local.1 = (f32[10,8,4224]{2,1,0:T(8,128)S(1)}, f32[10,8,4224]{2,1,0:T(8,128)S(1)}, f32[10,8,4224]{2,1,0:T(8,128)S(1)}, f32[10,8,4224]{2,1,0:T(8,128)S(1)}, f32[...) custom-call(f32[8,8,4096]{2,1,0:T(8,128)S(1)} %get-tuple-element.28.data_ref, ...), custom_call_target="tpu_custom_call" | custom-call | tf_op jit(solution)/shard_map/local/pallas_call | solution.py:727
  25.8 0.0 collective-permute-done.2.slope_ref
  25.9 0.0 collective-permute-done.1.up_ref
  25.9 0.0 collective-permute-done.3.down_ref
  25.9 5.1 %join.1 = (f32[1,8,4224]{2,1,0:T(8,128)S(1)}, f32[3,8,4224]{2,1,0:T(8,128)S(1)}, f32[5,8,4224]{2,1,0:T(8,128)S(1)}, f32[1,8,4224]{2,1,0:T(8,128)S(1)}, f32[3,8,4224]{2,1,0:T(8,128)S(1)}, /*index=5*/f32[24,128]{1,0:T(8,128)S(1)}) custom-call(f32[10,8,4224]{2,1,0:T(8,128)S(1)} %get-tuple-element.24.d_ref, f32[10,8,4096]{2,1,0:T(8,128)S(1)} %get-tuple-element.25.si_ref, ...), custom_call_target="tpu_custom_call" | custom-call | tf_op jit(solution)/shard_map/join/pallas_call | solution.py:733
  31.0 2.8 %collective-permute-start.6 = (f32[24,128]{1,0:T(8,128)S(1)}, f32[24,128]{1,0:T(8,128)S(1)}, u32[]{:S(2)}, u32[]{:S(2)}) collective-permute-start(f32[24,128]{1,0:T(8,128)S(1)} %get-tuple-element.40), channel_id=1, source_target_pairs={{0,3},{1,2},{2,1},{3,0},{4,7},{5,6},{6,5},{7,4},{8,11},{9,10},{10,... | collective-permute-start | bytes 36872 | tf_op jit(solution)/shard_map/ppermute | solution.py:744
  33.8 4.0 %collective-permute-start.5 = (f32[24,128]{1,0:T(8,128)S(1)}, f32[24,128]{1,0:T(8,128)S(1)}, u32[]{:S(2)}, u32[]{:S(2)}) collective-permute-start(f32[24,128]{1,0:T(8,128)S(1)} %get-tuple-element.40), channel_id=1, source_target_pairs={{0,2},{1,3},{2,0},{3,1},{4,6},{5,7},{6,4},{7,5},{8,10},{9,11},{10,... | collective-permute-start | bytes 36872 | tf_op jit(solution)/shard_map/ppermute | solution.py:744
  37.7 0.0 collective-permute-start.4
  37.8 0.0 collective-permute-done.6
  37.8 1.7 %collective-permute-done.5 = f32[24,128]{1,0:T(8,128)S(1)} collective-permute-done((f32[24,128]{1,0:T(8,128)S(1)}, f32[24,128]{1,0:T(8,128)S(1)}, u32[]{:S(2)}, u32[]{:S(2)}) %collective-permute-start.5) | collective-permute-done | bytes 12320 | tf_op jit(solution)/shard_map/ppermute | solution.py:744
  39.5 0.0 collective-permute-done.4
  39.5 2.7 %collective-permute-start.9 = (f32[24,128]{1,0:T(8,128)S(1)}, f32[24,128]{1,0:T(8,128)S(1)}, u32[]{:S(2)}, u32[]{:S(2)}) collective-permute-start(f32[24,128]{1,0:T(8,128)S(1)} %add_add_fusion.1), channel_id=1, source_target_pairs={{0,12},{1,13},{2,14},{3,15},{4,8},{5,9},{6,10},{7,11},{8,4},{9,5},... | collective-permute-start | bytes 36872 | tf_op jit(solution)/shard_map/ppermute | solution.py:744
  42.2 0.4 collective-permute-start.8
  42.6 1.3 %collective-permute-start.7 = (f32[24,128]{1,0:T(8,128)S(1)}, f32[24,128]{1,0:T(8,128)S(1)}, u32[]{:S(2)}, u32[]{:S(2)}) collective-permute-start(f32[24,128]{1,0:T(8,128)S(1)} %add_add_fusion.1), channel_id=1, source_target_pairs={{0,4},{1,5},{2,6},{3,7},{4,0},{5,1},{6,2},{7,3},{8,12},{9,13},{10,... | collective-permute-start | bytes 36872 | tf_op jit(solution)/shard_map/ppermute | solution.py:744
  43.9 1.1 %collective-permute-done.9 = f32[24,128]{1,0:T(8,128)S(1)} collective-permute-done((f32[24,128]{1,0:T(8,128)S(1)}, f32[24,128]{1,0:T(8,128)S(1)}, u32[]{:S(2)}, u32[]{:S(2)}) %collective-permute-start.9) | collective-permute-done | bytes 12320 | tf_op jit(solution)/shard_map/ppermute | solution.py:744
  45.1 1.8 %collective-permute-done.8 = f32[24,128]{1,0:T(8,128)S(1)} collective-permute-done((f32[24,128]{1,0:T(8,128)S(1)}, f32[24,128]{1,0:T(8,128)S(1)}, u32[]{:S(2)}, u32[]{:S(2)}) %collective-permute-start.8) | collective-permute-done | bytes 12320 | tf_op jit(solution)/shard_map/ppermute | solution.py:744
  46.9 0.0 collective-permute-done.7
  46.9 1.8 %last.1 = (f32[8,8,4096]{2,1,0:T(8,128)}, f32[8,8,4096]{2,1,0:T(8,128)}) custom-call(f32[24,128]{1,0:T(8,128)S(1)} %add_add_fusion.moments_ref, f32[10,8,4224]{2,1,0:T(8,128)S(1)} %get-tuple-element.29.m_ref, f32[10,8,4224]{2,1,0:T(8,128)S(1)} %get-tuple-element.24.d_ref, f32[10,8,4224]{2,1,0:T(8,128)S(1)} %get-tuple-element.31.g_in, ...), custom_call_target="tpu_custom_call" | custom-call | tf_op jit(solution)/shard_map/last/pallas_call | solution.py:748
  (2 shorter events, 0.0 us)
Async XLA Ops:
  1.8 6.4 %collective-permute-start = (f32[8,16384]{1,0:T(8,128)S(1)}, f32[8,16384]{1,0:T(8,128)S(1)}, u32[]{:S(2)}, u32[]{:S(2)}) collective-permute-start(f32[8,16384]{1,0:T(8,128)S(1)} %pack.1), channel_id=1, source_target_pairs={{1,0},{2,1},{3,2},{4,3},{5,4},{6,5},{7,6},{8,7},{9,8},{10,9},{11,1... | collective-permute-start | bytes 1572872 | tf_op jit(solution)/shard_map/ppermute | solution.py:699
  6.8 19.0 %collective-permute-start.1 = (f32[8,20992]{1,0:T(8,128)S(1)}, f32[8,20992]{1,0:T(8,128)S(1)}, u32[]{:S(2)}, u32[]{:S(2)}) collective-permute-start(f32[8,20992]{1,0:T(8,128)S(1)} %get-tuple-element.38), channel_id=1, source_target_pairs={{1,0},{2,1},{3,2},{4,3},{5,4},{6,5},{7,6},{8,7},{9,8},{10,9},{11,1... | collective-permute-start | bytes 2015240 | tf_op jit(solution)/shard_map/ppermute | solution.py:699
  9.2 16.7 %collective-permute-start.3 = (f32[8,20480]{1,0:T(8,128)S(1)}, f32[8,20480]{1,0:T(8,128)S(1)}, u32[]{:S(2)}, u32[]{:S(2)}) collective-permute-start(f32[8,20480]{1,0:T(8,128)S(1)} %get-tuple-element.30.down_ref), channel_id=1, source_target_pairs={{0,1},{1,2},{2,3},{3,4},{4,5},{5,6},{6,7},{7,8},{8,9},{9,10},{10,1... | collective-permute-start | bytes 1966088 | tf_op jit(solution)/shard_map/ppermute | solution.py:702
  16.6 9.2 %collective-permute-start.2 = (f32[8,4096]{1,0:T(8,128)S(1)}, f32[8,4096]{1,0:T(8,128)S(1)}, u32[]{:S(2)}, u32[]{:S(2)}) collective-permute-start(f32[8,4096]{1,0:T(8,128)S(1)} %get-tuple-element.39), channel_id=1, source_target_pairs={{0,1},{1,2},{2,3},{3,4},{4,5},{5,6},{6,7},{7,8},{8,9},{9,10},{10,1... | collective-permute-start | bytes 393224 | tf_op jit(solution)/shard_map/ppermute | solution.py:702
  31.0 6.8 %collective-permute-start.6 = (f32[24,128]{1,0:T(8,128)S(1)}, f32[24,128]{1,0:T(8,128)S(1)}, u32[]{:S(2)}, u32[]{:S(2)}) collective-permute-start(f32[24,128]{1,0:T(8,128)S(1)} %get-tuple-element.40), channel_id=1, source_target_pairs={{0,3},{1,2},{2,1},{3,0},{4,7},{5,6},{6,5},{7,4},{8,11},{9,10},{10,... | collective-permute-start | bytes 36872 | tf_op jit(solution)/shard_map/ppermute | solution.py:744
  33.8 5.7 %collective-permute-start.5 = (f32[24,128]{1,0:T(8,128)S(1)}, f32[24,128]{1,0:T(8,128)S(1)}, u32[]{:S(2)}, u32[]{:S(2)}) collective-permute-start(f32[24,128]{1,0:T(8,128)S(1)} %get-tuple-element.40), channel_id=1, source_target_pairs={{0,2},{1,3},{2,0},{3,1},{4,6},{5,7},{6,4},{7,5},{8,10},{9,11},{10,... | collective-permute-start | bytes 36872 | tf_op jit(solution)/shard_map/ppermute | solution.py:744
  37.7 1.7 %collective-permute-start.4 = (f32[24,128]{1,0:T(8,128)S(1)}, f32[24,128]{1,0:T(8,128)S(1)}, u32[]{:S(2)}, u32[]{:S(2)}) collective-permute-start(f32[24,128]{1,0:T(8,128)S(1)} %get-tuple-element.40), channel_id=1, source_target_pairs={{0,1},{1,0},{2,3},{3,2},{4,5},{5,4},{6,7},{7,6},{8,9},{9,8},{10,11... | collective-permute-start | bytes 36872 | tf_op jit(solution)/shard_map/ppermute | solution.py:744
  39.5 5.6 %collective-permute-start.9 = (f32[24,128]{1,0:T(8,128)S(1)}, f32[24,128]{1,0:T(8,128)S(1)}, u32[]{:S(2)}, u32[]{:S(2)}) collective-permute-start(f32[24,128]{1,0:T(8,128)S(1)} %add_add_fusion.1), channel_id=1, source_target_pairs={{0,12},{1,13},{2,14},{3,15},{4,8},{5,9},{6,10},{7,11},{8,4},{9,5},... | collective-permute-start | bytes 36872 | tf_op jit(solution)/shard_map/ppermute | solution.py:744
  42.2 4.7 %collective-permute-start.8 = (f32[24,128]{1,0:T(8,128)S(1)}, f32[24,128]{1,0:T(8,128)S(1)}, u32[]{:S(2)}, u32[]{:S(2)}) collective-permute-start(f32[24,128]{1,0:T(8,128)S(1)} %add_add_fusion.1), channel_id=1, source_target_pairs={{0,8},{1,9},{2,10},{3,11},{4,12},{5,13},{6,14},{7,15},{8,0},{9,1},... | collective-permute-start | bytes 36872 | tf_op jit(solution)/shard_map/ppermute | solution.py:744
  42.6 4.3 %collective-permute-start.7 = (f32[24,128]{1,0:T(8,128)S(1)}, f32[24,128]{1,0:T(8,128)S(1)}, u32[]{:S(2)}, u32[]{:S(2)}) collective-permute-start(f32[24,128]{1,0:T(8,128)S(1)} %add_add_fusion.1), channel_id=1, source_target_pairs={{0,4},{1,5},{2,6},{3,7},{4,0},{5,1},{6,2},{7,3},{8,12},{9,13},{10,... | collective-permute-start | bytes 36872 | tf_op jit(solution)/shard_map/ppermute | solution.py:744
